TPU v7x, 256 devices: a whole 4x4x8 slice. The times are simulated.
256 devices in a mesh: lon: 64 (over y, x, z_lo), lat: 4 (over z_hi, core).
Axes of the slice: x: 4, y: 4, z: 8 (z_hi: 2, z_lo: 4; z = z_hi * 4 + z_lo), core: 2. Of those that a mesh axis runs over, the one named last changes fastest.
Arguments:
- ocean_field: float32 [32, 256, 8192], P(None, 'lat', 'lon'), may hold values from -6 to 6
- cotangent: bfloat16 [32, 256, 8192], P(None, 'lat', 'lon'), may hold values from -12 to 12
- mix_coarse: float32 [4, 32, 32], replicated, may hold values from -1 to 1
- mix_detail: float32 [3, 32, 32], replicated, may hold values from -1 to 1
- skip_weight: float32 [32, 32], replicated, may hold values from -1 to 1
- bias_vector: float32 [32], replicated, may hold values from -0.5 to 0.5
Outputs:
- activated: bfloat16 [32, 256, 8192], P(None, 'lat', 'lon')
- grad_field: float32 [32, 256, 8192], P(None, 'lat', 'lon')
- grad_mix_coarse: float32 [4, 32, 32], replicated
- grad_mix_detail: float32 [3, 32, 32], replicated
- grad_skip: float32 [32, 32], replicated
- grad_bias: float32 [32], replicated
All inputs are finite; a program needn't handle non-finite values.
Results may differ from a plain program's by a relative error of at most 0.001.
Values sent between devices are 32-bit elements; how exact they have to be, the bound alone decides.
No kernel may reach another device: no remote copies, remote signals or barrier semaphores. Data moves between devices by JAX's collectives and lax.ppermute only.
A program may use at most 128 MiB of HBM per device.

v0:
```python
import math

import jax
import jax.numpy as jnp
from jax import lax
from jax.sharding import PartitionSpec as P

low_taps = (
    -0.010597401785069032,
    0.0328830116668852,
    0.030841381835560764,
    -0.18703481171909309,
    -0.027983769416859854,
    0.6308807679298589,
    0.7148465705529157,
    0.2303778133088965,
)
high_taps = (
    -0.2303778133088965,
    0.7148465705529157,
    -0.6308807679298589,
    -0.027983769416859854,
    0.18703481171909309,
    0.030841381835560764,
    -0.0328830116668852,
    -0.010597401785069032,
)


def with_halo(block, sides, width, periodic):
    for axis, dim in sides:
        count = lax.axis_size(axis)
        forward = [(i, i + 1) for i in range(count - 1)]
        if periodic:
            forward.append((count - 1, 0))
        backward = [(target, source) for source, target in forward]
        low = lax.ppermute(
            lax.slice_in_dim(block, block.shape[dim] - width, None, axis=dim), axis, forward
        )
        high = lax.ppermute(lax.slice_in_dim(block, 0, width, axis=dim), axis, backward)
        block = jnp.concatenate([low, block, high], axis=dim)
    return block


def halo_lon_analysis(values):
    return with_halo(values, (("lon", 3),), 3, True)


def halo_lat_analysis(values):
    return with_halo(values, (("lat", 2),), 3, False)


def halo_lon_synthesis(values):
    return with_halo(values, (("lon", 3),), 2, True)


def halo_lat_synthesis(values):
    return with_halo(values, (("lat", 2),), 2, False)


def band_table(in_len, out_len, tap_list, factor, offset, sign):
    rows = jnp.arange(in_len, dtype=jnp.int32)[:, None]
    cols = jnp.arange(out_len, dtype=jnp.int32)[None, :]
    if sign > 0:
        where = rows - factor * cols
    else:
        where = cols + offset - factor * rows
    table = jnp.zeros((in_len, out_len), jnp.float32)
    for tap_index in range(8):
        table = table + tap_list[tap_index] * (where == tap_index).astype(jnp.float32)
    return table


def band_product(values, table):
    return jnp.einsum("abcp,pk->abck", values, table, precision=lax.Precision.HIGHEST)


def filter_pass(padded, along, length, tap_list):
    if along == 3:
        table = band_table(padded.shape[3], length, tap_list, 2, 0, 1)
        return band_product(padded, table)
    summed = tap_list[0] * lax.slice_in_dim(padded, 0, 2 * length - 1, 2, along)
    for offset in range(1, 8):
        summed = summed + tap_list[offset] * lax.slice_in_dim(
            padded, offset, offset + 2 * length - 1, 2, along
        )
    return summed


def shifted(padded, offset, length, along):
    return lax.slice_in_dim(padded, offset, offset + length, 1, along)


def upsample_pass(low_padded, high_padded, along, length):
    if along == 3:
        in_len = low_padded.shape[3]
        result = band_product(low_padded, band_table(in_len, 2 * length, low_taps, 2, 7, -1))
        if high_padded is not None:
            result = result + band_product(
                high_padded, band_table(in_len, 2 * length, high_taps, 2, 7, -1)
            )
        return result

    def halves(padded, tap_list):
        even_part = (
            tap_list[1] * shifted(padded, 3, length, along)
            + tap_list[3] * shifted(padded, 2, length, along)
            + tap_list[5] * shifted(padded, 1, length, along)
            + tap_list[7] * shifted(padded, 0, length, along)
        )
        odd_part = (
            tap_list[0] * shifted(padded, 4, length, along)
            + tap_list[2] * shifted(padded, 3, length, along)
            + tap_list[4] * shifted(padded, 2, length, along)
            + tap_list[6] * shifted(padded, 1, length, along)
        )
        return (even_part, odd_part)

    even_part, odd_part = halves(low_padded, low_taps)
    if high_padded is not None:
        even_high, odd_high = halves(high_padded, high_taps)
        even_part = even_part + even_high
        odd_part = odd_part + odd_high
    merged = jnp.stack([even_part, odd_part], axis=along + 1)
    new_shape = list(even_part.shape)
    new_shape[along] = 2 * length
    return merged.reshape(new_shape)


def analyze(values, lon_pad, details):
    lon_len = values.shape[3] // 2
    lat_len = values.shape[2] // 2
    tap_sets = (low_taps, high_taps) if details else (low_taps,)
    padded = lon_pad(values)
    lon_parts = jnp.concatenate(
        [filter_pass(padded, 3, lon_len, tap_list) for tap_list in tap_sets], 0
    )
    padded = halo_lat_analysis(lon_parts)
    lat_low = filter_pass(padded, 2, lat_len, low_taps)
    if not details:
        return lat_low
    lat_high = filter_pass(padded, 2, lat_len, high_taps)
    return (lat_low[0:1], jnp.stack([lat_high[0], lat_low[1], lat_high[1]], 0))


def synthesize(approx, detail, lon_pad):
    lat_len = approx.shape[2]
    lon_len = approx.shape[3]
    if detail is None:
        padded = halo_lat_synthesis(approx)
        rows_up = upsample_pass(padded, None, 2, lat_len)
        padded = lon_pad(rows_up)
        return upsample_pass(padded, None, 3, lon_len)
    stacked = jnp.concatenate([approx, detail[1:2], detail[0:1], detail[2:3]], 0)
    padded = halo_lat_synthesis(stacked)
    rows_up = upsample_pass(padded[0:2], padded[2:4], 2, lat_len)
    padded = lon_pad(rows_up)
    return upsample_pass(padded[0:1], padded[1:2], 3, lon_len)


def mixing(coefficients, weights):
    return jnp.einsum("sirl,sio->sorl", coefficients, weights, precision=lax.Precision.HIGHEST)


def unmixing(coefficients, weights):
    return jnp.einsum("sorl,sio->sirl", coefficients, weights, precision=lax.Precision.HIGHEST)


def contraction(first_coef, second_coef):
    return jnp.einsum("sirl,sorl->sio", first_coef, second_coef, precision=lax.Precision.HIGHEST)


def fine_levels(values):
    level_one = analyze(values, halo_lon_analysis, False)
    level_two = analyze(level_one, halo_lon_analysis, False)
    return analyze(level_two, halo_lon_analysis, True)


def finish(level_three, detail_mixed):
    level_two = synthesize(level_three, detail_mixed, halo_lon_synthesis)
    level_one = synthesize(level_two, None, halo_lon_synthesis)
    return synthesize(level_one, None, halo_lon_synthesis)[0]


def gelu_slope(pre_act):
    cumulative = 0.5 * (1.0 + jax.scipy.special.erf(pre_act / math.sqrt(2.0)))
    density = jnp.exp(-0.5 * pre_act * pre_act) / math.sqrt(2.0 * math.pi)
    return cumulative + pre_act * density


def on_device(ocean_field, cotangent, mix_coarse, mix_detail, skip_weight, bias_vector):
    approx, detail_three = fine_levels(ocean_field[None])
    coarse_low, detail_four = analyze(approx, halo_lon_analysis, True)
    coarse = jnp.concatenate([coarse_low, detail_four], 0)
    mixed_coef = mixing(coarse, mix_coarse)
    level_three = synthesize(mixed_coef[0:1], mixed_coef[1:4], halo_lon_synthesis)
    kernel = finish(level_three, mixing(detail_three, mix_detail))
    pre_act = (
        kernel
        + jnp.einsum("irl,io->orl", ocean_field, skip_weight, precision=lax.Precision.HIGHEST)
        + bias_vector[:, None, None]
    )
    activated = jax.nn.gelu(pre_act, approximate=False).astype(jnp.bfloat16)
    grad_pre = cotangent.astype(jnp.float32) * gelu_slope(pre_act)
    grad_approx, grad_detail = fine_levels(grad_pre[None])
    local_detail = contraction(detail_three, grad_detail)
    local_skip = jnp.einsum("irl,orl->io", ocean_field, grad_pre, precision=lax.Precision.HIGHEST)
    local_bias = jnp.sum(grad_pre, axis=(1, 2))
    grad_low, grad_four = analyze(grad_approx, halo_lon_analysis, True)
    grad_coarse = jnp.concatenate([grad_low, grad_four], 0)
    summed_coarse, summed_detail, summed_skip, summed_bias = lax.psum(
        (contraction(coarse, grad_coarse), local_detail, local_skip, local_bias), ("lon", "lat")
    )
    back_coarse = unmixing(grad_coarse, mix_coarse)
    grad_three = synthesize(back_coarse[0:1], back_coarse[1:4], halo_lon_synthesis)
    grad_field = finish(grad_three, unmixing(grad_detail, mix_detail))
    grad_field = grad_field + jnp.einsum(
        "orl,io->irl", grad_pre, skip_weight, precision=lax.Precision.HIGHEST
    )
    cell_count = (
        ocean_field.shape[1] * lax.axis_size("lat") * ocean_field.shape[2] * lax.axis_size("lon")
    )
    grad_mix_coarse = summed_coarse / math.sqrt(cell_count // 256)
    grad_mix_detail = summed_detail / math.sqrt(cell_count // 64)
    grad_skip = summed_skip / math.sqrt(cell_count)
    grad_bias = summed_bias / math.sqrt(cell_count)
    return (activated, grad_field, grad_mix_coarse, grad_mix_detail, grad_skip, grad_bias)


def solution(mesh):
    return jax.shard_map(
        on_device,
        mesh=mesh,
        in_specs=(P(None, "lat", "lon"), P(None, "lat", "lon"), P(), P(), P(), P()),
        out_specs=(P(None, "lat", "lon"), P(None, "lat", "lon"), P(), P(), P(), P()),
        check_vma=False,
    )
```

profile of v0, /device:TPU:1, one launch (start us, length us, event | category | flops | bytes accessed | tf_op | source)
XLA Modules:
  0.0 597.7 jit_solution(6460846090396140500)
XLA Ops:
  3.0 2.5 collective-permute-start
  5.9 7.4 %collective-permute-start.1 = (f32[1,32,64,3]{2,1,3,0:T(8,128)S(1)}, f32[1,32,64,3]{2,1,3,0:T(8,128)S(1)}, u32[]{:S(2)}, u32[]{:S(2)}) collective-permute-start(f32[1,32,64,3]{2,1,3,0:T(8,128)S(1)} %copy.65), channel_id=1, source_target_pairs={{4,0},{8,4},{12,8},{16,12},{20,16},{24,20},{28,24},{32,28},{36,32}... | collective-permute-start | bytes 73736 | tf_op jit(solution)/shard_map/ppermute | solution.py:40
  13.3 2.5 fusion.42
  18.2 3.4 fusion.11
  21.6 8.4 %collective-permute-start.2 = (f32[1,32,3,64]{3,2,1,0:T(4,128)S(1)}, f32[1,32,3,64]{3,2,1,0:T(4,128)S(1)}, u32[]{:S(2)}, u32[]{:S(2)}) collective-permute-start(f32[1,32,3,64]{3,2,1,0:T(4,128)S(1)} %get-tuple-element.43), channel_id=1, source_target_pairs={{0,1},{1,2},{2,3},{4,5},{5,6},{6,7},{8,9},{9,10},{10,11},{12,13},{... | collective-permute-start | bytes 73736 | tf_op jit(solution)/shard_map/ppermute | solution.py:37
  36.6 3.0 collective-permute-done.3
  39.7 2.1 slice.842
  41.8 2.1 slice.843
  52.1 2.3 multiply_add_fusion.1
  54.8 7.5 %collective-permute-start.5 = (f32[1,32,32,3]{3,2,1,0:T(8,128)S(1)}, f32[1,32,32,3]{3,2,1,0:T(8,128)S(1)}, u32[]{:S(2)}, u32[]{:S(2)}) collective-permute-start(f32[1,32,32,3]{3,2,1,0:T(8,128)S(1)} %get-tuple-element.70), channel_id=1, source_target_pairs={{4,0},{8,4},{12,8},{16,12},{20,16},{24,20},{28,24},{32,28},{36,32}... | collective-permute-start | bytes 36872 | tf_op jit(solution)/shard_map/ppermute | solution.py:40
  62.8 11.5 %collective-permute-done.4 = f32[1,32,32,3]{3,2,1,0:T(8,128)S(1)} collective-permute-done((f32[1,32,32,3]{3,2,1,0:T(8,128)S(1)}, f32[1,32,32,3]{3,2,1,0:T(8,128)S(1)}, u32[]{:S(2)}, u32[]{:S(2)}) %collective-permute-start.4) | collective-permute-done | bytes 12320 | tf_op jit(solution)/shard_map/ppermute | solution.py:37
  75.0 5.6 collective-permute-start.6
  84.0 6.4 %collective-permute-done.7 = f32[1,32,3,32]{3,2,1,0:T(4,128)S(1)} collective-permute-done((f32[1,32,3,32]{3,2,1,0:T(4,128)S(1)}, f32[1,32,3,32]{3,2,1,0:T(4,128)S(1)}, u32[]{:S(2)}, u32[]{:S(2)}) %collective-permute-start.7) | collective-permute-done | bytes 12320 | tf_op jit(solution)/shard_map/ppermute | solution.py:40
  96.5 7.5 %collective-permute-start.9 = (f32[1,32,16,3]{3,2,1,0:T(8,128)S(1)}, f32[1,32,16,3]{3,2,1,0:T(8,128)S(1)}, u32[]{:S(2)}, u32[]{:S(2)}) collective-permute-start(f32[1,32,16,3]{3,2,1,0:T(8,128)S(1)} %get-tuple-element.98), channel_id=1, source_target_pairs={{4,0},{8,4},{12,8},{16,12},{20,16},{24,20},{28,24},{32,28},{36,32}... | collective-permute-start | bytes 18440 | tf_op jit(solution)/shard_map/ppermute | solution.py:40
  104.0 3.9 collective-permute-done.8
  110.4 2.9 collective-permute-start.10
  115.3 7.3 %collective-permute-done.11 = f32[2,32,3,16]{1,3,2,0:T(8,128)S(1)} collective-permute-done((f32[2,32,3,16]{1,3,2,0:T(8,128)S(1)}, f32[2,32,3,16]{1,3,2,0:T(8,128)S(1)}, u32[]{:S(2)}, u32[]{:S(2)}) %collective-permute-start.11) | collective-permute-done | bytes 12320 | tf_op jit(solution)/shard_map/ppermute | solution.py:40
  122.9 7.7 %collective-permute-start.13 = (f32[1,32,8,3]{1,3,2,0:T(4,128)S(1)}, f32[1,32,8,3]{1,3,2,0:T(4,128)S(1)}, u32[]{:S(2)}, u32[]{:S(2)}) collective-permute-start(f32[1,32,8,3]{1,3,2,0:T(4,128)S(1)} %get-tuple-element.116), channel_id=1, source_target_pairs={{4,0},{8,4},{12,8},{16,12},{20,16},{24,20},{28,24},{32,28},{36,32}... | collective-permute-start | bytes 9224 | tf_op jit(solution)/shard_map/ppermute | solution.py:40
  132.1 2.9 collective-permute-start.14
  137.0 7.1 %collective-permute-done.15 = f32[2,32,3,8]{1,3,2,0:T(8,128)S(1)} collective-permute-done((f32[2,32,3,8]{1,3,2,0:T(8,128)S(1)}, f32[2,32,3,8]{1,3,2,0:T(8,128)S(1)}, u32[]{:S(2)}, u32[]{:S(2)}) %collective-permute-start.15) | collective-permute-done | bytes 6176 | tf_op jit(solution)/shard_map/ppermute | solution.py:40
  146.4 7.5 %collective-permute-start.17 = (f32[4,32,2,8]{1,3,2,0:T(8,128)S(1)}, f32[4,32,2,8]{1,3,2,0:T(8,128)S(1)}, u32[]{:S(2)}, u32[]{:S(2)}) collective-permute-start(f32[4,32,2,8]{1,3,2,0:T(8,128)S(1)} %get-tuple-element.137), channel_id=1, source_target_pairs={{0,1},{1,2},{2,3},{4,5},{5,6},{6,7},{8,9},{9,10},{10,11},{12,13},{... | collective-permute-start | bytes 24584 | tf_op jit(solution)/shard_map/ppermute | solution.py:37
  155.2 7.8 %collective-permute-start.19 = (f32[2,32,8,2]{1,3,2,0:T(2,128)S(1)}, f32[2,32,8,2]{1,3,2,0:T(2,128)S(1)}, u32[]{:S(2)}, u32[]{:S(2)}) collective-permute-start(f32[2,32,8,2]{1,3,2,0:T(2,128)S(1)} %get-tuple-element.134), channel_id=1, source_target_pairs={{4,0},{8,4},{12,8},{16,12},{20,16},{24,20},{28,24},{32,28},{36,32}... | collective-permute-start | bytes 12296 | tf_op jit(solution)/shard_map/ppermute | solution.py:40
  166.6 9.0 %collective-permute-start.21 = (f32[4,32,2,16]{1,3,2,0:T(8,128)S(1)}, f32[4,32,2,16]{1,3,2,0:T(8,128)S(1)}, u32[]{:S(2)}, u32[]{:S(2)}) collective-permute-start(f32[4,32,2,16]{1,3,2,0:T(8,128)S(1)} %get-tuple-element.93), channel_id=1, source_target_pairs={{0,1},{1,2},{2,3},{4,5},{5,6},{6,7},{8,9},{9,10},{10,11},{12,13},{... | collective-permute-start | bytes 49160 | tf_op jit(solution)/shard_map/ppermute | solution.py:37
  177.4 8.2 %collective-permute-start.23 = (f32[2,32,16,2]{1,3,2,0:T(2,128)S(1)}, f32[2,32,16,2]{1,3,2,0:T(2,128)S(1)}, u32[]{:S(2)}, u32[]{:S(2)}) collective-permute-start(f32[2,32,16,2]{1,3,2,0:T(2,128)S(1)} %get-tuple-element.90), channel_id=1, source_target_pairs={{4,0},{8,4},{12,8},{16,12},{20,16},{24,20},{28,24},{32,28},{36,32}... | collective-permute-start | bytes 24584 | tf_op jit(solution)/shard_map/ppermute | solution.py:40
  190.2 9.0 %collective-permute-start.25 = (f32[1,32,2,32]{3,2,1,0:T(2,128)S(1)}, f32[1,32,2,32]{3,2,1,0:T(2,128)S(1)}, u32[]{:S(2)}, u32[]{:S(2)}) collective-permute-start(f32[1,32,2,32]{3,2,1,0:T(2,128)S(1)} %get-tuple-element.87), channel_id=1, source_target_pairs={{0,1},{1,2},{2,3},{4,5},{5,6},{6,7},{8,9},{9,10},{10,11},{12,13},{... | collective-permute-start | bytes 24584 | tf_op jit(solution)/shard_map/ppermute | solution.py:37
  201.7 8.2 %collective-permute-start.27 = (f32[1,32,32,2]{3,2,1,0:T(8,128)S(1)}, f32[1,32,32,2]{3,2,1,0:T(8,128)S(1)}, u32[]{:S(2)}, u32[]{:S(2)}) collective-permute-start(f32[1,32,32,2]{3,2,1,0:T(8,128)S(1)} %get-tuple-element.66), channel_id=1, source_target_pairs={{4,0},{8,4},{12,8},{16,12},{20,16},{24,20},{28,24},{32,28},{36,32}... | collective-permute-start | bytes 24584 | tf_op jit(solution)/shard_map/ppermute | solution.py:40
  209.9 11.0 %collective-permute-done.26 = f32[1,32,32,2]{3,2,1,0:T(8,128)S(1)} collective-permute-done((f32[1,32,32,2]{3,2,1,0:T(8,128)S(1)}, f32[1,32,32,2]{3,2,1,0:T(8,128)S(1)}, u32[]{:S(2)}, u32[]{:S(2)}) %collective-permute-start.26) | collective-permute-done | bytes 8224 | tf_op jit(solution)/shard_map/ppermute | solution.py:37
  223.7 9.2 %collective-permute-start.29 = (f32[1,32,2,64]{3,2,1,0:T(2,128)S(1)}, f32[1,32,2,64]{3,2,1,0:T(2,128)S(1)}, u32[]{:S(2)}, u32[]{:S(2)}) collective-permute-start(f32[1,32,2,64]{3,2,1,0:T(2,128)S(1)} %get-tuple-element.63), channel_id=1, source_target_pairs={{0,1},{1,2},{2,3},{4,5},{5,6},{6,7},{8,9},{9,10},{10,11},{12,13},{... | collective-permute-start | bytes 49160 | tf_op jit(solution)/shard_map/ppermute | solution.py:37
  238.9 7.5 %collective-permute-start.31 = (f32[1,32,64,2]{2,1,3,0:T(8,128)S(1)}, f32[1,32,64,2]{2,1,3,0:T(8,128)S(1)}, u32[]{:S(2)}, u32[]{:S(2)}) collective-permute-start(f32[1,32,64,2]{2,1,3,0:T(8,128)S(1)} %copy.80), channel_id=1, source_target_pairs={{4,0},{8,4},{12,8},{16,12},{20,16},{24,20},{28,24},{32,28},{36,32}... | collective-permute-start | bytes 49160 | tf_op jit(solution)/shard_map/ppermute | solution.py:40
  251.4 7.6 %fusion.842 = (f32[32]{0:T(128)}, f32[32,64,128]{2,1,0:T(8,128)S(1)}, bf16[32,64,128]{2,1,0:T(8,128)(2,1)}) fusion(bf16[32,64,128]{2,1,0:T(8,128)(2,1)} %param.7, f32[32]{0:T(128)S(1)} %copy-done.44, f32[32,64,128]{2,0,1:T(8,128)S(1)} %copy-done.7, s32[68]{0:T(128)S(1)} %copy-done.41, s32[128]{0:T(128)S(1)} %copy-done.39, f32[1,32,64,2]{3,2,1,0:T(8,128)} %copy.83, ...), kind=kOutput, calls=%fused_computation.1073 | convolution fusion | flops 234844128 | bytes 3703824 | tf_op jit(solution)/shard_map/abcp,pk->abck/dot_general | solution.py:75
  263.4 7.5 %collective-permute-start.33 = (f32[1,32,64,3]{2,1,3,0:T(8,128)}, f32[1,32,64,3]{2,1,3,0:T(8,128)S(1)}, u32[]{:S(2)}, u32[]{:S(2)}) collective-permute-start(f32[1,32,64,3]{2,1,3,0:T(8,128)} %copy.88), channel_id=1, source_target_pairs={{4,0},{8,4},{12,8},{16,12},{20,16},{24,20},{28,24},{32,28},{36,32}... | collective-permute-start | bytes 73736 | tf_op jit(solution)/shard_map/ppermute | solution.py:40
  274.1 3.7 fusion.10
  278.6 10.0 %collective-permute-start.34 = (f32[1,32,3,64]{3,2,1,0:T(4,128)}, f32[1,32,3,64]{3,2,1,0:T(4,128)S(1)}, u32[]{:S(2)}, u32[]{:S(2)}) collective-permute-start(f32[1,32,3,64]{3,2,1,0:T(4,128)} %get-tuple-element.36), channel_id=1, source_target_pairs={{0,1},{1,2},{2,3},{4,5},{5,6},{6,7},{8,9},{9,10},{10,11},{12,13},{... | collective-permute-start | bytes 73736 | tf_op jit(solution)/shard_map/ppermute | solution.py:37
  290.5 2.1 slice.952
  295.3 2.9 collective-permute-done.35
  299.6 2.1 slice.949
  301.7 2.1 slice.950
  307.9 2.1 slice.955
  312.0 2.7 multiply_add_fusion
  315.0 8.2 %collective-permute-start.37 = (f32[1,32,32,3]{3,2,1,0:T(8,128)S(1)}, f32[1,32,32,3]{3,2,1,0:T(8,128)S(1)}, u32[]{:S(2)}, u32[]{:S(2)}) collective-permute-start(f32[1,32,32,3]{3,2,1,0:T(8,128)S(1)} %get-tuple-element.62), channel_id=1, source_target_pairs={{4,0},{8,4},{12,8},{16,12},{20,16},{24,20},{28,24},{32,28},{36,32}... | collective-permute-start | bytes 36872 | tf_op jit(solution)/shard_map/ppermute | solution.py:40
  323.1 11.7 %collective-permute-done.36 = f32[1,32,32,3]{3,2,1,0:T(8,128)S(1)} collective-permute-done((f32[1,32,32,3]{3,2,1,0:T(8,128)S(1)}, f32[1,32,32,3]{3,2,1,0:T(8,128)S(1)}, u32[]{:S(2)}, u32[]{:S(2)}) %collective-permute-start.36) | collective-permute-done | bytes 12320 | tf_op jit(solution)/shard_map/ppermute | solution.py:37
  335.7 5.9 collective-permute-start.38
  346.9 4.5 collective-permute-done.39
  362.5 7.6 %collective-permute-start.41 = (f32[1,32,16,3]{3,2,1,0:T(8,128)S(1)}, f32[1,32,16,3]{3,2,1,0:T(8,128)S(1)}, u32[]{:S(2)}, u32[]{:S(2)}) collective-permute-start(f32[1,32,16,3]{3,2,1,0:T(8,128)S(1)} %get-tuple-element.86), channel_id=1, source_target_pairs={{4,0},{8,4},{12,8},{16,12},{20,16},{24,20},{28,24},{32,28},{36,32}... | collective-permute-start | bytes 18440 | tf_op jit(solution)/shard_map/ppermute | solution.py:40
  371.8 2.1 collective-permute-done.40
  376.5 4.3 collective-permute-start.42
  382.8 7.3 %collective-permute-done.43 = f32[2,32,3,16]{1,3,2,0:T(8,128)S(1)} collective-permute-done((f32[2,32,3,16]{1,3,2,0:T(8,128)S(1)}, f32[2,32,3,16]{1,3,2,0:T(8,128)S(1)}, u32[]{:S(2)}, u32[]{:S(2)}) %collective-permute-start.43) | collective-permute-done | bytes 12320 | tf_op jit(solution)/shard_map/ppermute | solution.py:40
  390.5 7.8 %collective-permute-start.45 = (f32[1,32,8,3]{1,3,2,0:T(4,128)S(1)}, f32[1,32,8,3]{1,3,2,0:T(4,128)S(1)}, u32[]{:S(2)}, u32[]{:S(2)}) collective-permute-start(f32[1,32,8,3]{1,3,2,0:T(4,128)S(1)} %get-tuple-element.110), channel_id=1, source_target_pairs={{4,0},{8,4},{12,8},{16,12},{20,16},{24,20},{28,24},{32,28},{36,32}... | collective-permute-start | bytes 9224 | tf_op jit(solution)/shard_map/ppermute | solution.py:40
  399.8 2.8 collective-permute-start.46
  404.6 7.1 %collective-permute-done.47 = f32[2,32,3,8]{1,3,2,0:T(8,128)S(1)} collective-permute-done((f32[2,32,3,8]{1,3,2,0:T(8,128)S(1)}, f32[2,32,3,8]{1,3,2,0:T(8,128)S(1)}, u32[]{:S(2)}, u32[]{:S(2)}) %collective-permute-start.47) | collective-permute-done | bytes 6176 | tf_op jit(solution)/shard_map/ppermute | solution.py:40
  414.0 7.5 %collective-permute-start.49 = (f32[4,32,2,8]{1,3,2,0:T(8,128)S(1)}, f32[4,32,2,8]{1,3,2,0:T(8,128)S(1)}, u32[]{:S(2)}, u32[]{:S(2)}) collective-permute-start(f32[4,32,2,8]{1,3,2,0:T(8,128)S(1)} %get-tuple-element.125), channel_id=1, source_target_pairs={{0,1},{1,2},{2,3},{4,5},{5,6},{6,7},{8,9},{9,10},{10,11},{12,13},{... | collective-permute-start | bytes 24584 | tf_op jit(solution)/shard_map/ppermute | solution.py:37
  422.8 7.9 %collective-permute-start.51 = (f32[2,32,8,2]{1,3,2,0:T(2,128)S(1)}, f32[2,32,8,2]{1,3,2,0:T(2,128)S(1)}, u32[]{:S(2)}, u32[]{:S(2)}) collective-permute-start(f32[2,32,8,2]{1,3,2,0:T(2,128)S(1)} %get-tuple-element.122), channel_id=1, source_target_pairs={{4,0},{8,4},{12,8},{16,12},{20,16},{24,20},{28,24},{32,28},{36,32}... | collective-permute-start | bytes 12296 | tf_op jit(solution)/shard_map/ppermute | solution.py:40
  434.2 9.0 %collective-permute-start.53 = (f32[4,32,2,16]{1,3,2,0:T(8,128)S(1)}, f32[4,32,2,16]{1,3,2,0:T(8,128)S(1)}, u32[]{:S(2)}, u32[]{:S(2)}) collective-permute-start(f32[4,32,2,16]{1,3,2,0:T(8,128)S(1)} %get-tuple-element.81), channel_id=1, source_target_pairs={{0,1},{1,2},{2,3},{4,5},{5,6},{6,7},{8,9},{9,10},{10,11},{12,13},{... | collective-permute-start | bytes 49160 | tf_op jit(solution)/shard_map/ppermute | solution.py:37
  443.2 2.1 convolution_bitcast_fusion.16
  446.3 8.1 %collective-permute-start.55 = (f32[2,32,16,2]{1,3,2,0:T(2,128)S(1)}, f32[2,32,16,2]{1,3,2,0:T(2,128)S(1)}, u32[]{:S(2)}, u32[]{:S(2)}) collective-permute-start(f32[2,32,16,2]{1,3,2,0:T(2,128)S(1)} %get-tuple-element.78), channel_id=1, source_target_pairs={{4,0},{8,4},{12,8},{16,12},{20,16},{24,20},{28,24},{32,28},{36,32}... | collective-permute-start | bytes 24584 | tf_op jit(solution)/shard_map/ppermute | solution.py:40
  454.8 73.3 %all-reduce = (f32[4,32,32]{2,1,0:T(8,128)S(1)}, f32[3,32,32]{2,1,0:T(8,128)S(1)}, f32[32,32]{0,1:T(8,128)S(1)}, f32[32]{0:T(128)S(1)}) all-reduce(f32[4,32,32]{2,1,0:T(8,128)S(1)} %convolution_bitcast_fusion.8, f32[3,32,32]{2,1,0:T(8,128)S(1)} %convolution_bitcast_fusion.11, ...), channel_id=1, replica_groups=mesh['lon'=64,'lat'=4] {'lon','lat'}, use_global_device_ids=true, to_apply=%region_0.0 | all-reduce | flops 8224 | bytes 65792 | tf_op jit(solution)/shard_map/psum | solution.py:211
  529.6 2.6 collective-permute-start.56
  532.2 6.9 %collective-permute-start.57 = (f32[1,32,2,32]{3,2,1,0:T(2,128)S(1)}, f32[1,32,2,32]{3,2,1,0:T(2,128)S(1)}, u32[]{:S(2)}, u32[]{:S(2)}) collective-permute-start(f32[1,32,2,32]{3,2,1,0:T(2,128)S(1)} %get-tuple-element.75), channel_id=1, source_target_pairs={{0,1},{1,2},{2,3},{4,5},{5,6},{6,7},{8,9},{9,10},{10,11},{12,13},{... | collective-permute-start | bytes 24584 | tf_op jit(solution)/shard_map/ppermute | solution.py:37
  541.3 9.6 %collective-permute-start.58 = (f32[1,32,32,2]{3,2,1,0:T(8,128)S(1)}, f32[1,32,32,2]{3,2,1,0:T(8,128)S(1)}, u32[]{:S(2)}, u32[]{:S(2)}) collective-permute-start(f32[1,32,32,2]{3,2,1,0:T(8,128)S(1)} %get-tuple-element.57), channel_id=1, source_target_pairs={{0,4},{4,8},{8,12},{12,16},{16,20},{20,24},{24,28},{28,32},{32,36}... | collective-permute-start | bytes 24584 | tf_op jit(solution)/shard_map/ppermute | solution.py:37
  551.5 9.6 %collective-permute-done.58 = f32[1,32,32,2]{3,2,1,0:T(8,128)S(1)} collective-permute-done((f32[1,32,32,2]{3,2,1,0:T(8,128)S(1)}, f32[1,32,32,2]{3,2,1,0:T(8,128)S(1)}, u32[]{:S(2)}, u32[]{:S(2)}) %collective-permute-start.58) | collective-permute-done | bytes 8224 | tf_op jit(solution)/shard_map/ppermute | solution.py:37
  561.1 3.5 collective-permute-done.59
  567.4 7.7 %collective-permute-start.61 = (f32[1,32,2,64]{3,2,1,0:T(2,128)S(1)}, f32[1,32,2,64]{3,2,1,0:T(2,128)S(1)}, u32[]{:S(2)}, u32[]{:S(2)}) collective-permute-start(f32[1,32,2,64]{3,2,1,0:T(2,128)S(1)} %get-tuple-element.55), channel_id=1, source_target_pairs={{0,1},{1,2},{2,3},{4,5},{5,6},{6,7},{8,9},{9,10},{10,11},{12,13},{... | collective-permute-start | bytes 49160 | tf_op jit(solution)/shard_map/ppermute | solution.py:37
  581.1 8.5 %collective-permute-start.63 = (f32[1,32,64,2]{2,1,3,0:T(8,128)S(1)}, f32[1,32,64,2]{2,1,3,0:T(8,128)S(1)}, u32[]{:S(2)}, u32[]{:S(2)}) collective-permute-start(f32[1,32,64,2]{2,1,3,0:T(8,128)S(1)} %copy.103), channel_id=1, source_target_pairs={{4,0},{8,4},{12,8},{16,12},{20,16},{24,20},{28,24},{32,28},{36,32}... | collective-permute-start | bytes 49160 | tf_op jit(solution)/shard_map/ppermute | solution.py:40
  593.2 4.0 convolution_add_fusion
  (370 shorter events, 140.7 us)
Async XLA Ops:
  3.0 13.4 %collective-permute-start = (f32[1,32,64,3]{2,1,3,0:T(8,128)S(1)}, f32[1,32,64,3]{2,1,3,0:T(8,128)S(1)}, u32[]{:S(2)}, u32[]{:S(2)}) collective-permute-start(f32[1,32,64,3]{2,1,3,0:T(8,128)S(1)} %copy.64), channel_id=1, source_target_pairs={{0,4},{4,8},{8,12},{12,16},{16,20},{20,24},{24,28},{28,32},{32,36}... | collective-permute-start | bytes 73736 | tf_op jit(solution)/shard_map/ppermute | solution.py:37
  5.9 10.9 %collective-permute-start.1 = (f32[1,32,64,3]{2,1,3,0:T(8,128)S(1)}, f32[1,32,64,3]{2,1,3,0:T(8,128)S(1)}, u32[]{:S(2)}, u32[]{:S(2)}) collective-permute-start(f32[1,32,64,3]{2,1,3,0:T(8,128)S(1)} %copy.65), channel_id=1, source_target_pairs={{4,0},{8,4},{12,8},{16,12},{20,16},{24,20},{28,24},{32,28},{36,32}... | collective-permute-start | bytes 73736 | tf_op jit(solution)/shard_map/ppermute | solution.py:40
  21.6 15.0 %collective-permute-start.2 = (f32[1,32,3,64]{3,2,1,0:T(4,128)S(1)}, f32[1,32,3,64]{3,2,1,0:T(4,128)S(1)}, u32[]{:S(2)}, u32[]{:S(2)}) collective-permute-start(f32[1,32,3,64]{3,2,1,0:T(4,128)S(1)} %get-tuple-element.43), channel_id=1, source_target_pairs={{0,1},{1,2},{2,3},{4,5},{5,6},{6,7},{8,9},{9,10},{10,11},{12,13},{... | collective-permute-start | bytes 73736 | tf_op jit(solution)/shard_map/ppermute | solution.py:37
  30.1 9.5 %collective-permute-start.3 = (f32[1,32,3,64]{3,2,1,0:T(4,128)S(1)}, f32[1,32,3,64]{3,2,1,0:T(4,128)S(1)}, u32[]{:S(2)}, u32[]{:S(2)}) collective-permute-start(f32[1,32,3,64]{3,2,1,0:T(4,128)S(1)} %get-tuple-element.44), channel_id=1, source_target_pairs={{1,0},{2,1},{3,2},{5,4},{6,5},{7,6},{9,8},{10,9},{11,10},{13,12},{... | collective-permute-start | bytes 73736 | tf_op jit(solution)/shard_map/ppermute | solution.py:40
  54.7 19.6 %collective-permute-start.4 = (f32[1,32,32,3]{3,2,1,0:T(8,128)S(1)}, f32[1,32,32,3]{3,2,1,0:T(8,128)S(1)}, u32[]{:S(2)}, u32[]{:S(2)}) collective-permute-start(f32[1,32,32,3]{3,2,1,0:T(8,128)S(1)} %get-tuple-element.69), channel_id=1, source_target_pairs={{0,4},{4,8},{8,12},{12,16},{16,20},{20,24},{24,28},{28,32},{32,36}... | collective-permute-start | bytes 36872 | tf_op jit(solution)/shard_map/ppermute | solution.py:37
  54.8 19.5 %collective-permute-start.5 = (f32[1,32,32,3]{3,2,1,0:T(8,128)S(1)}, f32[1,32,32,3]{3,2,1,0:T(8,128)S(1)}, u32[]{:S(2)}, u32[]{:S(2)}) collective-permute-start(f32[1,32,32,3]{3,2,1,0:T(8,128)S(1)} %get-tuple-element.70), channel_id=1, source_target_pairs={{4,0},{8,4},{12,8},{16,12},{20,16},{24,20},{28,24},{32,28},{36,32}... | collective-permute-start | bytes 36872 | tf_op jit(solution)/shard_map/ppermute | solution.py:40
  75.0 8.9 %collective-permute-start.6 = (f32[1,32,3,32]{3,2,1,0:T(4,128)S(1)}, f32[1,32,3,32]{3,2,1,0:T(4,128)S(1)}, u32[]{:S(2)}, u32[]{:S(2)}) collective-permute-start(f32[1,32,3,32]{3,2,1,0:T(4,128)S(1)} %get-tuple-element.67), channel_id=1, source_target_pairs={{0,1},{1,2},{2,3},{4,5},{5,6},{6,7},{8,9},{9,10},{10,11},{12,13},{... | collective-permute-start | bytes 36872 | tf_op jit(solution)/shard_map/ppermute | solution.py:37
  80.7 9.7 %collective-permute-start.7 = (f32[1,32,3,32]{3,2,1,0:T(4,128)S(1)}, f32[1,32,3,32]{3,2,1,0:T(4,128)S(1)}, u32[]{:S(2)}, u32[]{:S(2)}) collective-permute-start(f32[1,32,3,32]{3,2,1,0:T(4,128)S(1)} %get-tuple-element.68), channel_id=1, source_target_pairs={{1,0},{2,1},{3,2},{5,4},{6,5},{7,6},{9,8},{10,9},{11,10},{13,12},{... | collective-permute-start | bytes 36872 | tf_op jit(solution)/shard_map/ppermute | solution.py:40
  96.2 11.7 %collective-permute-start.8 = (f32[1,32,16,3]{3,2,1,0:T(8,128)S(1)}, f32[1,32,16,3]{3,2,1,0:T(8,128)S(1)}, u32[]{:S(2)}, u32[]{:S(2)}) collective-permute-start(f32[1,32,16,3]{3,2,1,0:T(8,128)S(1)} %get-tuple-element.97), channel_id=1, source_target_pairs={{0,4},{4,8},{8,12},{12,16},{16,20},{20,24},{24,28},{28,32},{32,36}... | collective-permute-start | bytes 18440 | tf_op jit(solution)/shard_map/ppermute | solution.py:37
  96.5 11.4 %collective-permute-start.9 = (f32[1,32,16,3]{3,2,1,0:T(8,128)S(1)}, f32[1,32,16,3]{3,2,1,0:T(8,128)S(1)}, u32[]{:S(2)}, u32[]{:S(2)}) collective-permute-start(f32[1,32,16,3]{3,2,1,0:T(8,128)S(1)} %get-tuple-element.98), channel_id=1, source_target_pairs={{4,0},{8,4},{12,8},{16,12},{20,16},{24,20},{28,24},{32,28},{36,32}... | collective-permute-start | bytes 18440 | tf_op jit(solution)/shard_map/ppermute | solution.py:40
  110.4 4.8 collective-permute-start.10
  113.3 9.3 %collective-permute-start.11 = (f32[2,32,3,16]{1,3,2,0:T(8,128)S(1)}, f32[2,32,3,16]{1,3,2,0:T(8,128)S(1)}, u32[]{:S(2)}, u32[]{:S(2)}) collective-permute-start(f32[2,32,3,16]{1,3,2,0:T(8,128)S(1)} %get-tuple-element.96), channel_id=1, source_target_pairs={{1,0},{2,1},{3,2},{5,4},{6,5},{7,6},{9,8},{10,9},{11,10},{13,12},{... | collective-permute-start | bytes 36872 | tf_op jit(solution)/shard_map/ppermute | solution.py:40
  122.8 8.8 %collective-permute-start.12 = (f32[1,32,8,3]{1,3,2,0:T(4,128)S(1)}, f32[1,32,8,3]{1,3,2,0:T(4,128)S(1)}, u32[]{:S(2)}, u32[]{:S(2)}) collective-permute-start(f32[1,32,8,3]{1,3,2,0:T(4,128)S(1)} %get-tuple-element.115), channel_id=1, source_target_pairs={{0,4},{4,8},{8,12},{12,16},{16,20},{20,24},{24,28},{28,32},{32,36}... | collective-permute-start | bytes 9224 | tf_op jit(solution)/shard_map/ppermute | solution.py:37
  122.9 8.7 %collective-permute-start.13 = (f32[1,32,8,3]{1,3,2,0:T(4,128)S(1)}, f32[1,32,8,3]{1,3,2,0:T(4,128)S(1)}, u32[]{:S(2)}, u32[]{:S(2)}) collective-permute-start(f32[1,32,8,3]{1,3,2,0:T(4,128)S(1)} %get-tuple-element.116), channel_id=1, source_target_pairs={{4,0},{8,4},{12,8},{16,12},{20,16},{24,20},{28,24},{32,28},{36,32}... | collective-permute-start | bytes 9224 | tf_op jit(solution)/shard_map/ppermute | solution.py:40
  132.1 4.9 collective-permute-start.14
  135.0 9.1 %collective-permute-start.15 = (f32[2,32,3,8]{1,3,2,0:T(8,128)S(1)}, f32[2,32,3,8]{1,3,2,0:T(8,128)S(1)}, u32[]{:S(2)}, u32[]{:S(2)}) collective-permute-start(f32[2,32,3,8]{1,3,2,0:T(8,128)S(1)} %get-tuple-element.144), channel_id=1, source_target_pairs={{1,0},{2,1},{3,2},{5,4},{6,5},{7,6},{9,8},{10,9},{11,10},{13,12},{... | collective-permute-start | bytes 18440 | tf_op jit(solution)/shard_map/ppermute | solution.py:40
  144.5 9.8 %collective-permute-start.16 = (f32[4,32,2,8]{1,3,2,0:T(8,128)S(1)}, f32[4,32,2,8]{1,3,2,0:T(8,128)S(1)}, u32[]{:S(2)}, u32[]{:S(2)}) collective-permute-start(f32[4,32,2,8]{1,3,2,0:T(8,128)S(1)} %get-tuple-element.138), channel_id=1, source_target_pairs={{1,0},{2,1},{3,2},{5,4},{6,5},{7,6},{9,8},{10,9},{11,10},{13,12},{... | collective-permute-start | bytes 24584 | tf_op jit(solution)/shard_map/ppermute | solution.py:40
  146.4 8.6 %collective-permute-start.17 = (f32[4,32,2,8]{1,3,2,0:T(8,128)S(1)}, f32[4,32,2,8]{1,3,2,0:T(8,128)S(1)}, u32[]{:S(2)}, u32[]{:S(2)}) collective-permute-start(f32[4,32,2,8]{1,3,2,0:T(8,128)S(1)} %get-tuple-element.137), channel_id=1, source_target_pairs={{0,1},{1,2},{2,3},{4,5},{5,6},{6,7},{8,9},{9,10},{10,11},{12,13},{... | collective-permute-start | bytes 24584 | tf_op jit(solution)/shard_map/ppermute | solution.py:37
  155.1 8.9 %collective-permute-start.18 = (f32[2,32,8,2]{1,3,2,0:T(2,128)S(1)}, f32[2,32,8,2]{1,3,2,0:T(2,128)S(1)}, u32[]{:S(2)}, u32[]{:S(2)}) collective-permute-start(f32[2,32,8,2]{1,3,2,0:T(2,128)S(1)} %get-tuple-element.133), channel_id=1, source_target_pairs={{0,4},{4,8},{8,12},{12,16},{16,20},{20,24},{24,28},{28,32},{32,36}... | collective-permute-start | bytes 12296 | tf_op jit(solution)/shard_map/ppermute | solution.py:37
  155.2 8.9 %collective-permute-start.19 = (f32[2,32,8,2]{1,3,2,0:T(2,128)S(1)}, f32[2,32,8,2]{1,3,2,0:T(2,128)S(1)}, u32[]{:S(2)}, u32[]{:S(2)}) collective-permute-start(f32[2,32,8,2]{1,3,2,0:T(2,128)S(1)} %get-tuple-element.134), channel_id=1, source_target_pairs={{4,0},{8,4},{12,8},{16,12},{20,16},{24,20},{28,24},{32,28},{36,32}... | collective-permute-start | bytes 12296 | tf_op jit(solution)/shard_map/ppermute | solution.py:40
  164.7 11.0 %collective-permute-start.20 = (f32[4,32,2,16]{1,3,2,0:T(8,128)S(1)}, f32[4,32,2,16]{1,3,2,0:T(8,128)S(1)}, u32[]{:S(2)}, u32[]{:S(2)}) collective-permute-start(f32[4,32,2,16]{1,3,2,0:T(8,128)S(1)} %get-tuple-element.94), channel_id=1, source_target_pairs={{1,0},{2,1},{3,2},{5,4},{6,5},{7,6},{9,8},{10,9},{11,10},{13,12},{... | collective-permute-start | bytes 49160 | tf_op jit(solution)/shard_map/ppermute | solution.py:40
  166.6 10.3 %collective-permute-start.21 = (f32[4,32,2,16]{1,3,2,0:T(8,128)S(1)}, f32[4,32,2,16]{1,3,2,0:T(8,128)S(1)}, u32[]{:S(2)}, u32[]{:S(2)}) collective-permute-start(f32[4,32,2,16]{1,3,2,0:T(8,128)S(1)} %get-tuple-element.93), channel_id=1, source_target_pairs={{0,1},{1,2},{2,3},{4,5},{5,6},{6,7},{8,9},{9,10},{10,11},{12,13},{... | collective-permute-start | bytes 49160 | tf_op jit(solution)/shard_map/ppermute | solution.py:37
  177.3 9.6 %collective-permute-start.22 = (f32[2,32,16,2]{1,3,2,0:T(2,128)S(1)}, f32[2,32,16,2]{1,3,2,0:T(2,128)S(1)}, u32[]{:S(2)}, u32[]{:S(2)}) collective-permute-start(f32[2,32,16,2]{1,3,2,0:T(2,128)S(1)} %get-tuple-element.89), channel_id=1, source_target_pairs={{0,4},{4,8},{8,12},{12,16},{16,20},{20,24},{24,28},{28,32},{32,36}... | collective-permute-start | bytes 24584 | tf_op jit(solution)/shard_map/ppermute | solution.py:37
  177.4 9.5 %collective-permute-start.23 = (f32[2,32,16,2]{1,3,2,0:T(2,128)S(1)}, f32[2,32,16,2]{1,3,2,0:T(2,128)S(1)}, u32[]{:S(2)}, u32[]{:S(2)}) collective-permute-start(f32[2,32,16,2]{1,3,2,0:T(2,128)S(1)} %get-tuple-element.90), channel_id=1, source_target_pairs={{4,0},{8,4},{12,8},{16,12},{20,16},{24,20},{28,24},{32,28},{36,32}... | collective-permute-start | bytes 24584 | tf_op jit(solution)/shard_map/ppermute | solution.py:40
  188.3 11.0 %collective-permute-start.24 = (f32[1,32,2,32]{3,2,1,0:T(2,128)S(1)}, f32[1,32,2,32]{3,2,1,0:T(2,128)S(1)}, u32[]{:S(2)}, u32[]{:S(2)}) collective-permute-start(f32[1,32,2,32]{3,2,1,0:T(2,128)S(1)} %get-tuple-element.88), channel_id=1, source_target_pairs={{1,0},{2,1},{3,2},{5,4},{6,5},{7,6},{9,8},{10,9},{11,10},{13,12},{... | collective-permute-start | bytes 24584 | tf_op jit(solution)/shard_map/ppermute | solution.py:40
  190.2 10.3 %collective-permute-start.25 = (f32[1,32,2,32]{3,2,1,0:T(2,128)S(1)}, f32[1,32,2,32]{3,2,1,0:T(2,128)S(1)}, u32[]{:S(2)}, u32[]{:S(2)}) collective-permute-start(f32[1,32,2,32]{3,2,1,0:T(2,128)S(1)} %get-tuple-element.87), channel_id=1, source_target_pairs={{0,1},{1,2},{2,3},{4,5},{5,6},{6,7},{8,9},{9,10},{10,11},{12,13},{... | collective-permute-start | bytes 24584 | tf_op jit(solution)/shard_map/ppermute | solution.py:37
  201.6 19.3 %collective-permute-start.26 = (f32[1,32,32,2]{3,2,1,0:T(8,128)S(1)}, f32[1,32,32,2]{3,2,1,0:T(8,128)S(1)}, u32[]{:S(2)}, u32[]{:S(2)}) collective-permute-start(f32[1,32,32,2]{3,2,1,0:T(8,128)S(1)} %get-tuple-element.65), channel_id=1, source_target_pairs={{0,4},{4,8},{8,12},{12,16},{16,20},{20,24},{24,28},{28,32},{32,36}... | collective-permute-start | bytes 24584 | tf_op jit(solution)/shard_map/ppermute | solution.py:37
  201.7 19.2 %collective-permute-start.27 = (f32[1,32,32,2]{3,2,1,0:T(8,128)S(1)}, f32[1,32,32,2]{3,2,1,0:T(8,128)S(1)}, u32[]{:S(2)}, u32[]{:S(2)}) collective-permute-start(f32[1,32,32,2]{3,2,1,0:T(8,128)S(1)} %get-tuple-element.66), channel_id=1, source_target_pairs={{4,0},{8,4},{12,8},{16,12},{20,16},{24,20},{28,24},{32,28},{36,32}... | collective-permute-start | bytes 24584 | tf_op jit(solution)/shard_map/ppermute | solution.py:40
  221.7 11.7 %collective-permute-start.28 = (f32[1,32,2,64]{3,2,1,0:T(2,128)S(1)}, f32[1,32,2,64]{3,2,1,0:T(2,128)S(1)}, u32[]{:S(2)}, u32[]{:S(2)}) collective-permute-start(f32[1,32,2,64]{3,2,1,0:T(2,128)S(1)} %get-tuple-element.64), channel_id=1, source_target_pairs={{1,0},{2,1},{3,2},{5,4},{6,5},{7,6},{9,8},{10,9},{11,10},{13,12},{... | collective-permute-start | bytes 49160 | tf_op jit(solution)/shard_map/ppermute | solution.py:40
  223.7 10.2 %collective-permute-start.29 = (f32[1,32,2,64]{3,2,1,0:T(2,128)S(1)}, f32[1,32,2,64]{3,2,1,0:T(2,128)S(1)}, u32[]{:S(2)}, u32[]{:S(2)}) collective-permute-start(f32[1,32,2,64]{3,2,1,0:T(2,128)S(1)} %get-tuple-element.63), channel_id=1, source_target_pairs={{0,1},{1,2},{2,3},{4,5},{5,6},{6,7},{8,9},{9,10},{10,11},{12,13},{... | collective-permute-start | bytes 49160 | tf_op jit(solution)/shard_map/ppermute | solution.py:37
  238.2 10.3 %collective-permute-start.30 = (f32[1,32,64,2]{2,1,3,0:T(8,128)S(1)}, f32[1,32,64,2]{2,1,3,0:T(8,128)S(1)}, u32[]{:S(2)}, u32[]{:S(2)}) collective-permute-start(f32[1,32,64,2]{2,1,3,0:T(8,128)S(1)} %copy.79), channel_id=1, source_target_pairs={{0,4},{4,8},{8,12},{12,16},{16,20},{20,24},{24,28},{28,32},{32,36}... | collective-permute-start | bytes 49160 | tf_op jit(solution)/shard_map/ppermute | solution.py:37
  238.9 11.1 %collective-permute-start.31 = (f32[1,32,64,2]{2,1,3,0:T(8,128)S(1)}, f32[1,32,64,2]{2,1,3,0:T(8,128)S(1)}, u32[]{:S(2)}, u32[]{:S(2)}) collective-permute-start(f32[1,32,64,2]{2,1,3,0:T(8,128)S(1)} %copy.80), channel_id=1, source_target_pairs={{4,0},{8,4},{12,8},{16,12},{20,16},{24,20},{28,24},{32,28},{36,32}... | collective-permute-start | bytes 49160 | tf_op jit(solution)/shard_map/ppermute | solution.py:40
  261.9 9.4 %collective-permute-start.32 = (f32[1,32,64,3]{2,1,3,0:T(8,128)S(1)}, f32[1,32,64,3]{2,1,3,0:T(8,128)S(1)}, u32[]{:S(2)}, u32[]{:S(2)}) collective-permute-start(f32[1,32,64,3]{2,1,3,0:T(8,128)S(1)} %copy.87), channel_id=1, source_target_pairs={{0,4},{4,8},{8,12},{12,16},{16,20},{20,24},{24,28},{28,32},{32,36}... | collective-permute-start | bytes 73736 | tf_op jit(solution)/shard_map/ppermute | solution.py:37
  263.4 9.3 %collective-permute-start.33 = (f32[1,32,64,3]{2,1,3,0:T(8,128)}, f32[1,32,64,3]{2,1,3,0:T(8,128)S(1)}, u32[]{:S(2)}, u32[]{:S(2)}) collective-permute-start(f32[1,32,64,3]{2,1,3,0:T(8,128)} %copy.88), channel_id=1, source_target_pairs={{4,0},{8,4},{12,8},{16,12},{20,16},{24,20},{28,24},{32,28},{36,32}... | collective-permute-start | bytes 73736 | tf_op jit(solution)/shard_map/ppermute | solution.py:40
  278.6 16.1 %collective-permute-start.34 = (f32[1,32,3,64]{3,2,1,0:T(4,128)}, f32[1,32,3,64]{3,2,1,0:T(4,128)S(1)}, u32[]{:S(2)}, u32[]{:S(2)}) collective-permute-start(f32[1,32,3,64]{3,2,1,0:T(4,128)} %get-tuple-element.36), channel_id=1, source_target_pairs={{0,1},{1,2},{2,3},{4,5},{5,6},{6,7},{8,9},{9,10},{10,11},{12,13},{... | collective-permute-start | bytes 73736 | tf_op jit(solution)/shard_map/ppermute | solution.py:37
  288.6 9.6 %collective-permute-start.35 = (f32[1,32,3,64]{3,2,1,0:T(4,128)S(1)}, f32[1,32,3,64]{3,2,1,0:T(4,128)}, u32[]{:S(2)}, u32[]{:S(2)}) collective-permute-start(f32[1,32,3,64]{3,2,1,0:T(4,128)S(1)} %get-tuple-element.37), channel_id=1, source_target_pairs={{1,0},{2,1},{3,2},{5,4},{6,5},{7,6},{9,8},{10,9},{11,10},{13,12},{... | collective-permute-start | bytes 73736 | tf_op jit(solution)/shard_map/ppermute | solution.py:40
  314.9 20.0 %collective-permute-start.36 = (f32[1,32,32,3]{3,2,1,0:T(8,128)S(1)}, f32[1,32,32,3]{3,2,1,0:T(8,128)S(1)}, u32[]{:S(2)}, u32[]{:S(2)}) collective-permute-start(f32[1,32,32,3]{3,2,1,0:T(8,128)S(1)} %get-tuple-element.61), channel_id=1, source_target_pairs={{0,4},{4,8},{8,12},{12,16},{16,20},{20,24},{24,28},{28,32},{32,36}... | collective-permute-start | bytes 36872 | tf_op jit(solution)/shard_map/ppermute | solution.py:37
  315.0 19.9 %collective-permute-start.37 = (f32[1,32,32,3]{3,2,1,0:T(8,128)S(1)}, f32[1,32,32,3]{3,2,1,0:T(8,128)S(1)}, u32[]{:S(2)}, u32[]{:S(2)}) collective-permute-start(f32[1,32,32,3]{3,2,1,0:T(8,128)S(1)} %get-tuple-element.62), channel_id=1, source_target_pairs={{4,0},{8,4},{12,8},{16,12},{20,16},{24,20},{28,24},{32,28},{36,32}... | collective-permute-start | bytes 36872 | tf_op jit(solution)/shard_map/ppermute | solution.py:40
  335.7 10.6 %collective-permute-start.38 = (f32[1,32,3,32]{3,2,1,0:T(4,128)S(1)}, f32[1,32,3,32]{3,2,1,0:T(4,128)S(1)}, u32[]{:S(2)}, u32[]{:S(2)}) collective-permute-start(f32[1,32,3,32]{3,2,1,0:T(4,128)S(1)} %get-tuple-element.59), channel_id=1, source_target_pairs={{0,1},{1,2},{2,3},{4,5},{5,6},{6,7},{8,9},{9,10},{10,11},{12,13},{... | collective-permute-start | bytes 36872 | tf_op jit(solution)/shard_map/ppermute | solution.py:37
  341.6 9.8 %collective-permute-start.39 = (f32[1,32,3,32]{3,2,1,0:T(4,128)S(1)}, f32[1,32,3,32]{3,2,1,0:T(4,128)}, u32[]{:S(2)}, u32[]{:S(2)}) collective-permute-start(f32[1,32,3,32]{3,2,1,0:T(4,128)S(1)} %get-tuple-element.60), channel_id=1, source_target_pairs={{1,0},{2,1},{3,2},{5,4},{6,5},{7,6},{9,8},{10,9},{11,10},{13,12},{... | collective-permute-start | bytes 36872 | tf_op jit(solution)/shard_map/ppermute | solution.py:40
  362.4 11.5 %collective-permute-start.40 = (f32[1,32,16,3]{3,2,1,0:T(8,128)S(1)}, f32[1,32,16,3]{3,2,1,0:T(8,128)S(1)}, u32[]{:S(2)}, u32[]{:S(2)}) collective-permute-start(f32[1,32,16,3]{3,2,1,0:T(8,128)S(1)} %get-tuple-element.85), channel_id=1, source_target_pairs={{0,4},{4,8},{8,12},{12,16},{16,20},{20,24},{24,28},{28,32},{32,36}... | collective-permute-start | bytes 18440 | tf_op jit(solution)/shard_map/ppermute | solution.py:37
  362.5 11.5 %collective-permute-start.41 = (f32[1,32,16,3]{3,2,1,0:T(8,128)S(1)}, f32[1,32,16,3]{3,2,1,0:T(8,128)S(1)}, u32[]{:S(2)}, u32[]{:S(2)}) collective-permute-start(f32[1,32,16,3]{3,2,1,0:T(8,128)S(1)} %get-tuple-element.86), channel_id=1, source_target_pairs={{4,0},{8,4},{12,8},{16,12},{20,16},{24,20},{28,24},{32,28},{36,32}... | collective-permute-start | bytes 18440 | tf_op jit(solution)/shard_map/ppermute | solution.py:40
  376.5 6.3 %collective-permute-start.42 = (f32[2,32,3,16]{1,3,2,0:T(8,128)S(1)}, f32[2,32,3,16]{1,3,2,0:T(8,128)S(1)}, u32[]{:S(2)}, u32[]{:S(2)}) collective-permute-start(f32[2,32,3,16]{1,3,2,0:T(8,128)S(1)} %get-tuple-element.83), channel_id=1, source_target_pairs={{0,1},{1,2},{2,3},{4,5},{5,6},{6,7},{8,9},{9,10},{10,11},{12,13},{... | collective-permute-start | bytes 36872 | tf_op jit(solution)/shard_map/ppermute | solution.py:37
  380.8 9.3 %collective-permute-start.43 = (f32[2,32,3,16]{1,3,2,0:T(8,128)S(1)}, f32[2,32,3,16]{1,3,2,0:T(8,128)S(1)}, u32[]{:S(2)}, u32[]{:S(2)}) collective-permute-start(f32[2,32,3,16]{1,3,2,0:T(8,128)S(1)} %get-tuple-element.84), channel_id=1, source_target_pairs={{1,0},{2,1},{3,2},{5,4},{6,5},{7,6},{9,8},{10,9},{11,10},{13,12},{... | collective-permute-start | bytes 36872 | tf_op jit(solution)/shard_map/ppermute | solution.py:40
  390.4 8.9 %collective-permute-start.44 = (f32[1,32,8,3]{1,3,2,0:T(4,128)S(1)}, f32[1,32,8,3]{1,3,2,0:T(4,128)S(1)}, u32[]{:S(2)}, u32[]{:S(2)}) collective-permute-start(f32[1,32,8,3]{1,3,2,0:T(4,128)S(1)} %get-tuple-element.109), channel_id=1, source_target_pairs={{0,4},{4,8},{8,12},{12,16},{16,20},{20,24},{24,28},{28,32},{32,36}... | collective-permute-start | bytes 9224 | tf_op jit(solution)/shard_map/ppermute | solution.py:37
  390.5 8.8 %collective-permute-start.45 = (f32[1,32,8,3]{1,3,2,0:T(4,128)S(1)}, f32[1,32,8,3]{1,3,2,0:T(4,128)S(1)}, u32[]{:S(2)}, u32[]{:S(2)}) collective-permute-start(f32[1,32,8,3]{1,3,2,0:T(4,128)S(1)} %get-tuple-element.110), channel_id=1, source_target_pairs={{4,0},{8,4},{12,8},{16,12},{20,16},{24,20},{28,24},{32,28},{36,32}... | collective-permute-start | bytes 9224 | tf_op jit(solution)/shard_map/ppermute | solution.py:40
  399.8 4.8 collective-permute-start.46
  402.6 9.1 %collective-permute-start.47 = (f32[2,32,3,8]{1,3,2,0:T(8,128)S(1)}, f32[2,32,3,8]{1,3,2,0:T(8,128)S(1)}, u32[]{:S(2)}, u32[]{:S(2)}) collective-permute-start(f32[2,32,3,8]{1,3,2,0:T(8,128)S(1)} %get-tuple-element.132), channel_id=1, source_target_pairs={{1,0},{2,1},{3,2},{5,4},{6,5},{7,6},{9,8},{10,9},{11,10},{13,12},{... | collective-permute-start | bytes 18440 | tf_op jit(solution)/shard_map/ppermute | solution.py:40
  412.0 9.8 %collective-permute-start.48 = (f32[4,32,2,8]{1,3,2,0:T(8,128)S(1)}, f32[4,32,2,8]{1,3,2,0:T(8,128)S(1)}, u32[]{:S(2)}, u32[]{:S(2)}) collective-permute-start(f32[4,32,2,8]{1,3,2,0:T(8,128)S(1)} %get-tuple-element.126), channel_id=1, source_target_pairs={{1,0},{2,1},{3,2},{5,4},{6,5},{7,6},{9,8},{10,9},{11,10},{13,12},{... | collective-permute-start | bytes 24584 | tf_op jit(solution)/shard_map/ppermute | solution.py:40
  414.0 8.6 %collective-permute-start.49 = (f32[4,32,2,8]{1,3,2,0:T(8,128)S(1)}, f32[4,32,2,8]{1,3,2,0:T(8,128)S(1)}, u32[]{:S(2)}, u32[]{:S(2)}) collective-permute-start(f32[4,32,2,8]{1,3,2,0:T(8,128)S(1)} %get-tuple-element.125), channel_id=1, source_target_pairs={{0,1},{1,2},{2,3},{4,5},{5,6},{6,7},{8,9},{9,10},{10,11},{12,13},{... | collective-permute-start | bytes 24584 | tf_op jit(solution)/shard_map/ppermute | solution.py:37
  422.7 9.0 %collective-permute-start.50 = (f32[2,32,8,2]{1,3,2,0:T(2,128)S(1)}, f32[2,32,8,2]{1,3,2,0:T(2,128)S(1)}, u32[]{:S(2)}, u32[]{:S(2)}) collective-permute-start(f32[2,32,8,2]{1,3,2,0:T(2,128)S(1)} %get-tuple-element.121), channel_id=1, source_target_pairs={{0,4},{4,8},{8,12},{12,16},{16,20},{20,24},{24,28},{28,32},{32,36}... | collective-permute-start | bytes 12296 | tf_op jit(solution)/shard_map/ppermute | solution.py:37
  422.8 8.9 %collective-permute-start.51 = (f32[2,32,8,2]{1,3,2,0:T(2,128)S(1)}, f32[2,32,8,2]{1,3,2,0:T(2,128)S(1)}, u32[]{:S(2)}, u32[]{:S(2)}) collective-permute-start(f32[2,32,8,2]{1,3,2,0:T(2,128)S(1)} %get-tuple-element.122), channel_id=1, source_target_pairs={{4,0},{8,4},{12,8},{16,12},{20,16},{24,20},{28,24},{32,28},{36,32}... | collective-permute-start | bytes 12296 | tf_op jit(solution)/shard_map/ppermute | solution.py:40
  432.3 13.5 %collective-permute-start.52 = (f32[4,32,2,16]{1,3,2,0:T(8,128)S(1)}, f32[4,32,2,16]{1,3,2,0:T(8,128)S(1)}, u32[]{:S(2)}, u32[]{:S(2)}) collective-permute-start(f32[4,32,2,16]{1,3,2,0:T(8,128)S(1)} %get-tuple-element.82), channel_id=1, source_target_pairs={{1,0},{2,1},{3,2},{5,4},{6,5},{7,6},{9,8},{10,9},{11,10},{13,12},{... | collective-permute-start | bytes 49160 | tf_op jit(solution)/shard_map/ppermute | solution.py:40
  434.2 11.6 %collective-permute-start.53 = (f32[4,32,2,16]{1,3,2,0:T(8,128)S(1)}, f32[4,32,2,16]{1,3,2,0:T(8,128)S(1)}, u32[]{:S(2)}, u32[]{:S(2)}) collective-permute-start(f32[4,32,2,16]{1,3,2,0:T(8,128)S(1)} %get-tuple-element.81), channel_id=1, source_target_pairs={{0,1},{1,2},{2,3},{4,5},{5,6},{6,7},{8,9},{9,10},{10,11},{12,13},{... | collective-permute-start | bytes 49160 | tf_op jit(solution)/shard_map/ppermute | solution.py:37
  446.2 81.9 %collective-permute-start.54 = (f32[2,32,16,2]{1,3,2,0:T(2,128)S(1)}, f32[2,32,16,2]{1,3,2,0:T(2,128)S(1)}, u32[]{:S(2)}, u32[]{:S(2)}) collective-permute-start(f32[2,32,16,2]{1,3,2,0:T(2,128)S(1)} %get-tuple-element.77), channel_id=1, source_target_pairs={{0,4},{4,8},{8,12},{12,16},{16,20},{20,24},{24,28},{28,32},{32,36}... | collective-permute-start | bytes 24584 | tf_op jit(solution)/shard_map/ppermute | solution.py:37
  446.3 81.8 %collective-permute-start.55 = (f32[2,32,16,2]{1,3,2,0:T(2,128)S(1)}, f32[2,32,16,2]{1,3,2,0:T(2,128)S(1)}, u32[]{:S(2)}, u32[]{:S(2)}) collective-permute-start(f32[2,32,16,2]{1,3,2,0:T(2,128)S(1)} %get-tuple-element.78), channel_id=1, source_target_pairs={{4,0},{8,4},{12,8},{16,12},{20,16},{24,20},{28,24},{32,28},{36,32}... | collective-permute-start | bytes 24584 | tf_op jit(solution)/shard_map/ppermute | solution.py:40
  529.6 10.1 %collective-permute-start.56 = (f32[1,32,2,32]{3,2,1,0:T(2,128)S(1)}, f32[1,32,2,32]{3,2,1,0:T(2,128)S(1)}, u32[]{:S(2)}, u32[]{:S(2)}) collective-permute-start(f32[1,32,2,32]{3,2,1,0:T(2,128)S(1)} %get-tuple-element.76), channel_id=1, source_target_pairs={{1,0},{2,1},{3,2},{5,4},{6,5},{7,6},{9,8},{10,9},{11,10},{13,12},{... | collective-permute-start | bytes 24584 | tf_op jit(solution)/shard_map/ppermute | solution.py:40
  532.2 8.1 %collective-permute-start.57 = (f32[1,32,2,32]{3,2,1,0:T(2,128)S(1)}, f32[1,32,2,32]{3,2,1,0:T(2,128)S(1)}, u32[]{:S(2)}, u32[]{:S(2)}) collective-permute-start(f32[1,32,2,32]{3,2,1,0:T(2,128)S(1)} %get-tuple-element.75), channel_id=1, source_target_pairs={{0,1},{1,2},{2,3},{4,5},{5,6},{6,7},{8,9},{9,10},{10,11},{12,13},{... | collective-permute-start | bytes 24584 | tf_op jit(solution)/shard_map/ppermute | solution.py:37
  541.3 19.8 %collective-permute-start.58 = (f32[1,32,32,2]{3,2,1,0:T(8,128)S(1)}, f32[1,32,32,2]{3,2,1,0:T(8,128)S(1)}, u32[]{:S(2)}, u32[]{:S(2)}) collective-permute-start(f32[1,32,32,2]{3,2,1,0:T(8,128)S(1)} %get-tuple-element.57), channel_id=1, source_target_pairs={{0,4},{4,8},{8,12},{12,16},{16,20},{20,24},{24,28},{28,32},{32,36}... | collective-permute-start | bytes 24584 | tf_op jit(solution)/shard_map/ppermute | solution.py:37
  550.9 13.7 %collective-permute-start.59 = (f32[1,32,32,2]{3,2,1,0:T(8,128)S(1)}, f32[1,32,32,2]{3,2,1,0:T(8,128)S(1)}, u32[]{:S(2)}, u32[]{:S(2)}) collective-permute-start(f32[1,32,32,2]{3,2,1,0:T(8,128)S(1)} %get-tuple-element.58), channel_id=1, source_target_pairs={{4,0},{8,4},{12,8},{16,12},{20,16},{24,20},{28,24},{32,28},{36,32}... | collective-permute-start | bytes 24584 | tf_op jit(solution)/shard_map/ppermute | solution.py:40
  565.5 9.6 %collective-permute-start.60 = (f32[1,32,2,64]{3,2,1,0:T(2,128)S(1)}, f32[1,32,2,64]{3,2,1,0:T(2,128)S(1)}, u32[]{:S(2)}, u32[]{:S(2)}) collective-permute-start(f32[1,32,2,64]{3,2,1,0:T(2,128)S(1)} %get-tuple-element.56), channel_id=1, source_target_pairs={{1,0},{2,1},{3,2},{5,4},{6,5},{7,6},{9,8},{10,9},{11,10},{13,12},{... | collective-permute-start | bytes 49160 | tf_op jit(solution)/shard_map/ppermute | solution.py:40
  567.4 8.7 %collective-permute-start.61 = (f32[1,32,2,64]{3,2,1,0:T(2,128)S(1)}, f32[1,32,2,64]{3,2,1,0:T(2,128)S(1)}, u32[]{:S(2)}, u32[]{:S(2)}) collective-permute-start(f32[1,32,2,64]{3,2,1,0:T(2,128)S(1)} %get-tuple-element.55), channel_id=1, source_target_pairs={{0,1},{1,2},{2,3},{4,5},{5,6},{6,7},{8,9},{9,10},{10,11},{12,13},{... | collective-permute-start | bytes 49160 | tf_op jit(solution)/shard_map/ppermute | solution.py:37
  580.4 11.0 %collective-permute-start.62 = (f32[1,32,64,2]{2,1,3,0:T(8,128)S(1)}, f32[1,32,64,2]{2,1,3,0:T(8,128)S(1)}, u32[]{:S(2)}, u32[]{:S(2)}) collective-permute-start(f32[1,32,64,2]{2,1,3,0:T(8,128)S(1)} %copy.102), channel_id=1, source_target_pairs={{0,4},{4,8},{8,12},{12,16},{16,20},{20,24},{24,28},{28,32},{32,36}... | collective-permute-start | bytes 49160 | tf_op jit(solution)/shard_map/ppermute | solution.py:37
  581.1 10.8 %collective-permute-start.63 = (f32[1,32,64,2]{2,1,3,0:T(8,128)S(1)}, f32[1,32,64,2]{2,1,3,0:T(8,128)S(1)}, u32[]{:S(2)}, u32[]{:S(2)}) collective-permute-start(f32[1,32,64,2]{2,1,3,0:T(8,128)S(1)} %copy.103), channel_id=1, source_target_pairs={{4,0},{8,4},{12,8},{16,12},{20,16},{24,20},{28,24},{32,28},{36,32}... | collective-permute-start | bytes 49160 | tf_op jit(solution)/shard_map/ppermute | solution.py:40
  (47 other events, 846.4 us)
where the time goes:
time: 607 us; the launch traced here: 598 us
  starting transfers between devices  271 us (45%)
  waiting for transfers between devices  111 us (18%)
  local copies, waits for them, and re-layouts  82.3 us (14%)
  blocking collectives  73.3 us (12%)
  matrix products  38.2 us (6%)
  other arithmetic  18.9 us (3%)
    ppermute x32, starting transfers between devices, with_halo(): lax.ppermute(lax.slice_in_dim(block, 0, width, axis=dim), axis, backward)  149 us
    ppermute x32, starting transfers between devices, with_halo(): lax.ppermute(lax.slice_in_dim(block, block.shape[dim] - width, None, axis...  123 us
    psum x1, blocking collectives, on_device(): lax.psum((contraction(coarse, grad_coarse), local_detail, local_skip, loc...  73.3 us
    ppermute x32, waiting for transfers between devices, with_halo(): lax.ppermute(lax.slice_in_dim(block, block.shape[dim] - width, None, axis...  61.4 us
    ppermute x32, waiting for transfers between devices, with_halo(): lax.ppermute(lax.slice_in_dim(block, 0, width, axis=dim), axis, backward)  49.3 us
    slice x28, local copies, waits for them, and re-layouts, filter_pass(): lax.slice_in_dim(padded, offset, offset + 2 * length - 1, 2, along)  43.4 us
    dot_general x24, matrix products, band_product(): jnp.einsum('abcp,pk->abck', values, table, precision=lax.Precision.HIGHEST)  30.1 us
    slice x30, local copies, waits for them, and re-layouts, with_halo(): lax.slice_in_dim(block, block.shape[dim] - width, None, axis=dim)  13.6 us
  transfers between devices with their start and end apart: 64, of which 29 were waited for; matrix products, arithmetic and copies ran while one was open for 6% of the time, Pallas kernels for 0%

commit v1 on v0

v1 whole, which is shorter than its diff:
```python
import math

import jax
import jax.numpy as jnp
import numpy as np
from jax import lax
from jax.experimental import pallas as pl
from jax.experimental.pallas import tpu as pltpu
from jax.sharding import PartitionSpec as P
from ml_dtypes import bfloat16

F32 = jnp.float32
BF16 = jnp.bfloat16

low_taps = (
    -0.010597401785069032,
    0.0328830116668852,
    0.030841381835560764,
    -0.18703481171909309,
    -0.027983769416859854,
    0.6308807679298589,
    0.7148465705529157,
    0.2303778133088965,
)
high_taps = (
    -0.2303778133088965,
    0.7148465705529157,
    -0.6308807679298589,
    -0.027983769416859854,
    0.18703481171909309,
    0.030841381835560764,
    -0.0328830116668852,
    -0.010597401785069032,
)

CHANNELS = 32
LAT_PARTS = 4
LAT_BLOCK = 64
LON_BLOCK = 128
LAT_BAND = (0, 1, 0, 1, 3, 2, 3)
LON_BAND = (0, 0, 1, 1, 2, 3, 3)
LO_LANES = 42
HI_LANE = 64


def level_matrix(size, taps, periodic):
    matrix = np.zeros((size // 2, size))
    for k in range(size // 2):
        for j in range(8):
            m = 2 * k + j - 3
            if periodic:
                matrix[k, m % size] += taps[j]
            elif 0 <= m < size:
                matrix[k, m] += taps[j]
    return matrix


def composed(size, periodic):
    two = level_matrix(size // 2, low_taps, periodic) @ level_matrix(size, low_taps, periodic)
    three_low = level_matrix(size // 4, low_taps, periodic) @ two
    three_high = level_matrix(size // 4, high_taps, periodic) @ two
    four_low = level_matrix(size // 8, low_taps, periodic) @ three_low
    four_high = level_matrix(size // 8, high_taps, periodic) @ three_low
    return (four_low, four_high, three_low, three_high)


def lane_table():
    lanes = [None] * 128
    inner = []
    for s in range(7):
        count = 14 if s < 4 else 22
        for e in range(6):
            lanes[s * 6 + e] = (s, e)
            lanes[HI_LANE + s * 6 + e] = (s, count - 6 + e)
        inner += [(s, e) for e in range(6, count - 6)]
    free = [lane for lane in range(128) if lanes[lane] is None]
    for lane, entry in zip(free, inner):
        lanes[lane] = entry
    return lanes


LANES = lane_table()
SUBBAND_OF_LANE = np.array([-1 if entry is None else entry[0] for entry in LANES])


def lon_weights():
    maps = composed(8 * LON_BLOCK, True)
    start = 3 * LON_BLOCK
    weights = np.zeros((4, LON_BLOCK, 128))
    for lane, entry in enumerate(LANES):
        if entry is None:
            continue
        s, e = entry
        per_block = 8 if s < 4 else 16
        row = maps[LON_BAND[s]][3 * per_block - 3 + e]
        weights[LAT_BAND[s], :, lane] = row[start : start + LON_BLOCK]
    return weights.reshape(4 * LON_BLOCK, 128)


def row_entries(part):
    top4, bottom4 = list(range(6)) + [None] * 2, list(range(4, 10)) + [None] * 2
    top3, bottom3 = list(range(8)), list(range(8, 14)) + [None] * 2
    four = bottom4 + top4 if part % 2 == 0 else top4 + bottom4
    three = bottom3 + top3 if part % 2 == 0 else top3 + bottom3
    four[14:16] = [8, 9] if part < 2 else [0, 1]
    return four, three


def lat_weights():
    maps = composed(LAT_PARTS * LAT_BLOCK, False)
    weights = np.zeros((LAT_PARTS, 4, 16, LAT_BLOCK))
    for part in range(LAT_PARTS):
        entries = row_entries(part)
        for band in range(4):
            per_block = 4 if band < 2 else 8
            for row, e in enumerate(entries[0 if band < 2 else 1]):
                k = per_block * part - 3 + e if e is not None else -1
                if 0 <= k < per_block * LAT_PARTS:
                    weights[part, band, row] = maps[band][
                        k, part * LAT_BLOCK : (part + 1) * LAT_BLOCK
                    ]
    return weights.reshape(LAT_PARTS, 64, LAT_BLOCK)


def own_mask():
    mask = np.ones((LAT_PARTS, 16, 128), np.float32)
    four = (SUBBAND_OF_LANE >= 0) & (SUBBAND_OF_LANE < 4)
    for part in range(LAT_PARTS):
        bottom = 0 if part % 2 == 0 else 8
        for row in (bottom, bottom + 1, 14, 15):
            mask[part, row, four] = 0.0
    return mask


def high_low(matrix):
    matrix = matrix.astype(np.float32)
    high = matrix.astype(bfloat16)
    low = (matrix - high.astype(np.float32)).astype(bfloat16)
    return np.stack([high, low], axis=-3)


LON = lon_weights()
LAT = lat_weights()
LON_A = high_low(LON)
LON_S = high_low(LON.T)
LAT_A = high_low(np.stack([np.kron(np.eye(4), LAT[p]) for p in range(LAT_PARTS)]))
LAT_S = high_low(np.stack([np.kron(np.eye(4), LAT[p].T) for p in range(LAT_PARTS)]))
OWN = own_mask()


def split(x):
    high = x.astype(BF16)
    low = (x - high.astype(F32)).astype(BF16)
    return high, low


def dot(a, b):
    return jnp.dot(a, b, preferred_element_type=F32)


def dot_nt(a, b):
    return lax.dot_general(a, b, (((1,), (1,)), ((), ())), preferred_element_type=F32)


def dot3(a, b, product=dot):
    return product(a[0], b[0]) + (product(a[0], b[1]) + product(a[1], b[0]))


def both(ref):
    return ref[0], ref[1]


def grouped(x):
    return jnp.concatenate([x[4 * g : 4 * g + 4].reshape(256, 128) for g in range(8)], axis=1)


def tiled(x):
    return jnp.concatenate(
        [x[:, 8 * t : 8 * t + 8, :].reshape(256, 128) for t in range(8)], axis=1
    )


def analysis(groups, lat, lon):
    rows = dot3(lat, split(groups))
    blocks = []
    for g in range(8):
        part = rows[:, 128 * g : 128 * g + 128].reshape(4, 4, 16, 128)
        blocks.append(
            jnp.concatenate([part[:, b].reshape(64, 128) for b in range(4)], axis=1)
        )
    return dot3(split(jnp.concatenate(blocks, axis=0)), lon).reshape(32, 16, 128)


def synthesis(frame, lat, lon):
    wide = dot3(split(frame), lon).reshape(8, 4, 16, 512)
    groups = []
    for g in range(8):
        part = jnp.stack(
            [wide[g, :, :, 128 * b : 128 * b + 128] for b in range(4)], axis=1
        )
        groups.append(part.reshape(256, 128))
    return dot3(lat, split(jnp.concatenate(groups, axis=1)))


def lane_index(shape):
    return lax.broadcasted_iota(jnp.int32, shape, len(shape) - 1)


def subband_lanes(shape, s):
    lane = lax.rem(lane_index(shape), 128)
    mask = (lane >= 6 * s) & (lane < 6 * s + 6)
    mask = mask | ((lane >= HI_LANE + 6 * s) & (lane < HI_LANE + 6 * s + 6))
    inner = [i for i in range(128) if LANES[i] is not None and LANES[i][0] == s]
    inner = [i for i in inner if not (i < LO_LANES or HI_LANE <= i < HI_LANE + LO_LANES)]
    runs = []
    for i in inner:
        if runs and runs[-1][1] == i:
            runs[-1][1] = i + 1
        else:
            runs.append([i, i + 1])
    for first, last in runs:
        mask = mask | ((lane >= first) & (lane < last))
    return mask


def roll64(x):
    return pltpu.roll(x, 64, 2)


def whole(frame_a, frame_b, from_left, from_right):
    lane = lane_index(frame_a.shape)
    low = lane < LO_LANES
    high = (lane >= HI_LANE) & (lane < HI_LANE + LO_LANES)
    frame_a = frame_a + jnp.where(low, from_left, 0.0) + jnp.where(high, roll64(from_right), 0.0)
    frame_b = frame_b + jnp.where(low, roll64(from_left), 0.0) + jnp.where(high, from_right, 0.0)
    return frame_a, frame_b


def mixed(frame_a, frame_b, weights_ref):
    data = split(
        jnp.concatenate([frame_a.reshape(256, 128), frame_b.reshape(256, 128)], axis=1)
    )
    result = jnp.zeros((256, 256), F32)
    for s in range(7):
        product = dot3((weights_ref[s, 0], weights_ref[s, 1]), data)
        result = jnp.where(subband_lanes((256, 256), s), product, result)
    return jnp.concatenate(
        [result[:, :128].reshape(32, 8, 128), result[:, 128:].reshape(32, 8, 128)], axis=1
    ).reshape(512, 128)


def store_frame(frame, a_ref, b_ref, far_ref):
    a_ref[...] = frame[:, :8]
    b_ref[...] = frame[:, 8:]
    far_ref[...] = frame[:, 14:16]


def analysis_kernel(part_ref, x_ref, lat_ref, lon_ref, a_ref, b_ref, far_ref):
    frame = analysis(grouped(x_ref[...]), both(lat_ref[0]), both(lon_ref))
    store_frame(frame, a_ref, b_ref, far_ref)


def expand_matrix():
    row = lax.broadcasted_iota(jnp.int32, (256, 32), 0)
    return (row // 8 == lane_index((256, 32))).astype(BF16)


def same_row(shape):
    row = lax.broadcasted_iota(jnp.int32, shape, 0)
    return lax.rem(row, 8) == lax.rem(lane_index(shape), 8)


def prepare_kernel(x_ref, coarse_ref, detail_ref, skip_ref, bias_ref, mix_ref, unmix_ref, pre_ref):
    expand = expand_matrix()
    diagonal = same_row((256, 256))
    for s in range(8):
        weight = coarse_ref[s] if s < 4 else (detail_ref[s - 4] if s < 7 else skip_ref[...])
        for k, part in enumerate(split(weight)):
            forward = dot_nt(dot_nt(expand, part).astype(BF16), expand)
            backward = dot_nt(dot(expand, part).astype(BF16), expand)
            mix_ref[s, k] = jnp.where(diagonal, forward, 0.0).astype(BF16)
            unmix_ref[s, k] = jnp.where(diagonal, backward, 0.0).astype(BF16)
    product = dot3((mix_ref[7, 0], mix_ref[7, 1]), split(tiled(x_ref[...])))
    bias = bias_ref[...]
    for t in range(8):
        pre_ref[:, 8 * t : 8 * t + 8, :] = (
            product[:, 128 * t : 128 * t + 128].reshape(32, 8, 128) + bias
        )


def lat_sum_kernel(
    part_ref, mask_ref, a_ref, b_ref, near_ref, other_ref, far_ref, fa_ref, fb_ref, low_ref, high_ref
):
    shape = (32, 8, 128)
    keep = lax.broadcasted_iota(jnp.int32, shape, 1) < 6
    mask = mask_ref[0]
    frame_a = a_ref[...] * mask[None, :8] + jnp.where(keep, near_ref[...], 0.0)
    frame_b = b_ref[...] * mask[None, 8:] + jnp.where(keep, other_ref[...], 0.0)
    fa_ref[...] = frame_a
    fb_ref[...] = frame_b
    lane = lane_index((32, 2, 128))
    four = lane < 0
    for s in range(4):
        four = four | subband_lanes((32, 2, 128), s)
    fb_ref[:, 6:8, :] += jnp.where(four, far_ref[...], 0.0)
    frame_b = fb_ref[...]
    first = lane_index(shape) < 64
    low_ref[...] = jnp.where(first, frame_a, roll64(frame_b))
    high_ref[...] = jnp.where(first, roll64(frame_a), frame_b)


def forward_kernel(
    part_ref,
    fa_ref,
    fb_ref,
    left_ref,
    right_ref,
    pre_ref,
    cot_ref,
    mix_ref,
    lat_a_ref,
    lat_s_ref,
    lon_a_ref,
    lon_s_ref,
    act_ref,
    grad_ref,
    ca_ref,
    cb_ref,
    a_ref,
    b_ref,
    far_ref,
):
    frame_a, frame_b = whole(fa_ref[...], fb_ref[...], left_ref[...], right_ref[...])
    ca_ref[...] = frame_a
    cb_ref[...] = frame_b
    kernel = synthesis(mixed(frame_a, frame_b, mix_ref), both(lat_s_ref[0]), both(lon_s_ref))
    grads = []
    for g in range(8):
        channels = slice(4 * g, 4 * g + 4)
        pre = kernel[:, 128 * g : 128 * g + 128] + pre_ref[channels].reshape(256, 128)
        cumulative = 0.5 * (1.0 + lax.erf(pre * math.sqrt(0.5)))
        density = jnp.exp(-0.5 * pre * pre) * (1.0 / math.sqrt(2.0 * math.pi))
        act_ref[channels] = (pre * cumulative).astype(BF16).reshape(4, 64, 128)
        grad = cot_ref[channels].astype(F32).reshape(256, 128) * (cumulative + pre * density)
        grad_ref[channels] = grad.reshape(4, 64, 128)
        grads.append(grad)
    frame = analysis(jnp.concatenate(grads, axis=1), both(lat_a_ref[0]), both(lon_a_ref))
    store_frame(frame, a_ref, b_ref, far_ref)


def weights_kernel(x_ref, g_ref, ca_ref, cb_ref, a_ref, b_ref, sum_ref):
    diagonal = same_row((256, 256))

    def reduced(product):
        rows = jnp.where(diagonal, product, 0.0).reshape(32, 8, 256)
        return split(jnp.sum(rows, axis=1))

    def placed(parts, offset):
        row = lax.broadcasted_iota(jnp.int32, (256, 128), 0)
        place = (row // 8 + offset == lane_index((256, 128))).astype(BF16)
        return dot(parts[0], place) + dot(parts[1], place)

    coef = jnp.concatenate([ca_ref[...].reshape(256, 128), cb_ref[...].reshape(256, 128)], axis=1)
    grad = split(
        jnp.concatenate([a_ref[...].reshape(256, 128), b_ref[...].reshape(256, 128)], axis=1)
    )
    sums = [jnp.zeros((32, 128), F32), jnp.zeros((32, 128), F32)]
    for s in range(7):
        chosen = split(jnp.where(subband_lanes((256, 256), s), coef, 0.0))
        product = dot3(chosen, grad, dot_nt)
        sums[s // 4] = sums[s // 4] + placed(reduced(product), 32 * (s % 4))
    field = split(tiled(x_ref[...]))
    grad_pre = split(tiled(g_ref[...]))
    sums[1] = sums[1] + placed(reduced(dot3(field, grad_pre, dot_nt)), 96)
    ones = jnp.ones((8, 1024), BF16)
    bias = split(dot_nt(ones, grad_pre[0]) + dot_nt(ones, grad_pre[1]))
    sum_ref[0:32] = sums[0]
    sum_ref[32:64] = sums[1]
    sum_ref[64:72] = placed(bias, 0)


def skip_back_kernel(g_ref, unmix_ref, out_ref):
    product = dot3((unmix_ref[7, 0], unmix_ref[7, 1]), split(tiled(g_ref[...])))
    for t in range(8):
        out_ref[:, 8 * t : 8 * t + 8, :] = product[:, 128 * t : 128 * t + 128].reshape(32, 8, 128)


def backward_kernel(
    part_ref, fa_ref, fb_ref, left_ref, right_ref, skip_ref, unmix_ref, lat_s_ref, lon_s_ref, out_ref
):
    frame_a, frame_b = whole(fa_ref[...], fb_ref[...], left_ref[...], right_ref[...])
    field = synthesis(mixed(frame_a, frame_b, unmix_ref), both(lat_s_ref[0]), both(lon_s_ref))
    for g in range(8):
        channels = slice(4 * g, 4 * g + 4)
        out_ref[channels] = skip_ref[channels] + field[:, 128 * g : 128 * g + 128].reshape(
            4, 64, 128
        )


def full_spec(shape):
    return pl.BlockSpec(shape, lambda *_: (0,) * len(shape))


def part_spec(shape):
    return pl.BlockSpec(shape, lambda _, part: (part[0],) + (0,) * (len(shape) - 1))


def shape_of(*shape, dtype=F32):
    return jax.ShapeDtypeStruct(shape, dtype)


def call(kernel, outs, args, part=None, by_part=()):
    in_specs = [
        part_spec((1,) + arg.shape[1:]) if i in by_part else full_spec(arg.shape)
        for i, arg in enumerate(args)
    ]
    out_specs = [full_spec(out.shape) for out in outs]
    params = pltpu.CompilerParams(vmem_limit_bytes=48 * 1024 * 1024)
    if part is None:
        return pl.pallas_call(
            kernel,
            grid=(1,),
            in_specs=in_specs,
            out_specs=out_specs,
            out_shape=list(outs),
            compiler_params=params,
        )(*args)
    grid_spec = pltpu.PrefetchScalarGridSpec(
        num_scalar_prefetch=1, grid=(1,), in_specs=in_specs, out_specs=out_specs
    )
    return pl.pallas_call(
        kernel, grid_spec=grid_spec, out_shape=list(outs), compiler_params=params
    )(part, *args)


TILE = shape_of(32, 8, 128)
FAR = shape_of(32, 2, 128)
FIELD = shape_of(32, 64, 128)


def exchange(a, b, far, part):
    near = lax.ppermute(a, "lat", [(i, i ^ 1) for i in range(LAT_PARTS)])
    other = lax.ppermute(b, "lat", [(1, 2), (2, 1)])
    far = lax.ppermute(far, "lat", [(i, i ^ 2) for i in range(LAT_PARTS)])
    fa, fb, low, high = call(
        lat_sum_kernel, (TILE,) * 4, (jnp.asarray(OWN), a, b, near, other, far), part, (0,)
    )
    count = lax.axis_size("lon")
    from_left = lax.ppermute(high, "lon", [(i, (i + 1) % count) for i in range(count)])
    from_right = lax.ppermute(low, "lon", [((i + 1) % count, i) for i in range(count)])
    return fa, fb, from_left, from_right


def total(values):
    for step in (1, 2):
        values = values + lax.ppermute(
            values, "lat", [(i, i ^ step) for i in range(lax.axis_size("lat"))]
        )
    for step in (1, 2, 4, 8, 16, 32):
        values = values + lax.ppermute(
            values, "lon", [(i, i ^ step) for i in range(lax.axis_size("lon"))]
        )
    return values


def on_device(ocean_field, cotangent, mix_coarse, mix_detail, skip_weight, bias_vector):
    part = lax.axis_index("lat").astype(jnp.int32).reshape(1)
    lat_a, lat_s = jnp.asarray(LAT_A), jnp.asarray(LAT_S)
    lon_a, lon_s = jnp.asarray(LON_A), jnp.asarray(LON_S)
    a, b, far = call(
        analysis_kernel, (TILE, TILE, FAR), (ocean_field, lat_a, lon_a), part, (1,)
    )
    weights = shape_of(8, 2, 256, 256, dtype=BF16)
    bias = jnp.broadcast_to(bias_vector[:, None, None], (CHANNELS, 1, 128))
    mix, unmix, pre = call(
        prepare_kernel,
        (weights, weights, FIELD),
        (ocean_field, mix_coarse, mix_detail, skip_weight, bias),
    )
    fa, fb, from_left, from_right = exchange(a, b, far, part)
    activated, grad_pre, coef_a, coef_b, a, b, far = call(
        forward_kernel,
        (shape_of(32, 64, 128, dtype=BF16), FIELD, TILE, TILE, TILE, TILE, FAR),
        (fa, fb, from_left, from_right, pre, cotangent, mix, lat_a, lat_s, lon_a, lon_s),
        part,
        (7, 8),
    )
    (sums,) = call(
        weights_kernel, (shape_of(72, 128),), (ocean_field, grad_pre, coef_a, coef_b, a, b)
    )
    (skip_back,) = call(skip_back_kernel, (FIELD,), (grad_pre, unmix))
    fa, fb, from_left, from_right = exchange(a, b, far, part)
    (grad_field,) = call(
        backward_kernel,
        (FIELD,),
        (fa, fb, from_left, from_right, skip_back, unmix, lat_s, lon_s),
        part,
        (6,),
    )
    sums = total(sums)
    cells = LAT_PARTS * LAT_BLOCK * LON_BLOCK * lax.axis_size("lon")
    coarse = sums[0:32].reshape(32, 4, 32).transpose(1, 0, 2) / math.sqrt(cells // 256)
    detail = sums[32:64, :96].reshape(32, 3, 32).transpose(1, 0, 2) / math.sqrt(cells // 64)
    grad_skip = sums[32:64, 96:] / math.sqrt(cells)
    grad_bias = sums[64, :32] / math.sqrt(cells)
    return (activated, grad_field, coarse, detail, grad_skip, grad_bias)


def solution(mesh):
    return jax.shard_map(
        on_device,
        mesh=mesh,
        in_specs=(P(None, "lat", "lon"), P(None, "lat", "lon"), P(), P(), P(), P()),
        out_specs=(P(None, "lat", "lon"), P(None, "lat", "lon"), P(), P(), P(), P()),
        check_vma=False,
    )
```

time: 607 us -> 99.1 us (0.16)
  the two profiles are of different devices: /device:TPU:1 before, /device:TPU:16 now
where the time goes in v1:
time: 99.1 us; the launch traced here: 98.6 us
  starting transfers between devices  44.6 us (45%)
  waiting for transfers between devices  21.2 us (21%)
  Pallas kernels  20.8 us (21%)
  local copies, waits for them, and re-layouts  9.97 us (10%)
  other arithmetic  1.25 us (1%)
    ppermute x2, starting transfers between devices, exchange(): far = lax.ppermute(far, 'lat', [(i, i ^ 2) for i in range(LAT_PARTS)])  13 us
    ppermute x6, waiting for transfers between devices, total(): lax.ppermute(values, 'lon', [(i, i ^ step) for i in range(lax.axis_size('...  12.3 us
    ppermute x2, starting transfers between devices, exchange(): lax.ppermute(low, 'lon', [((i + 1) % count, i) for i in range(count)])  12 us
    pallas_call x5, Pallas kernels, call(): pl.pallas_call(kernel, grid_spec=grid_spec, out_shape=list(outs), compile...  10.9 us
    ppermute x2, starting transfers between devices, total(): lax.ppermute(values, 'lat', [(i, i ^ step) for i in range(lax.axis_size('...  10.1 us
    pallas_call x3, Pallas kernels, call(): pl.pallas_call(kernel, grid=(1,), in_specs=in_specs, out_specs=out_specs,...  9.9 us
    unnamed x35, local copies, waits for them, and re-layouts  9.07 us
    ppermute x6, starting transfers between devices, total(): lax.ppermute(values, 'lon', [(i, i ^ step) for i in range(lax.axis_size('...  6.16 us
  transfers between devices with their start and end apart: 18, of which 8 were waited for; matrix products, arithmetic and copies ran while one was open for 0% of the time, Pallas kernels for 9%

profile of v1, /device:TPU:16, one launch (start us, length us, event | category | flops | bytes accessed | tf_op | source)
XLA Modules:
  0.0 98.6 jit_solution(16648404826438092018)
XLA Ops:
  0.6 0.0 copy-start
  0.7 1.2 %copy-done = f32[32,64,128]{2,1,0:T(8,128)S(1)} copy-done((f32[32,64,128]{2,1,0:T(8,128)S(1)}, f32[32,64,128]{2,1,0:T(8,128)}, u32[]{:S(2)}) %copy-start) | copy-done | bytes 1048600
  1.9 1.2 %copy-done.3 = bf16[4,2,256,256]{3,2,1,0:T(8,128)(2,1)S(1)} copy-done((bf16[4,2,256,256]{3,2,1,0:T(8,128)(2,1)S(1)}, bf16[4,2,256,256]{3,2,1,0:T(8,128)(2,1)}, u32[]{:S(2)}) %copy-start.3) | copy-done | bytes 1048600
  3.1 0.9 copy-done.8
  4.1 1.1 %shard_map.154 = (f32[32,8,128]{2,1,0:T(8,128)S(1)}, f32[32,8,128]{2,1,0:T(8,128)S(1)}, f32[32,2,128]{2,1,0:T(2,128)S(1)}) custom-call(s32[1]{0:T(128)} %bitcast.part_ref, f32[32,64,128]{2,1,0:T(8,128)S(1)} %copy-done, bf16[4,2,256,256]{3,2,1,0:T(8,128)(2,1)S(1)} %copy-done.3, bf16[2,512,128]{2,1,0:T(8,128)(2,1)S(1)} %copy-done.8), custom_call_target="tpu_custom_call" | custom-call | tf_op jit(solution)/shard_map/pallas_call | solution.py:431
  5.1 0.1 collective-permute-start
  5.2 0.7 collective-permute-start.1
  5.9 8.5 %collective-permute-start.2 = (f32[32,2,128]{2,1,0:T(2,128)S(1)}, f32[32,2,128]{2,1,0:T(2,128)S(1)}, u32[]{:S(2)}, u32[]{:S(2)}) collective-permute-start(f32[32,2,128]{2,1,0:T(2,128)S(1)} %get-tuple-element.29), channel_id=1, source_target_pairs={{0,2},{1,3},{2,0},{3,1},{4,6},{5,7},{6,4},{7,5},{8,10},{9,11},{10,... | collective-permute-start | bytes 98312 | tf_op jit(solution)/shard_map/ppermute | solution.py:444
  14.4 3.3 %collective-permute-done.2.far_ref = f32[32,2,128]{2,1,0:T(2,128)S(1)} collective-permute-done((f32[32,2,128]{2,1,0:T(2,128)S(1)}, f32[32,2,128]{2,1,0:T(2,128)S(1)}, u32[]{:S(2)}, u32[]{:S(2)}) %collective-permute-start.2) | collective-permute-done | bytes 32800 | tf_op jit(solution)/shard_map/ppermute | solution.py:444
  17.7 0.0 collective-permute-done.near_ref
  17.7 0.0 collective-permute-done.1.other_ref
  17.7 0.8 copy-done.11
  18.5 0.2 shard_map.155
  18.7 1.1 %collective-permute-start.3 = (f32[32,8,128]{2,1,0:T(8,128)S(1)}, f32[32,8,128]{2,1,0:T(8,128)S(1)}, u32[]{:S(2)}, u32[]{:S(2)}) collective-permute-start(f32[32,8,128]{2,1,0:T(8,128)S(1)} %get-tuple-element.32), channel_id=1, source_target_pairs={{0,4},{4,8},{8,12},{12,16},{16,20},{20,24},{24,28},{28,32},{32,36}... | collective-permute-start | bytes 393224 | tf_op jit(solution)/shard_map/ppermute | solution.py:449
  19.8 5.8 %collective-permute-start.4 = (f32[32,8,128]{2,1,0:T(8,128)S(1)}, f32[32,8,128]{2,1,0:T(8,128)S(1)}, u32[]{:S(2)}, u32[]{:S(2)}) collective-permute-start(f32[32,8,128]{2,1,0:T(8,128)S(1)} %get-tuple-element.33), channel_id=1, source_target_pairs={{4,0},{8,4},{12,8},{16,12},{20,16},{24,20},{28,24},{32,28},{36,32}... | collective-permute-start | bytes 393224 | tf_op jit(solution)/shard_map/ppermute | solution.py:450
  25.6 0.1 broadcast_in_dim.2.bias_ref
  25.7 0.0 copy-done.1
  25.7 0.0 copy-start.13
  25.7 0.8 copy-done.13
  26.5 0.8 copy-done.14
  27.3 0.7 copy-done.15
  28.0 4.9 %shard_map.156 = (bf16[8,2,256,256]{3,2,1,0:T(8,128)(2,1)S(1)}, bf16[8,2,256,256]{3,2,1,0:T(8,128)(2,1)}, f32[32,64,128]{2,1,0:T(8,128)S(1)}) custom-call(f32[32,64,128]{2,1,0:T(8,128)S(1)} %copy-done.1, f32[4,32,32]{2,1,0:T(8,128)S(1)} %copy-done.13, f32[3,32,32]{2,1,0:T(8,128)S(1)} %copy-done.14, f32[32,32]{1,0:T(8,128)S(1)} %copy-done.15, ...), custom_call_target="tpu_custom_call" | custom-call | tf_op jit(solution)/shard_map/pallas_call | solution.py:420
  32.9 1.3 %copy-done.6 = bf16[8,2,256,256]{3,2,1,0:T(8,128)(2,1)} copy-done((bf16[8,2,256,256]{3,2,1,0:T(8,128)(2,1)}, bf16[8,2,256,256]{3,2,1,0:T(8,128)(2,1)S(1)}, u32[]{:S(2)}) %copy-start.6) | copy-done | bytes 2097176
  34.3 0.0 collective-permute-done.3.left_ref
  34.3 0.0 collective-permute-done.4.right_ref
  34.3 5.8 %shard_map.157 = (bf16[32,64,128]{2,1,0:T(8,128)(2,1)}, f32[32,64,128]{2,1,0:T(8,128)S(1)}, f32[32,8,128]{2,1,0:T(8,128)S(1)}, f32[32,8,128]{2,1,0:T(8,128)S(1)}...) custom-call(s32[1]{0:T(128)} %bitcast.part_ref, ...), custom_call_target="tpu_custom_call" | custom-call | tf_op jit(solution)/shard_map/pallas_call | solution.py:431
  40.1 0.0 copy-start.12
  40.1 4.4 %shard_map.161 = f32[72,128]{1,0:T(8,128)S(1)} custom-call(f32[32,64,128]{2,1,0:T(8,128)S(1)} %copy-done.1, f32[32,64,128]{2,1,0:T(8,128)S(1)} %get-tuple-element.44.g_ref, f32[32,8,128]{2,1,0:T(8,128)S(1)} %get-tuple-element.46.ca_ref, f32[32,8,128]{2,1,0:T(8,128)S(1)} %get-tuple-element.47.cb_ref, f32[32,8,128]{2,1,0:T(8,128)S(1)} %get-tuple-element.37.a_ref, ...), custom_call_target="tpu_custom_call" | custom-call | tf_op jit(solution)/shard_map/pallas_call | solution.py:420
  44.5 3.0 %collective-permute-start.10 = (f32[72,128]{1,0:T(8,128)S(1)}, f32[72,128]{1,0:T(8,128)S(1)}, u32[]{:S(2)}, u32[]{:S(2)}) collective-permute-start(f32[72,128]{1,0:T(8,128)S(1)} %shard_map.161), channel_id=1, source_target_pairs={{0,1},{1,0},{2,3},{3,2},{4,5},{5,4},{6,7},{7,6},{8,9},{9,8},{10,11... | collective-permute-start | bytes 110600 | tf_op jit(solution)/shard_map/ppermute | solution.py:456
  47.5 0.1 collective-permute-start.5
  47.5 0.7 collective-permute-start.6
  48.2 0.1 collective-permute-done.10
  48.3 7.2 %collective-permute-start.11 = (f32[72,128]{1,0:T(8,128)S(1)}, f32[72,128]{1,0:T(8,128)S(1)}, u32[]{:S(2)}, u32[]{:S(2)}) collective-permute-start(f32[72,128]{1,0:T(8,128)S(1)} %add.24), channel_id=1, source_target_pairs={{0,2},{1,3},{2,0},{3,1},{4,6},{5,7},{6,4},{7,5},{8,10},{9,11},{10,... | collective-permute-start | bytes 110600 | tf_op jit(solution)/shard_map/ppermute | solution.py:456
  55.5 3.4 %collective-permute-done.11 = f32[72,128]{1,0:T(8,128)S(1)} collective-permute-done((f32[72,128]{1,0:T(8,128)S(1)}, f32[72,128]{1,0:T(8,128)S(1)}, u32[]{:S(2)}, u32[]{:S(2)}) %collective-permute-start.11) | collective-permute-done | bytes 36896 | tf_op jit(solution)/shard_map/ppermute | solution.py:456
  59.0 0.0 collective-permute-start.12
  59.0 4.3 %collective-permute-done.12 = f32[72,128]{1,0:T(8,128)S(1)} collective-permute-done((f32[72,128]{1,0:T(8,128)S(1)}, f32[72,128]{1,0:T(8,128)S(1)}, u32[]{:S(2)}, u32[]{:S(2)}) %collective-permute-start.12) | collective-permute-done | bytes 36896 | tf_op jit(solution)/shard_map/ppermute | solution.py:460
  63.2 0.0 collective-permute-start.13
  63.3 4.4 %collective-permute-start.7 = (f32[32,2,128]{2,1,0:T(2,128)S(1)}, f32[32,2,128]{2,1,0:T(2,128)S(1)}, u32[]{:S(2)}, u32[]{:S(2)}) collective-permute-start(f32[32,2,128]{2,1,0:T(2,128)S(1)} %get-tuple-element.39), channel_id=1, source_target_pairs={{0,2},{1,3},{2,0},{3,1},{4,6},{5,7},{6,4},{7,5},{8,10},{9,11},{10,... | collective-permute-start | bytes 98312 | tf_op jit(solution)/shard_map/ppermute | solution.py:444
  67.7 0.6 collective-permute-done.13
  68.3 1.1 %collective-permute-start.14 = (f32[72,128]{1,0:T(8,128)S(1)}, f32[72,128]{1,0:T(8,128)S(1)}, u32[]{:S(2)}, u32[]{:S(2)}) collective-permute-start(f32[72,128]{1,0:T(8,128)S(1)} %add.27), channel_id=1, source_target_pairs={{0,16},{4,20},{8,24},{12,28},{16,0},{20,4},{24,8},{28,12},{32,48},... | collective-permute-start | bytes 110600 | tf_op jit(solution)/shard_map/ppermute | solution.py:460
  69.4 2.0 %collective-permute-done.7.far_ref = f32[32,2,128]{2,1,0:T(2,128)S(1)} collective-permute-done((f32[32,2,128]{2,1,0:T(2,128)S(1)}, f32[32,2,128]{2,1,0:T(2,128)S(1)}, u32[]{:S(2)}, u32[]{:S(2)}) %collective-permute-start.7) | collective-permute-done | bytes 32800 | tf_op jit(solution)/shard_map/ppermute | solution.py:444
  71.4 0.0 collective-permute-done.5.near_ref
  71.4 0.0 collective-permute-done.6.other_ref
  71.4 0.2 shard_map.158
  71.6 0.7 collective-permute-start.8
  72.3 6.2 %collective-permute-start.9 = (f32[32,8,128]{2,1,0:T(8,128)S(1)}, f32[32,8,128]{2,1,0:T(8,128)S(1)}, u32[]{:S(2)}, u32[]{:S(2)}) collective-permute-start(f32[32,8,128]{2,1,0:T(8,128)S(1)} %get-tuple-element.43), channel_id=1, source_target_pairs={{4,0},{8,4},{12,8},{16,12},{20,16},{24,20},{28,24},{32,28},{36,32}... | collective-permute-start | bytes 393224 | tf_op jit(solution)/shard_map/ppermute | solution.py:450
  78.5 0.0 collective-permute-done.14
  78.5 0.8 collective-permute-start.15
  79.3 4.8 %collective-permute-done.15 = f32[72,128]{1,0:T(8,128)S(1)} collective-permute-done((f32[72,128]{1,0:T(8,128)S(1)}, f32[72,128]{1,0:T(8,128)S(1)}, u32[]{:S(2)}, u32[]{:S(2)}) %collective-permute-start.15) | collective-permute-done | bytes 36896 | tf_op jit(solution)/shard_map/ppermute | solution.py:460
  84.1 1.3 %collective-permute-start.16 = (f32[72,128]{1,0:T(8,128)S(1)}, f32[72,128]{1,0:T(8,128)S(1)}, u32[]{:S(2)}, u32[]{:S(2)}) collective-permute-start(f32[72,128]{1,0:T(8,128)S(1)} %add.29), channel_id=1, source_target_pairs={{0,64},{4,68},{8,72},{12,76},{16,80},{20,84},{24,88},{28,92},{32,9... | collective-permute-start | bytes 110600 | tf_op jit(solution)/shard_map/ppermute | solution.py:460
  85.4 2.7 %collective-permute-done.16 = f32[72,128]{1,0:T(8,128)S(1)} collective-permute-done((f32[72,128]{1,0:T(8,128)S(1)}, f32[72,128]{1,0:T(8,128)S(1)}, u32[]{:S(2)}, u32[]{:S(2)}) %collective-permute-start.16) | collective-permute-done | bytes 36896 | tf_op jit(solution)/shard_map/ppermute | solution.py:460
  88.0 3.0 %collective-permute-start.17 = (f32[72,128]{1,0:T(8,128)S(1)}, f32[72,128]{1,0:T(8,128)S(1)}, u32[]{:S(2)}, u32[]{:S(2)}) collective-permute-start(f32[72,128]{1,0:T(8,128)S(1)} %add.30), channel_id=1, source_target_pairs={{0,128},{4,132},{8,136},{12,140},{16,144},{20,148},{24,152},{28,15... | collective-permute-start | bytes 110600 | tf_op jit(solution)/shard_map/ppermute | solution.py:460
  91.1 0.6 shard_map.159.skip_ref
  91.7 0.0 collective-permute-done.8.left_ref
  91.7 0.0 collective-permute-done.9.right_ref
  91.7 0.6 copy-done.5
  92.3 3.7 %shard_map.160 = f32[32,64,128]{2,1,0:T(8,128)} custom-call(s32[1]{0:T(128)} %bitcast.part_ref, f32[32,8,128]{2,1,0:T(8,128)S(1)} %get-tuple-element.40.fa_ref, f32[32,8,128]{2,1,0:T(8,128)S(1)} %get-tuple-element.41.fb_ref, f32[32,8,128]{2,1,0:T(8,128)S(1)} %collective-permute-done.8.left_ref, f32[32,8,128]{2,1,0:T(8,128)S(1)} %collective-permute-done.9.right_ref, ...), custom_call_target="tpu_custom_call" | custom-call | tf_op jit(solution)/shard_map/pallas_call | solution.py:431
  96.0 0.0 collective-permute-done.17
  96.0 0.5 fusion
  96.5 0.7 slice_multiply_fusion
  97.2 0.1 div.36
  97.3 0.6 copy.22
  97.9 0.1 div.40
  98.0 0.6 copy.20
  (31 shorter events, 0.1 us)
Async XLA Ops:
  0.6 24.9 %copy-start.16 = (f32[32]{0:T(128)S(1)}, f32[32]{0:T(128)}, u32[]{:S(2)}) copy-start(f32[32]{0:T(128)} %param.16) | copy-start | bytes 388
  0.6 1.2 %copy-start = (f32[32,64,128]{2,1,0:T(8,128)S(1)}, f32[32,64,128]{2,1,0:T(8,128)}, u32[]{:S(2)}) copy-start(f32[32,64,128]{2,1,0:T(8,128)} %x_ref.5) | copy-start | bytes 3145732
  1.9 1.2 %copy-start.3 = (bf16[4,2,256,256]{3,2,1,0:T(8,128)(2,1)S(1)}, bf16[4,2,256,256]{3,2,1,0:T(8,128)(2,1)}, u32[]{:S(2)}) copy-start(bf16[4,2,256,256]{3,2,1,0:T(8,128)(2,1)} %constant.25.clone.lat_ref.lat_a_ref) | copy-start | bytes 3145732
  3.1 0.9 copy-start.8
  4.0 21.6 %copy-start.1 = (f32[32,64,128]{2,1,0:T(8,128)S(1)}, f32[32,64,128]{2,1,0:T(8,128)}, u32[]{:S(2)}) copy-start(f32[32,64,128]{2,1,0:T(8,128)} %x_ref.5) | copy-start | bytes 3145732
  4.1 30.2 %copy-start.4 = (bf16[4,2,256,256]{3,2,1,0:T(8,128)(2,1)S(1)}, bf16[4,2,256,256]{3,2,1,0:T(8,128)(2,1)}, u32[]{:S(2)}) copy-start(bf16[4,2,256,256]{3,2,1,0:T(8,128)(2,1)} %constant.25.clone.lat_ref.lat_a_ref) | copy-start | bytes 3145732
  4.1 30.2 %copy-start.7 = (bf16[2,128,512]{2,1,0:T(8,128)(2,1)S(1)}, bf16[2,128,512]{2,1,0:T(8,128)(2,1)}, u32[]{:S(2)}) copy-start(bf16[2,128,512]{2,1,0:T(8,128)(2,1)} %constant.28.clone.lon_s_ref) | copy-start | bytes 786436
  4.1 30.2 %copy-start.9 = (bf16[2,512,128]{2,1,0:T(8,128)(2,1)S(1)}, bf16[2,512,128]{2,1,0:T(8,128)(2,1)}, u32[]{:S(2)}) copy-start(bf16[2,512,128]{2,1,0:T(8,128)(2,1)} %constant.27.clone.lon_ref.lon_a_ref) | copy-start | bytes 786436
  4.1 30.2 %copy-start.10 = (bf16[32,64,128]{2,1,0:T(8,128)(2,1)S(1)}, bf16[32,64,128]{2,1,0:T(8,128)(2,1)}, u32[]{:S(2)}) copy-start(bf16[32,64,128]{2,1,0:T(8,128)(2,1)} %cot_ref.1) | copy-start | bytes 1572868
  5.1 12.6 %collective-permute-start = (f32[32,8,128]{2,1,0:T(8,128)S(1)}, f32[32,8,128]{2,1,0:T(8,128)S(1)}, u32[]{:S(2)}, u32[]{:S(2)}) collective-permute-start(f32[32,8,128]{2,1,0:T(8,128)S(1)} %get-tuple-element.27.a_ref), channel_id=1, source_target_pairs={{0,1},{1,0},{2,3},{3,2},{4,5},{5,4},{6,7},{7,6},{8,9},{9,8},{10,11... | collective-permute-start | bytes 393224 | tf_op jit(solution)/shard_map/ppermute | solution.py:442
  5.2 12.5 %collective-permute-start.1 = (f32[32,8,128]{2,1,0:T(8,128)S(1)}, f32[32,8,128]{2,1,0:T(8,128)S(1)}, u32[]{:S(2)}, u32[]{:S(2)}) collective-permute-start(f32[32,8,128]{2,1,0:T(8,128)S(1)} %get-tuple-element.28.b_ref), channel_id=1, source_target_pairs={{1,2},{2,1},{5,6},{6,5},{9,10},{10,9},{13,14},{14,13},{17,18},{18,... | collective-permute-start | bytes 393224 | tf_op jit(solution)/shard_map/ppermute | solution.py:443
  5.9 11.8 %collective-permute-start.2 = (f32[32,2,128]{2,1,0:T(2,128)S(1)}, f32[32,2,128]{2,1,0:T(2,128)S(1)}, u32[]{:S(2)}, u32[]{:S(2)}) collective-permute-start(f32[32,2,128]{2,1,0:T(2,128)S(1)} %get-tuple-element.29), channel_id=1, source_target_pairs={{0,2},{1,3},{2,0},{3,1},{4,6},{5,7},{6,4},{7,5},{8,10},{9,11},{10,... | collective-permute-start | bytes 98312 | tf_op jit(solution)/shard_map/ppermute | solution.py:444
  17.7 0.8 copy-start.11
  18.7 15.6 %collective-permute-start.3 = (f32[32,8,128]{2,1,0:T(8,128)S(1)}, f32[32,8,128]{2,1,0:T(8,128)S(1)}, u32[]{:S(2)}, u32[]{:S(2)}) collective-permute-start(f32[32,8,128]{2,1,0:T(8,128)S(1)} %get-tuple-element.32), channel_id=1, source_target_pairs={{0,4},{4,8},{8,12},{12,16},{16,20},{20,24},{24,28},{28,32},{32,36}... | collective-permute-start | bytes 393224 | tf_op jit(solution)/shard_map/ppermute | solution.py:449
  19.8 14.5 %collective-permute-start.4 = (f32[32,8,128]{2,1,0:T(8,128)S(1)}, f32[32,8,128]{2,1,0:T(8,128)S(1)}, u32[]{:S(2)}, u32[]{:S(2)}) collective-permute-start(f32[32,8,128]{2,1,0:T(8,128)S(1)} %get-tuple-element.33), channel_id=1, source_target_pairs={{4,0},{8,4},{12,8},{16,12},{20,16},{24,20},{28,24},{32,28},{36,32}... | collective-permute-start | bytes 393224 | tf_op jit(solution)/shard_map/ppermute | solution.py:450
  25.7 0.8 copy-start.13
  26.5 0.8 copy-start.14
  27.3 0.7 copy-start.15
  32.9 1.3 %copy-start.6 = (bf16[8,2,256,256]{3,2,1,0:T(8,128)(2,1)}, bf16[8,2,256,256]{3,2,1,0:T(8,128)(2,1)S(1)}, u32[]{:S(2)}) copy-start(bf16[8,2,256,256]{3,2,1,0:T(8,128)(2,1)S(1)} %get-tuple-element.35.mix_ref) | copy-start | bytes 6291460
  40.1 31.3 %copy-start.12 = (f32[4,16,128]{2,1,0:T(8,128)S(1)}, f32[4,16,128]{2,1,0:T(8,128)}, u32[]{:S(2)}) copy-start(f32[4,16,128]{2,1,0:T(8,128)} %constant.29.clone.mask_ref) | copy-start | bytes 98308
  40.1 50.9 %copy-start.2 = (bf16[8,2,256,256]{3,2,1,0:T(8,128)(2,1)S(1)}, bf16[8,2,256,256]{3,2,1,0:T(8,128)(2,1)}, u32[]{:S(2)}) copy-start(bf16[8,2,256,256]{3,2,1,0:T(8,128)(2,1)} %get-tuple-element.45.unmix_ref) | copy-start | bytes 6291460
  44.5 3.8 %collective-permute-start.10 = (f32[72,128]{1,0:T(8,128)S(1)}, f32[72,128]{1,0:T(8,128)S(1)}, u32[]{:S(2)}, u32[]{:S(2)}) collective-permute-start(f32[72,128]{1,0:T(8,128)S(1)} %shard_map.161), channel_id=1, source_target_pairs={{0,1},{1,0},{2,3},{3,2},{4,5},{5,4},{6,7},{7,6},{8,9},{9,8},{10,11... | collective-permute-start | bytes 110600 | tf_op jit(solution)/shard_map/ppermute | solution.py:456
  47.5 23.9 %collective-permute-start.5 = (f32[32,8,128]{2,1,0:T(8,128)S(1)}, f32[32,8,128]{2,1,0:T(8,128)S(1)}, u32[]{:S(2)}, u32[]{:S(2)}) collective-permute-start(f32[32,8,128]{2,1,0:T(8,128)S(1)} %get-tuple-element.37.a_ref), channel_id=1, source_target_pairs={{0,1},{1,0},{2,3},{3,2},{4,5},{5,4},{6,7},{7,6},{8,9},{9,8},{10,11... | collective-permute-start | bytes 393224 | tf_op jit(solution)/shard_map/ppermute | solution.py:442
  47.5 23.9 %collective-permute-start.6 = (f32[32,8,128]{2,1,0:T(8,128)S(1)}, f32[32,8,128]{2,1,0:T(8,128)S(1)}, u32[]{:S(2)}, u32[]{:S(2)}) collective-permute-start(f32[32,8,128]{2,1,0:T(8,128)S(1)} %get-tuple-element.38.b_ref), channel_id=1, source_target_pairs={{1,2},{2,1},{5,6},{6,5},{9,10},{10,9},{13,14},{14,13},{17,18},{18,... | collective-permute-start | bytes 393224 | tf_op jit(solution)/shard_map/ppermute | solution.py:443
  48.3 10.6 %collective-permute-start.11 = (f32[72,128]{1,0:T(8,128)S(1)}, f32[72,128]{1,0:T(8,128)S(1)}, u32[]{:S(2)}, u32[]{:S(2)}) collective-permute-start(f32[72,128]{1,0:T(8,128)S(1)} %add.24), channel_id=1, source_target_pairs={{0,2},{1,3},{2,0},{3,1},{4,6},{5,7},{6,4},{7,5},{8,10},{9,11},{10,... | collective-permute-start | bytes 110600 | tf_op jit(solution)/shard_map/ppermute | solution.py:456
  59.0 4.3 %collective-permute-start.12 = (f32[72,128]{1,0:T(8,128)S(1)}, f32[72,128]{1,0:T(8,128)S(1)}, u32[]{:S(2)}, u32[]{:S(2)}) collective-permute-start(f32[72,128]{1,0:T(8,128)S(1)} %add.25), channel_id=1, source_target_pairs={{0,4},{4,0},{8,12},{12,8},{16,20},{20,16},{24,28},{28,24},{32,36},... | collective-permute-start | bytes 110600 | tf_op jit(solution)/shard_map/ppermute | solution.py:460
  63.2 5.1 %collective-permute-start.13 = (f32[72,128]{1,0:T(8,128)S(1)}, f32[72,128]{1,0:T(8,128)S(1)}, u32[]{:S(2)}, u32[]{:S(2)}) collective-permute-start(f32[72,128]{1,0:T(8,128)S(1)} %add.26), channel_id=1, source_target_pairs={{0,8},{4,12},{8,0},{12,4},{16,24},{20,28},{24,16},{28,20},{32,40},... | collective-permute-start | bytes 110600 | tf_op jit(solution)/shard_map/ppermute | solution.py:460
  63.3 8.1 %collective-permute-start.7 = (f32[32,2,128]{2,1,0:T(2,128)S(1)}, f32[32,2,128]{2,1,0:T(2,128)S(1)}, u32[]{:S(2)}, u32[]{:S(2)}) collective-permute-start(f32[32,2,128]{2,1,0:T(2,128)S(1)} %get-tuple-element.39), channel_id=1, source_target_pairs={{0,2},{1,3},{2,0},{3,1},{4,6},{5,7},{6,4},{7,5},{8,10},{9,11},{10,... | collective-permute-start | bytes 98312 | tf_op jit(solution)/shard_map/ppermute | solution.py:444
  68.3 10.2 %collective-permute-start.14 = (f32[72,128]{1,0:T(8,128)S(1)}, f32[72,128]{1,0:T(8,128)S(1)}, u32[]{:S(2)}, u32[]{:S(2)}) collective-permute-start(f32[72,128]{1,0:T(8,128)S(1)} %add.27), channel_id=1, source_target_pairs={{0,16},{4,20},{8,24},{12,28},{16,0},{20,4},{24,8},{28,12},{32,48},... | collective-permute-start | bytes 110600 | tf_op jit(solution)/shard_map/ppermute | solution.py:460
  71.6 20.1 %collective-permute-start.8 = (f32[32,8,128]{2,1,0:T(8,128)S(1)}, f32[32,8,128]{2,1,0:T(8,128)S(1)}, u32[]{:S(2)}, u32[]{:S(2)}) collective-permute-start(f32[32,8,128]{2,1,0:T(8,128)S(1)} %get-tuple-element.42), channel_id=1, source_target_pairs={{0,4},{4,8},{8,12},{12,16},{16,20},{20,24},{24,28},{28,32},{32,36}... | collective-permute-start | bytes 393224 | tf_op jit(solution)/shard_map/ppermute | solution.py:449
  72.3 19.4 %collective-permute-start.9 = (f32[32,8,128]{2,1,0:T(8,128)S(1)}, f32[32,8,128]{2,1,0:T(8,128)S(1)}, u32[]{:S(2)}, u32[]{:S(2)}) collective-permute-start(f32[32,8,128]{2,1,0:T(8,128)S(1)} %get-tuple-element.43), channel_id=1, source_target_pairs={{4,0},{8,4},{12,8},{16,12},{20,16},{24,20},{28,24},{32,28},{36,32}... | collective-permute-start | bytes 393224 | tf_op jit(solution)/shard_map/ppermute | solution.py:450
  78.5 5.5 %collective-permute-start.15 = (f32[72,128]{1,0:T(8,128)S(1)}, f32[72,128]{1,0:T(8,128)S(1)}, u32[]{:S(2)}, u32[]{:S(2)}) collective-permute-start(f32[72,128]{1,0:T(8,128)S(1)} %add.28), channel_id=1, source_target_pairs={{0,32},{4,36},{8,40},{12,44},{16,48},{20,52},{24,56},{28,60},{32,0... | collective-permute-start | bytes 110600 | tf_op jit(solution)/shard_map/ppermute | solution.py:460
  84.1 4.0 %collective-permute-start.16 = (f32[72,128]{1,0:T(8,128)S(1)}, f32[72,128]{1,0:T(8,128)S(1)}, u32[]{:S(2)}, u32[]{:S(2)}) collective-permute-start(f32[72,128]{1,0:T(8,128)S(1)} %add.29), channel_id=1, source_target_pairs={{0,64},{4,68},{8,72},{12,76},{16,80},{20,84},{24,88},{28,92},{32,9... | collective-permute-start | bytes 110600 | tf_op jit(solution)/shard_map/ppermute | solution.py:460
  88.0 7.9 %collective-permute-start.17 = (f32[72,128]{1,0:T(8,128)S(1)}, f32[72,128]{1,0:T(8,128)S(1)}, u32[]{:S(2)}, u32[]{:S(2)}) collective-permute-start(f32[72,128]{1,0:T(8,128)S(1)} %add.30), channel_id=1, source_target_pairs={{0,128},{4,132},{8,136},{12,140},{16,144},{20,148},{24,152},{28,15... | collective-permute-start | bytes 110600 | tf_op jit(solution)/shard_map/ppermute | solution.py:460
  91.1 1.2 %copy-start.5 = (bf16[4,2,256,256]{3,2,1,0:T(8,128)(2,1)S(1)}, bf16[4,2,256,256]{3,2,1,0:T(8,128)(2,1)}, u32[]{:S(2)}) copy-start(bf16[4,2,256,256]{3,2,1,0:T(8,128)(2,1)} %constant.26.clone.lat_s_ref) | copy-start | bytes 3145732

commit v2 on v1

--- a/solution.py
+++ b/solution.py
@@ -1,3 +1,4 @@
+import functools
 import math
 
 import jax
@@ -143,9 +144,10 @@
 LAT = lat_weights()
 LON_A = high_low(LON)
 LON_S = high_low(LON.T)
-LAT_A = high_low(np.stack([np.kron(np.eye(4), LAT[p]) for p in range(LAT_PARTS)]))
-LAT_S = high_low(np.stack([np.kron(np.eye(4), LAT[p].T) for p in range(LAT_PARTS)]))
+LAT_A = high_low(np.stack([np.tile(LAT[p], (1, 4)) for p in range(LAT_PARTS)]))
+LAT_S = high_low(np.stack([np.tile(LAT[p].T, (1, 4)) for p in range(LAT_PARTS)]))
 OWN = own_mask()
+SUBBANDS = np.tile(SUBBAND_OF_LANE.astype(np.float32), (8, 1))
 
 
 def split(x):
@@ -168,6 +170,15 @@
 
 def both(ref):
     return ref[0], ref[1]
+
+
+def block_diagonal(ref):
+    row = lax.broadcasted_iota(jnp.int32, (256, 256), 0)
+    keep = row // 64 == lane_index((256, 256)) // 64
+    return tuple(
+        jnp.where(keep, jnp.concatenate([ref[0, k]] * 4, axis=0), 0.0).astype(BF16)
+        for k in range(2)
+    )
 
 
 def grouped(x):
@@ -206,23 +217,6 @@
     return lax.broadcasted_iota(jnp.int32, shape, len(shape) - 1)
 
 
-def subband_lanes(shape, s):
-    lane = lax.rem(lane_index(shape), 128)
-    mask = (lane >= 6 * s) & (lane < 6 * s + 6)
-    mask = mask | ((lane >= HI_LANE + 6 * s) & (lane < HI_LANE + 6 * s + 6))
-    inner = [i for i in range(128) if LANES[i] is not None and LANES[i][0] == s]
-    inner = [i for i in inner if not (i < LO_LANES or HI_LANE <= i < HI_LANE + LO_LANES)]
-    runs = []
-    for i in inner:
-        if runs and runs[-1][1] == i:
-            runs[-1][1] = i + 1
-        else:
-            runs.append([i, i + 1])
-    for first, last in runs:
-        mask = mask | ((lane >= first) & (lane < last))
-    return mask
-
-
 def roll64(x):
     return pltpu.roll(x, 64, 2)
 
@@ -236,17 +230,29 @@
     return frame_a, frame_b
 
 
-def mixed(frame_a, frame_b, weights_ref):
-    data = split(
-        jnp.concatenate([frame_a.reshape(256, 128), frame_b.reshape(256, 128)], axis=1)
-    )
-    result = jnp.zeros((256, 256), F32)
-    for s in range(7):
-        product = dot3((weights_ref[s, 0], weights_ref[s, 1]), data)
-        result = jnp.where(subband_lanes((256, 256), s), product, result)
-    return jnp.concatenate(
-        [result[:, :128].reshape(32, 8, 128), result[:, 128:].reshape(32, 8, 128)], axis=1
-    ).reshape(512, 128)
+def by_row(frame_a, frame_b, scratch):
+    scratch[...] = jnp.concatenate([frame_a, frame_b], axis=1).reshape(512, 128)
+    return jnp.concatenate([scratch[pl.ds(r, 32, stride=16), :] for r in range(16)], axis=1)
+
+
+def stacked(data, subbands):
+    lanes = jnp.concatenate([subbands[0:1]] * 16, axis=1)
+    return [
+        jnp.concatenate(
+            [jnp.where(lanes == float(s), part, 0.0).astype(BF16) for s in range(7)], axis=0
+        )
+        for part in (data, data - data.astype(BF16).astype(F32))
+    ]
+
+
+def mixed(frame_a, frame_b, weights, subbands, scratch):
+    data = stacked(by_row(frame_a, frame_b, scratch), subbands)
+    high, low = split(weights)
+    double = dot(jnp.concatenate([high, low], axis=0), data[0])
+    result = double[:32] + (double[32:] + dot(high, data[1]))
+    for r in range(16):
+        scratch[pl.ds(r, 32, stride=16), :] = result[:, 128 * r : 128 * r + 128]
+    return scratch[...]
 
 
 def store_frame(frame, a_ref, b_ref, far_ref):
@@ -256,7 +262,7 @@
 
 
 def analysis_kernel(part_ref, x_ref, lat_ref, lon_ref, a_ref, b_ref, far_ref):
-    frame = analysis(grouped(x_ref[...]), both(lat_ref[0]), both(lon_ref))
+    frame = analysis(grouped(x_ref[...]), block_diagonal(lat_ref), both(lon_ref))
     store_frame(frame, a_ref, b_ref, far_ref)
 
 
@@ -270,26 +276,38 @@
     return lax.rem(row, 8) == lax.rem(lane_index(shape), 8)
 
 
-def prepare_kernel(x_ref, coarse_ref, detail_ref, skip_ref, bias_ref, mix_ref, unmix_ref, pre_ref):
+def expanded(weight, product):
     expand = expand_matrix()
     diagonal = same_row((256, 256))
-    for s in range(8):
-        weight = coarse_ref[s] if s < 4 else (detail_ref[s - 4] if s < 7 else skip_ref[...])
-        for k, part in enumerate(split(weight)):
-            forward = dot_nt(dot_nt(expand, part).astype(BF16), expand)
-            backward = dot_nt(dot(expand, part).astype(BF16), expand)
-            mix_ref[s, k] = jnp.where(diagonal, forward, 0.0).astype(BF16)
-            unmix_ref[s, k] = jnp.where(diagonal, backward, 0.0).astype(BF16)
-    product = dot3((mix_ref[7, 0], mix_ref[7, 1]), split(tiled(x_ref[...])))
-    bias = bias_ref[...]
+    return tuple(
+        jnp.where(diagonal, dot_nt(product(expand, part).astype(BF16), expand), 0.0).astype(BF16)
+        for part in split(weight)
+    )
+
+
+def skip_kernel(x_ref, skip_ref, bias_ref, pre_ref):
+    weight = expanded(skip_ref[...], dot_nt)
+    product = dot3(weight, split(tiled(x_ref[...])))
+    bias = jnp.sum(expand_matrix().astype(F32) * bias_ref[...], axis=1, keepdims=True)
     for t in range(8):
         pre_ref[:, 8 * t : 8 * t + 8, :] = (
-            product[:, 128 * t : 128 * t + 128].reshape(32, 8, 128) + bias
-        )
+            product[:, 128 * t : 128 * t + 128] + bias
+        ).reshape(32, 8, 128)
 
 
 def lat_sum_kernel(
-    part_ref, mask_ref, a_ref, b_ref, near_ref, other_ref, far_ref, fa_ref, fb_ref, low_ref, high_ref
+    part_ref,
+    mask_ref,
+    a_ref,
+    b_ref,
+    near_ref,
+    other_ref,
+    far_ref,
+    subband_ref,
+    fa_ref,
+    fb_ref,
+    low_ref,
+    high_ref,
 ):
     shape = (32, 8, 128)
     keep = lax.broadcasted_iota(jnp.int32, shape, 1) < 6
@@ -298,10 +316,8 @@
     frame_b = b_ref[...] * mask[None, 8:] + jnp.where(keep, other_ref[...], 0.0)
     fa_ref[...] = frame_a
     fb_ref[...] = frame_b
-    lane = lane_index((32, 2, 128))
-    four = lane < 0
-    for s in range(4):
-        four = four | subband_lanes((32, 2, 128), s)
+    subband = subband_ref[0:2][None]
+    four = (subband >= 0.0) & (subband < 4.0)
     fb_ref[:, 6:8, :] += jnp.where(four, far_ref[...], 0.0)
     frame_b = fb_ref[...]
     first = lane_index(shape) < 64
@@ -317,7 +333,9 @@
     right_ref,
     pre_ref,
     cot_ref,
-    mix_ref,
+    coarse_ref,
+    detail_ref,
+    subband_ref,
     lat_a_ref,
     lat_s_ref,
     lon_a_ref,
@@ -329,11 +347,16 @@
     a_ref,
     b_ref,
     far_ref,
+    scratch,
 ):
     frame_a, frame_b = whole(fa_ref[...], fb_ref[...], left_ref[...], right_ref[...])
     ca_ref[...] = frame_a
     cb_ref[...] = frame_b
-    kernel = synthesis(mixed(frame_a, frame_b, mix_ref), both(lat_s_ref[0]), both(lon_s_ref))
+    weights = jnp.concatenate(
+        [coarse_ref[s].T for s in range(4)] + [detail_ref[s].T for s in range(3)], axis=1
+    )
+    frame = mixed(frame_a, frame_b, weights, subband_ref[...], scratch)
+    kernel = synthesis(frame, block_diagonal(lat_s_ref), both(lon_s_ref))
     grads = []
     for g in range(8):
         channels = slice(4 * g, 4 * g + 4)
@@ -344,52 +367,72 @@
         grad = cot_ref[channels].astype(F32).reshape(256, 128) * (cumulative + pre * density)
         grad_ref[channels] = grad.reshape(4, 64, 128)
         grads.append(grad)
-    frame = analysis(jnp.concatenate(grads, axis=1), both(lat_a_ref[0]), both(lon_a_ref))
+    frame = analysis(jnp.concatenate(grads, axis=1), block_diagonal(lat_a_ref), both(lon_a_ref))
     store_frame(frame, a_ref, b_ref, far_ref)
 
 
-def weights_kernel(x_ref, g_ref, ca_ref, cb_ref, a_ref, b_ref, sum_ref):
-    diagonal = same_row((256, 256))
-
-    def reduced(product):
-        rows = jnp.where(diagonal, product, 0.0).reshape(32, 8, 256)
-        return split(jnp.sum(rows, axis=1))
-
+def weights_kernel(
+    x_ref, g_ref, ca_ref, cb_ref, a_ref, b_ref, subband_ref, sum_ref, scratch_c, scratch_g
+):
     def placed(parts, offset):
         row = lax.broadcasted_iota(jnp.int32, (256, 128), 0)
         place = (row // 8 + offset == lane_index((256, 128))).astype(BF16)
         return dot(parts[0], place) + dot(parts[1], place)
 
-    coef = jnp.concatenate([ca_ref[...].reshape(256, 128), cb_ref[...].reshape(256, 128)], axis=1)
-    grad = split(
-        jnp.concatenate([a_ref[...].reshape(256, 128), b_ref[...].reshape(256, 128)], axis=1)
-    )
-    sums = [jnp.zeros((32, 128), F32), jnp.zeros((32, 128), F32)]
-    for s in range(7):
-        chosen = split(jnp.where(subband_lanes((256, 256), s), coef, 0.0))
-        product = dot3(chosen, grad, dot_nt)
-        sums[s // 4] = sums[s // 4] + placed(reduced(product), 32 * (s % 4))
+    coef = stacked(by_row(ca_ref[...], cb_ref[...], scratch_c), subband_ref[...])
+    high, low = split(by_row(a_ref[...], b_ref[...], scratch_g))
+    double = dot_nt(jnp.concatenate([high, low], axis=0), coef[0])
+    mix = double[:32] + (double[32:] + dot_nt(high, coef[1]))
+    mix = jnp.concatenate([mix, jnp.zeros((32, 32), F32)], axis=1)
     field = split(tiled(x_ref[...]))
     grad_pre = split(tiled(g_ref[...]))
-    sums[1] = sums[1] + placed(reduced(dot3(field, grad_pre, dot_nt)), 96)
+    product = jnp.where(same_row((256, 256)), dot3(grad_pre, field, dot_nt), 0.0)
+    skip = split(jnp.sum(product.reshape(32, 8, 256), axis=1))
     ones = jnp.ones((8, 1024), BF16)
     bias = split(dot_nt(ones, grad_pre[0]) + dot_nt(ones, grad_pre[1]))
-    sum_ref[0:32] = sums[0]
-    sum_ref[32:64] = sums[1]
+    sum_ref[0:32] = mix[:, :128]
+    sum_ref[32:64] = mix[:, 128:] + placed(skip, 96)
     sum_ref[64:72] = placed(bias, 0)
 
 
-def skip_back_kernel(g_ref, unmix_ref, out_ref):
-    product = dot3((unmix_ref[7, 0], unmix_ref[7, 1]), split(tiled(g_ref[...])))
+def result_kernel(sum_ref, coarse_ref, detail_ref, skip_ref, bias_ref, cells):
+    first = sum_ref[0:32].T
+    second = sum_ref[32:64].T
+    for s in range(4):
+        coarse_ref[s] = first[32 * s : 32 * s + 32] * (1.0 / math.sqrt(cells // 256))
+    for s in range(3):
+        detail_ref[s] = second[32 * s : 32 * s + 32] * (1.0 / math.sqrt(cells // 64))
+    skip_ref[...] = second[96:] * (1.0 / math.sqrt(cells))
+    bias_ref[...] = sum_ref[64:65, :32] * (1.0 / math.sqrt(cells))
+
+
+def skip_back_kernel(g_ref, skip_ref, out_ref):
+    product = dot3(expanded(skip_ref[...], dot), split(tiled(g_ref[...])))
     for t in range(8):
         out_ref[:, 8 * t : 8 * t + 8, :] = product[:, 128 * t : 128 * t + 128].reshape(32, 8, 128)
 
 
 def backward_kernel(
-    part_ref, fa_ref, fb_ref, left_ref, right_ref, skip_ref, unmix_ref, lat_s_ref, lon_s_ref, out_ref
+    part_ref,
+    fa_ref,
+    fb_ref,
+    left_ref,
+    right_ref,
+    skip_ref,
+    coarse_ref,
+    detail_ref,
+    subband_ref,
+    lat_s_ref,
+    lon_s_ref,
+    out_ref,
+    scratch,
 ):
     frame_a, frame_b = whole(fa_ref[...], fb_ref[...], left_ref[...], right_ref[...])
-    field = synthesis(mixed(frame_a, frame_b, unmix_ref), both(lat_s_ref[0]), both(lon_s_ref))
+    weights = jnp.concatenate(
+        [coarse_ref[s] for s in range(4)] + [detail_ref[s] for s in range(3)], axis=1
+    )
+    frame = mixed(frame_a, frame_b, weights, subband_ref[...], scratch)
+    field = synthesis(frame, block_diagonal(lat_s_ref), both(lon_s_ref))
     for g in range(8):
         channels = slice(4 * g, 4 * g + 4)
         out_ref[channels] = skip_ref[channels] + field[:, 128 * g : 128 * g + 128].reshape(
@@ -409,7 +452,10 @@
     return jax.ShapeDtypeStruct(shape, dtype)
 
 
-def call(kernel, outs, args, part=None, by_part=()):
+FRAME = pltpu.VMEM((512, 128), F32)
+
+
+def call(kernel, outs, args, part=None, by_part=(), scratch=()):
     in_specs = [
         part_spec((1,) + arg.shape[1:]) if i in by_part else full_spec(arg.shape)
         for i, arg in enumerate(args)
@@ -423,10 +469,15 @@
             in_specs=in_specs,
             out_specs=out_specs,
             out_shape=list(outs),
+            scratch_shapes=list(scratch),
             compiler_params=params,
         )(*args)
     grid_spec = pltpu.PrefetchScalarGridSpec(
-        num_scalar_prefetch=1, grid=(1,), in_specs=in_specs, out_specs=out_specs
+        num_scalar_prefetch=1,
+        grid=(1,),
+        in_specs=in_specs,
+        out_specs=out_specs,
+        scratch_shapes=list(scratch),
     )
     return pl.pallas_call(
         kernel, grid_spec=grid_spec, out_shape=list(outs), compiler_params=params
@@ -438,72 +489,88 @@
 FIELD = shape_of(32, 64, 128)
 
 
-def exchange(a, b, far, part):
+def exchange(a, b, far, part, subbands, before):
     near = lax.ppermute(a, "lat", [(i, i ^ 1) for i in range(LAT_PARTS)])
     other = lax.ppermute(b, "lat", [(1, 2), (2, 1)])
     far = lax.ppermute(far, "lat", [(i, i ^ 2) for i in range(LAT_PARTS)])
+    (near, other, far), before = lax.optimization_barrier(((near, other, far), before))
     fa, fb, low, high = call(
-        lat_sum_kernel, (TILE,) * 4, (jnp.asarray(OWN), a, b, near, other, far), part, (0,)
+        lat_sum_kernel,
+        (TILE,) * 4,
+        (jnp.asarray(OWN), a, b, near, other, far, subbands),
+        part,
+        (0,),
     )
     count = lax.axis_size("lon")
     from_left = lax.ppermute(high, "lon", [(i, (i + 1) % count) for i in range(count)])
     from_right = lax.ppermute(low, "lon", [((i + 1) % count, i) for i in range(count)])
-    return fa, fb, from_left, from_right
+    return (fa, fb, from_left, from_right), before
+
+
+def swapped(values, axis, distance):
+    count = lax.axis_size(axis)
+    return lax.ppermute(values, axis, [(i, i ^ distance) for i in range(count)])
 
 
 def total(values):
-    for step in (1, 2):
-        values = values + lax.ppermute(
-            values, "lat", [(i, i ^ step) for i in range(lax.axis_size("lat"))]
-        )
-    for step in (1, 2, 4, 8, 16, 32):
-        values = values + lax.ppermute(
-            values, "lon", [(i, i ^ step) for i in range(lax.axis_size("lon"))]
-        )
-    return values
+    values = values + swapped(values, "lat", 1)
+    for distance in (4, 16):
+        steps = [swapped(values, "lon", distance * k) for k in (1, 3, 2)]
+        values = values + steps[0] + (steps[1] + steps[2])
+    values = values + swapped(values, "lon", 1)
+    count = lax.axis_size("lon")
+    pairs = [
+        (4 * lon + lat, 4 * (lon ^ 2) + (lat ^ 2)) for lon in range(count) for lat in range(4)
+    ]
+    steps = (
+        swapped(values, "lon", 2),
+        lax.ppermute(values, ("lon", "lat"), pairs),
+        swapped(values, "lat", 2),
+    )
+    return values + steps[0] + (steps[1] + steps[2])
 
 
 def on_device(ocean_field, cotangent, mix_coarse, mix_detail, skip_weight, bias_vector):
     part = lax.axis_index("lat").astype(jnp.int32).reshape(1)
     lat_a, lat_s = jnp.asarray(LAT_A), jnp.asarray(LAT_S)
     lon_a, lon_s = jnp.asarray(LON_A), jnp.asarray(LON_S)
+    subbands = jnp.asarray(SUBBANDS)
     a, b, far = call(
         analysis_kernel, (TILE, TILE, FAR), (ocean_field, lat_a, lon_a), part, (1,)
     )
-    weights = shape_of(8, 2, 256, 256, dtype=BF16)
-    bias = jnp.broadcast_to(bias_vector[:, None, None], (CHANNELS, 1, 128))
-    mix, unmix, pre = call(
-        prepare_kernel,
-        (weights, weights, FIELD),
-        (ocean_field, mix_coarse, mix_detail, skip_weight, bias),
-    )
-    fa, fb, from_left, from_right = exchange(a, b, far, part)
+    (pre,) = call(skip_kernel, (FIELD,), (ocean_field, skip_weight, bias_vector.reshape(1, 32)))
+    shares, pre = exchange(a, b, far, part, subbands, pre)
     activated, grad_pre, coef_a, coef_b, a, b, far = call(
         forward_kernel,
         (shape_of(32, 64, 128, dtype=BF16), FIELD, TILE, TILE, TILE, TILE, FAR),
-        (fa, fb, from_left, from_right, pre, cotangent, mix, lat_a, lat_s, lon_a, lon_s),
+        (*shares, pre, cotangent, mix_coarse, mix_detail, subbands, lat_a, lat_s, lon_a, lon_s),
         part,
-        (7, 8),
+        (9, 10),
+        (FRAME,),
     )
     (sums,) = call(
-        weights_kernel, (shape_of(72, 128),), (ocean_field, grad_pre, coef_a, coef_b, a, b)
-    )
-    (skip_back,) = call(skip_back_kernel, (FIELD,), (grad_pre, unmix))
-    fa, fb, from_left, from_right = exchange(a, b, far, part)
+        weights_kernel,
+        (shape_of(72, 128),),
+        (ocean_field, grad_pre, coef_a, coef_b, a, b, subbands),
+        scratch=(FRAME, FRAME),
+    )
+    (skip_back,) = call(skip_back_kernel, (FIELD,), (grad_pre, skip_weight))
+    shares, skip_back = exchange(a, b, far, part, subbands, skip_back)
     (grad_field,) = call(
         backward_kernel,
         (FIELD,),
-        (fa, fb, from_left, from_right, skip_back, unmix, lat_s, lon_s),
+        (*shares, skip_back, mix_coarse, mix_detail, subbands, lat_s, lon_s),
         part,
-        (6,),
-    )
-    sums = total(sums)
+        (8,),
+        (FRAME,),
+    )
     cells = LAT_PARTS * LAT_BLOCK * LON_BLOCK * lax.axis_size("lon")
-    coarse = sums[0:32].reshape(32, 4, 32).transpose(1, 0, 2) / math.sqrt(cells // 256)
-    detail = sums[32:64, :96].reshape(32, 3, 32).transpose(1, 0, 2) / math.sqrt(cells // 64)
-    grad_skip = sums[32:64, 96:] / math.sqrt(cells)
-    grad_bias = sums[64, :32] / math.sqrt(cells)
-    return (activated, grad_field, coarse, detail, grad_skip, grad_bias)
+    coarse, detail, grad_skip, grad_bias = call(
+        functools.partial(result_kernel, cells=cells),
+        (shape_of(4, 32, 32), shape_of(3, 32, 32), shape_of(32, 32), shape_of(1, 32)),
+        (total(sums),),
+    )
+    return (activated, grad_field, coarse, detail, grad_skip, grad_bias.reshape(32))
 
 
 def solution(mesh):

time: 99.1 us -> 81.2 us (0.82)
  the two profiles are of different devices: /device:TPU:16 before, /device:TPU:1 now
where the time goes in v2:
time: 81.2 us; the launch traced here: 81 us
  starting transfers between devices  48 us (59%)
  waiting for transfers between devices  16.8 us (21%)
  Pallas kernels  11.5 us (14%)
  local copies, waits for them, and re-layouts  3.69 us (5%)
  between operations  0.91 us (1%)
    ppermute x2, starting transfers between devices, exchange(): lax.ppermute(low, 'lon', [((i + 1) % count, i) for i in range(count)])  14.3 us
    ppermute x2, starting transfers between devices, exchange(): other = lax.ppermute(b, 'lat', [(1, 2), (2, 1)])  13.2 us
    ppermute x10, starting transfers between devices, swapped(): return lax.ppermute(values, axis, [(i, i ^ distance) for i in range(count)])  10.6 us
    pallas_call x5, Pallas kernels, call(): pl.pallas_call(kernel, grid_spec=grid_spec, out_shape=list(outs), compile...  7.55 us
    ppermute x2, starting transfers between devices, exchange(): near = lax.ppermute(a, 'lat', [(i, i ^ 1) for i in range(LAT_PARTS)])  5.66 us
    ppermute x10, waiting for transfers between devices, swapped(): return lax.ppermute(values, axis, [(i, i ^ distance) for i in range(count)])  5.66 us
    ppermute x2, waiting for transfers between devices, exchange(): far = lax.ppermute(far, 'lat', [(i, i ^ 2) for i in range(LAT_PARTS)])  5.63 us
    ppermute x2, waiting for transfers between devices, exchange(): lax.ppermute(high, 'lon', [(i, (i + 1) % count) for i in range(count)])  5.53 us
  transfers between devices with their start and end apart: 21, of which 7 were waited for; matrix products, arithmetic and copies ran while one was open for 0% of the time, Pallas kernels for 3%

profile of v2, /device:TPU:1, one launch (start us, length us, event | category | flops | bytes accessed | tf_op | source)
XLA Modules:
  0.0 81.0 jit_solution(8094379379402274152)
XLA Ops:
  0.6 0.0 copy-start
  0.6 1.2 %copy-done = f32[32,64,128]{2,1,0:T(8,128)S(1)} copy-done((f32[32,64,128]{2,1,0:T(8,128)S(1)}, f32[32,64,128]{2,1,0:T(8,128)}, u32[]{:S(2)}) %copy-start) | copy-done | bytes 1048600
  1.9 0.9 %copy-done.2 = bf16[2,512,128]{2,1,0:T(8,128)(2,1)S(1)} copy-done((bf16[2,512,128]{2,1,0:T(8,128)(2,1)S(1)}, bf16[2,512,128]{2,1,0:T(8,128)(2,1)}, u32[]{:S(2)}) %copy-start.2) | copy-done | bytes 262168
  2.8 0.9 %copy-done.3 = bf16[4,2,64,256]{3,2,1,0:T(8,128)(2,1)S(1)} copy-done((bf16[4,2,64,256]{3,2,1,0:T(8,128)(2,1)S(1)}, bf16[4,2,64,256]{3,2,1,0:T(8,128)(2,1)}, u32[]{:S(2)}) %copy-start.3) | copy-done | bytes 262168
  3.8 1.1 %shard_map.163 = (f32[32,8,128]{2,1,0:T(8,128)S(1)}, f32[32,8,128]{2,1,0:T(8,128)S(1)}, f32[32,2,128]{2,1,0:T(2,128)S(1)}) custom-call(s32[1]{0:T(128)} %bitcast.part_ref, f32[32,64,128]{2,1,0:T(8,128)S(1)} %copy-done, bf16[4,2,64,256]{3,2,1,0:T(8,128)(2,1)S(1)} %copy-done.3, bf16[2,512,128]{2,1,0:T(8,128)(2,1)S(1)} %copy-done.2), custom_call_target="tpu_custom_call" | custom-call | tf_op jit(solution)/shard_map/pallas_call | solution.py:482
  4.8 3.3 %collective-permute-start = (f32[32,8,128]{2,1,0:T(8,128)S(1)}, f32[32,8,128]{2,1,0:T(8,128)S(1)}, u32[]{:S(2)}, u32[]{:S(2)}) collective-permute-start(f32[32,8,128]{2,1,0:T(8,128)S(1)} %get-tuple-element.36.a_ref), channel_id=1, source_target_pairs={{0,1},{1,0},{2,3},{3,2},{4,5},{5,4},{6,7},{7,6},{8,9},{9,8},{10,11... | collective-permute-start | bytes 393224 | tf_op jit(solution)/shard_map/ppermute | solution.py:493
  8.2 7.0 %collective-permute-start.1 = (f32[32,8,128]{2,1,0:T(8,128)S(1)}, f32[32,8,128]{2,1,0:T(8,128)S(1)}, u32[]{:S(2)}, u32[]{:S(2)}) collective-permute-start(f32[32,8,128]{2,1,0:T(8,128)S(1)} %get-tuple-element.37.b_ref), channel_id=1, source_target_pairs={{1,2},{2,1},{5,6},{6,5},{9,10},{10,9},{13,14},{14,13},{17,18},{18,... | collective-permute-start | bytes 393224 | tf_op jit(solution)/shard_map/ppermute | solution.py:494
  15.2 0.0 copy-start.13
  15.2 0.1 collective-permute-start.2
  15.3 0.0 copy-done.1
  15.3 0.0 copy-done.12
  15.3 0.5 copy-done.13
  15.8 0.0 copy-start.9
  15.8 0.8 %shard_map.164.pre_ref = f32[32,64,128]{2,1,0:T(8,128)S(1)} custom-call(f32[32,64,128]{2,1,0:T(8,128)S(1)} %copy-done.1, f32[32,32]{1,0:T(8,128)S(1)} %copy-done.12, f32[1,32]{1,0:T(1,128)S(1)} %bitcast.3), custom_call_target="tpu_custom_call" | custom-call | tf_op jit(solution)/shard_map/pallas_call | solution.py:466
  16.7 0.0 copy-start.4
  16.7 0.0 copy-start.5
  16.7 0.0 copy-start.8
  16.7 5.6 %collective-permute-done.2.far_ref = f32[32,2,128]{2,1,0:T(2,128)S(1)} collective-permute-done((f32[32,2,128]{2,1,0:T(2,128)S(1)}, f32[32,2,128]{2,1,0:T(2,128)S(1)}, u32[]{:S(2)}, u32[]{:S(2)}) %collective-permute-start.2) | collective-permute-done | bytes 32800 | tf_op jit(solution)/shard_map/ppermute | solution.py:495
  22.3 0.0 collective-permute-done.near_ref
  22.3 0.0 collective-permute-done.1.other_ref
  22.3 0.0 copy-done.10
  22.4 0.2 shard_map.165
  22.5 0.4 collective-permute-start.3
  22.9 7.2 %collective-permute-start.4 = (f32[32,8,128]{2,1,0:T(8,128)S(1)}, f32[32,8,128]{2,1,0:T(8,128)S(1)}, u32[]{:S(2)}, u32[]{:S(2)}) collective-permute-start(f32[32,8,128]{2,1,0:T(8,128)S(1)} %get-tuple-element.45), channel_id=1, source_target_pairs={{4,0},{8,4},{12,8},{16,12},{20,16},{24,20},{28,24},{32,28},{36,32}... | collective-permute-start | bytes 393224 | tf_op jit(solution)/shard_map/ppermute | solution.py:506
  30.1 2.9 %collective-permute-done.3.left_ref = f32[32,8,128]{2,1,0:T(8,128)S(1)} collective-permute-done((f32[32,8,128]{2,1,0:T(8,128)S(1)}, f32[32,8,128]{2,1,0:T(8,128)S(1)}, u32[]{:S(2)}, u32[]{:S(2)}) %collective-permute-start.3) | collective-permute-done | bytes 131104 | tf_op jit(solution)/shard_map/ppermute | solution.py:505
  33.0 0.0 collective-permute-done.4.right_ref
  33.1 3.6 %shard_map.166 = (bf16[32,64,128]{2,1,0:T(8,128)(2,1)}, f32[32,64,128]{2,1,0:T(8,128)S(1)}, f32[32,8,128]{2,1,0:T(8,128)S(1)}, f32[32,8,128]{2,1,0:T(8,128)S(1)}...) custom-call(s32[1]{0:T(128)} %bitcast.part_ref, ...), custom_call_target="tpu_custom_call" | custom-call | tf_op jit(solution)/shard_map/pallas_call | solution.py:482
  36.7 1.6 %shard_map.170 = f32[72,128]{1,0:T(8,128)S(1)} custom-call(f32[32,64,128]{2,1,0:T(8,128)S(1)} %copy-done.1, f32[32,64,128]{2,1,0:T(8,128)S(1)} %get-tuple-element.51.g_ref, f32[32,8,128]{2,1,0:T(8,128)S(1)} %get-tuple-element.60.ca_ref, f32[32,8,128]{2,1,0:T(8,128)S(1)} %get-tuple-element.61.cb_ref, f32[32,8,128]{2,1,0:T(8,128)S(1)} %get-tuple-element.48.a_ref, ...), custom_call_target="tpu_custom_call" | custom-call | tf_op jit(solution)/shard_map/pallas_call | solution.py:466
  38.2 0.1 collective-permute-start.10
  38.3 1.2 %collective-permute-done.10 = f32[72,128]{1,0:T(8,128)S(1)} collective-permute-done((f32[72,128]{1,0:T(8,128)S(1)}, f32[72,128]{1,0:T(8,128)S(1)}, u32[]{:S(2)}, u32[]{:S(2)}) %collective-permute-start.10) | collective-permute-done | bytes 36896 | tf_op jit(solution)/shard_map/ppermute | solution.py:512
  39.5 0.0 collective-permute-start.13
  39.5 0.7 collective-permute-start.12
  40.2 2.0 %collective-permute-start.11 = (f32[72,128]{1,0:T(8,128)S(1)}, f32[72,128]{1,0:T(8,128)S(1)}, u32[]{:S(2)}, u32[]{:S(2)}) collective-permute-start(f32[72,128]{1,0:T(8,128)S(1)} %add.33), channel_id=1, source_target_pairs={{0,16},{4,20},{8,24},{12,28},{16,0},{20,4},{24,8},{28,12},{32,48},... | collective-permute-start | bytes 110600 | tf_op jit(solution)/shard_map/ppermute | solution.py:512
  42.2 1.8 %collective-permute-done.13 = f32[72,128]{1,0:T(8,128)S(1)} collective-permute-done((f32[72,128]{1,0:T(8,128)S(1)}, f32[72,128]{1,0:T(8,128)S(1)}, u32[]{:S(2)}, u32[]{:S(2)}) %collective-permute-start.13) | collective-permute-done | bytes 36896 | tf_op jit(solution)/shard_map/ppermute | solution.py:512
  43.9 0.1 collective-permute-done.12
  44.0 0.0 collective-permute-done.11
  44.1 2.5 %collective-permute-start.16 = (f32[72,128]{1,0:T(8,128)S(1)}, f32[72,128]{1,0:T(8,128)S(1)}, u32[]{:S(2)}, u32[]{:S(2)}) collective-permute-start(f32[72,128]{1,0:T(8,128)S(1)} %add_add_fusion.2), channel_id=1, source_target_pairs={{0,128},{4,132},{8,136},{12,140},{16,144},{20,148},{24,152},{28,15... | collective-permute-start | bytes 110600 | tf_op jit(solution)/shard_map/ppermute | solution.py:512
  46.6 0.8 collective-permute-start.15
  47.3 0.0 collective-permute-start.14
  47.3 2.3 %collective-permute-start.5 = (f32[32,8,128]{2,1,0:T(8,128)S(1)}, f32[32,8,128]{2,1,0:T(8,128)S(1)}, u32[]{:S(2)}, u32[]{:S(2)}) collective-permute-start(f32[32,8,128]{2,1,0:T(8,128)S(1)} %get-tuple-element.48.a_ref), channel_id=1, source_target_pairs={{0,1},{1,0},{2,3},{3,2},{4,5},{5,4},{6,7},{7,6},{8,9},{9,8},{10,11... | collective-permute-start | bytes 393224 | tf_op jit(solution)/shard_map/ppermute | solution.py:493
  49.7 6.2 %collective-permute-start.6 = (f32[32,8,128]{2,1,0:T(8,128)S(1)}, f32[32,8,128]{2,1,0:T(8,128)S(1)}, u32[]{:S(2)}, u32[]{:S(2)}) collective-permute-start(f32[32,8,128]{2,1,0:T(8,128)S(1)} %get-tuple-element.49.b_ref), channel_id=1, source_target_pairs={{1,2},{2,1},{5,6},{6,5},{9,10},{10,9},{13,14},{14,13},{17,18},{18,... | collective-permute-start | bytes 393224 | tf_op jit(solution)/shard_map/ppermute | solution.py:494
  55.9 0.0 collective-permute-done.16
  55.9 0.0 collective-permute-done.15
  55.9 0.0 collective-permute-done.14
  56.0 0.9 %collective-permute-start.17 = (f32[72,128]{1,0:T(8,128)S(1)}, f32[72,128]{1,0:T(8,128)S(1)}, u32[]{:S(2)}, u32[]{:S(2)}) collective-permute-start(f32[72,128]{1,0:T(8,128)S(1)} %add_add_fusion.1), channel_id=1, source_target_pairs={{0,4},{4,0},{8,12},{12,8},{16,20},{20,16},{24,28},{28,24},{32,36},... | collective-permute-start | bytes 110600 | tf_op jit(solution)/shard_map/ppermute | solution.py:512
  56.9 0.0 collective-permute-start.7
  56.9 2.6 %collective-permute-done.17 = f32[72,128]{1,0:T(8,128)S(1)} collective-permute-done((f32[72,128]{1,0:T(8,128)S(1)}, f32[72,128]{1,0:T(8,128)S(1)}, u32[]{:S(2)}, u32[]{:S(2)}) %collective-permute-start.17) | collective-permute-done | bytes 36896 | tf_op jit(solution)/shard_map/ppermute | solution.py:512
  59.5 2.9 %collective-permute-start.20 = (f32[72,128]{1,0:T(8,128)S(1)}, f32[72,128]{1,0:T(8,128)S(1)}, u32[]{:S(2)}, u32[]{:S(2)}) collective-permute-start(f32[72,128]{1,0:T(8,128)S(1)} %add.40), channel_id=1, source_target_pairs={{0,2},{1,3},{2,0},{3,1},{4,6},{5,7},{6,4},{7,5},{8,10},{9,11},{10,... | collective-permute-start | bytes 110600 | tf_op jit(solution)/shard_map/ppermute | solution.py:512
  62.3 3.3 %collective-permute-start.19 = (f32[72,128]{1,0:T(8,128)S(1)}, f32[72,128]{1,0:T(8,128)S(1)}, u32[]{:S(2)}, u32[]{:S(2)}) collective-permute-start(f32[72,128]{1,0:T(8,128)S(1)} %add.40), channel_id=1, source_target_pairs={{0,10},{1,11},{2,8},{3,9},{4,14},{5,15},{6,12},{7,13},{8,2},{9,3},... | collective-permute-start | bytes 110600 | tf_op jit(solution)/shard_map/ppermute | solution.py:527
  65.7 0.0 collective-permute-done.7.far_ref
  65.7 0.7 collective-permute-start.18
  66.4 0.8 %shard_map.167.skip_ref = f32[32,64,128]{2,1,0:T(8,128)S(1)} custom-call(f32[32,64,128]{2,1,0:T(8,128)S(1)} %get-tuple-element.51.g_ref, f32[32,32]{1,0:T(8,128)S(1)} %copy-done.12), custom_call_target="tpu_custom_call" | custom-call | tf_op jit(solution)/shard_map/pallas_call | solution.py:466
  67.3 0.0 collective-permute-done.5.near_ref
  67.3 0.0 collective-permute-done.6.other_ref
  67.3 0.2 shard_map.168
  67.5 0.4 collective-permute-start.8
  67.8 7.2 %collective-permute-start.9 = (f32[32,8,128]{2,1,0:T(8,128)S(1)}, f32[32,8,128]{2,1,0:T(8,128)S(1)}, u32[]{:S(2)}, u32[]{:S(2)}) collective-permute-start(f32[32,8,128]{2,1,0:T(8,128)S(1)} %get-tuple-element.58), channel_id=1, source_target_pairs={{4,0},{8,4},{12,8},{16,12},{20,16},{24,20},{28,24},{32,28},{36,32}... | collective-permute-start | bytes 393224 | tf_op jit(solution)/shard_map/ppermute | solution.py:506
  75.0 0.0 collective-permute-done.20
  75.0 0.0 collective-permute-done.19
  75.0 0.0 collective-permute-done.18
  75.1 0.7 shard_map.171
  75.8 2.6 %collective-permute-done.8.left_ref = f32[32,8,128]{2,1,0:T(8,128)S(1)} collective-permute-done((f32[32,8,128]{2,1,0:T(8,128)S(1)}, f32[32,8,128]{2,1,0:T(8,128)S(1)}, u32[]{:S(2)}, u32[]{:S(2)}) %collective-permute-start.8) | collective-permute-done | bytes 131104 | tf_op jit(solution)/shard_map/ppermute | solution.py:505
  78.4 0.0 collective-permute-done.9.right_ref
  78.4 2.6 %shard_map.169 = f32[32,64,128]{2,1,0:T(8,128)} custom-call(s32[1]{0:T(128)} %bitcast.part_ref, f32[32,8,128]{2,1,0:T(8,128)S(1)} %get-tuple-element.55.fa_ref, f32[32,8,128]{2,1,0:T(8,128)S(1)} %get-tuple-element.56.fb_ref, f32[32,8,128]{2,1,0:T(8,128)S(1)} %collective-permute-done.8.left_ref, f32[32,8,128]{2,1,0:T(8,128)S(1)} %collective-permute-done.9.right_ref, ...), custom_call_target="tpu_custom_call" | custom-call | tf_op jit(solution)/shard_map/pallas_call | solution.py:482
  (20 shorter events, 0.1 us)
Async XLA Ops:
  0.6 1.2 %copy-start = (f32[32,64,128]{2,1,0:T(8,128)S(1)}, f32[32,64,128]{2,1,0:T(8,128)}, u32[]{:S(2)}) copy-start(f32[32,64,128]{2,1,0:T(8,128)} %x_ref.5) | copy-start | bytes 3145732
  1.9 0.9 %copy-start.2 = (bf16[2,512,128]{2,1,0:T(8,128)(2,1)S(1)}, bf16[2,512,128]{2,1,0:T(8,128)(2,1)}, u32[]{:S(2)}) copy-start(bf16[2,512,128]{2,1,0:T(8,128)(2,1)} %constant.18.clone.lon_ref.lon_a_ref) | copy-start | bytes 786436
  2.8 0.9 %copy-start.3 = (bf16[4,2,64,256]{3,2,1,0:T(8,128)(2,1)S(1)}, bf16[4,2,64,256]{3,2,1,0:T(8,128)(2,1)}, u32[]{:S(2)}) copy-start(bf16[4,2,64,256]{3,2,1,0:T(8,128)(2,1)} %constant.16.clone.lat_ref.lat_a_ref) | copy-start | bytes 786436
  3.8 11.5 %copy-start.1 = (f32[32,64,128]{2,1,0:T(8,128)S(1)}, f32[32,64,128]{2,1,0:T(8,128)}, u32[]{:S(2)}) copy-start(f32[32,64,128]{2,1,0:T(8,128)} %x_ref.5) | copy-start | bytes 3145732
  3.8 11.5 %copy-start.12 = (f32[32,32]{1,0:T(8,128)S(1)}, f32[32,32]{1,0:T(8,128)}, u32[]{:S(2)}) copy-start(f32[32,32]{1,0:T(8,128)} %skip_ref.3) | copy-start | bytes 12292
  4.8 17.5 %collective-permute-start = (f32[32,8,128]{2,1,0:T(8,128)S(1)}, f32[32,8,128]{2,1,0:T(8,128)S(1)}, u32[]{:S(2)}, u32[]{:S(2)}) collective-permute-start(f32[32,8,128]{2,1,0:T(8,128)S(1)} %get-tuple-element.36.a_ref), channel_id=1, source_target_pairs={{0,1},{1,0},{2,3},{3,2},{4,5},{5,4},{6,7},{7,6},{8,9},{9,8},{10,11... | collective-permute-start | bytes 393224 | tf_op jit(solution)/shard_map/ppermute | solution.py:493
  8.2 14.2 %collective-permute-start.1 = (f32[32,8,128]{2,1,0:T(8,128)S(1)}, f32[32,8,128]{2,1,0:T(8,128)S(1)}, u32[]{:S(2)}, u32[]{:S(2)}) collective-permute-start(f32[32,8,128]{2,1,0:T(8,128)S(1)} %get-tuple-element.37.b_ref), channel_id=1, source_target_pairs={{1,2},{2,1},{5,6},{6,5},{9,10},{10,9},{13,14},{14,13},{17,18},{18,... | collective-permute-start | bytes 393224 | tf_op jit(solution)/shard_map/ppermute | solution.py:494
  15.2 0.7 copy-start.13
  15.2 7.2 %collective-permute-start.2 = (f32[32,2,128]{2,1,0:T(2,128)S(1)}, f32[32,2,128]{2,1,0:T(2,128)S(1)}, u32[]{:S(2)}, u32[]{:S(2)}) collective-permute-start(f32[32,2,128]{2,1,0:T(2,128)S(1)} %get-tuple-element.38), channel_id=1, source_target_pairs={{0,2},{1,3},{2,0},{3,1},{4,6},{5,7},{6,4},{7,5},{8,10},{9,11},{10,... | collective-permute-start | bytes 98312 | tf_op jit(solution)/shard_map/ppermute | solution.py:495
  15.8 6.5 %copy-start.10 = (f32[4,16,128]{2,1,0:T(8,128)S(1)}, f32[4,16,128]{2,1,0:T(8,128)}, u32[]{:S(2)}) copy-start(f32[4,16,128]{2,1,0:T(8,128)} %constant.21.clone.mask_ref) | copy-start | bytes 98308
  15.8 6.5 %copy-start.11 = (f32[8,128]{1,0:T(8,128)S(1)}, f32[8,128]{1,0:T(8,128)}, u32[]{:S(2)}) copy-start(f32[8,128]{1,0:T(8,128)} %constant.20.clone.subband_ref) | copy-start | bytes 12292
  15.8 17.2 %copy-start.6 = (bf16[4,2,64,256]{3,2,1,0:T(8,128)(2,1)S(1)}, bf16[4,2,64,256]{3,2,1,0:T(8,128)(2,1)}, u32[]{:S(2)}) copy-start(bf16[4,2,64,256]{3,2,1,0:T(8,128)(2,1)} %constant.17.clone.lat_s_ref) | copy-start | bytes 786436
  15.8 17.2 %copy-start.7 = (bf16[32,64,128]{2,1,0:T(8,128)(2,1)S(1)}, bf16[32,64,128]{2,1,0:T(8,128)(2,1)}, u32[]{:S(2)}) copy-start(bf16[32,64,128]{2,1,0:T(8,128)(2,1)} %cot_ref.1) | copy-start | bytes 1572868
  15.8 17.2 %copy-start.9 = (f32[3,32,32]{2,1,0:T(8,128)S(1)}, f32[3,32,32]{2,1,0:T(8,128)}, u32[]{:S(2)}) copy-start(f32[3,32,32]{2,1,0:T(8,128)} %detail_ref.3) | copy-start | bytes 36868
  16.7 16.4 %copy-start.4 = (bf16[4,2,64,256]{3,2,1,0:T(8,128)(2,1)S(1)}, bf16[4,2,64,256]{3,2,1,0:T(8,128)(2,1)}, u32[]{:S(2)}) copy-start(bf16[4,2,64,256]{3,2,1,0:T(8,128)(2,1)} %constant.16.clone.lat_ref.lat_a_ref) | copy-start | bytes 786436
  16.7 16.4 %copy-start.5 = (bf16[2,128,512]{2,1,0:T(8,128)(2,1)S(1)}, bf16[2,128,512]{2,1,0:T(8,128)(2,1)}, u32[]{:S(2)}) copy-start(bf16[2,128,512]{2,1,0:T(8,128)(2,1)} %constant.19.clone.lon_s_ref) | copy-start | bytes 786436
  16.7 16.4 %copy-start.8 = (f32[4,32,32]{2,1,0:T(8,128)S(1)}, f32[4,32,32]{2,1,0:T(8,128)}, u32[]{:S(2)}) copy-start(f32[4,32,32]{2,1,0:T(8,128)} %coarse_ref.3) | copy-start | bytes 49156
  22.5 10.5 %collective-permute-start.3 = (f32[32,8,128]{2,1,0:T(8,128)S(1)}, f32[32,8,128]{2,1,0:T(8,128)S(1)}, u32[]{:S(2)}, u32[]{:S(2)}) collective-permute-start(f32[32,8,128]{2,1,0:T(8,128)S(1)} %get-tuple-element.44), channel_id=1, source_target_pairs={{0,4},{4,8},{8,12},{12,16},{16,20},{20,24},{24,28},{28,32},{32,36}... | collective-permute-start | bytes 393224 | tf_op jit(solution)/shard_map/ppermute | solution.py:505
  22.9 10.1 %collective-permute-start.4 = (f32[32,8,128]{2,1,0:T(8,128)S(1)}, f32[32,8,128]{2,1,0:T(8,128)S(1)}, u32[]{:S(2)}, u32[]{:S(2)}) collective-permute-start(f32[32,8,128]{2,1,0:T(8,128)S(1)} %get-tuple-element.45), channel_id=1, source_target_pairs={{4,0},{8,4},{12,8},{16,12},{20,16},{24,20},{28,24},{32,28},{36,32}... | collective-permute-start | bytes 393224 | tf_op jit(solution)/shard_map/ppermute | solution.py:506
  38.2 1.3 %collective-permute-start.10 = (f32[72,128]{1,0:T(8,128)S(1)}, f32[72,128]{1,0:T(8,128)S(1)}, u32[]{:S(2)}, u32[]{:S(2)}) collective-permute-start(f32[72,128]{1,0:T(8,128)S(1)} %shard_map.170), channel_id=1, source_target_pairs={{0,1},{1,0},{2,3},{3,2},{4,5},{5,4},{6,7},{7,6},{8,9},{9,8},{10,11... | collective-permute-start | bytes 110600 | tf_op jit(solution)/shard_map/ppermute | solution.py:512
  39.5 4.4 %collective-permute-start.13 = (f32[72,128]{1,0:T(8,128)S(1)}, f32[72,128]{1,0:T(8,128)S(1)}, u32[]{:S(2)}, u32[]{:S(2)}) collective-permute-start(f32[72,128]{1,0:T(8,128)S(1)} %add.33), channel_id=1, source_target_pairs={{0,32},{4,36},{8,40},{12,44},{16,48},{20,52},{24,56},{28,60},{32,0... | collective-permute-start | bytes 110600 | tf_op jit(solution)/shard_map/ppermute | solution.py:512
  39.5 4.5 %collective-permute-start.12 = (f32[72,128]{1,0:T(8,128)S(1)}, f32[72,128]{1,0:T(8,128)S(1)}, u32[]{:S(2)}, u32[]{:S(2)}) collective-permute-start(f32[72,128]{1,0:T(8,128)S(1)} %add.33), channel_id=1, source_target_pairs={{0,48},{4,52},{8,56},{12,60},{16,32},{20,36},{24,40},{28,44},{32,1... | collective-permute-start | bytes 110600 | tf_op jit(solution)/shard_map/ppermute | solution.py:512
  40.2 3.9 %collective-permute-start.11 = (f32[72,128]{1,0:T(8,128)S(1)}, f32[72,128]{1,0:T(8,128)S(1)}, u32[]{:S(2)}, u32[]{:S(2)}) collective-permute-start(f32[72,128]{1,0:T(8,128)S(1)} %add.33), channel_id=1, source_target_pairs={{0,16},{4,20},{8,24},{12,28},{16,0},{20,4},{24,8},{28,12},{32,48},... | collective-permute-start | bytes 110600 | tf_op jit(solution)/shard_map/ppermute | solution.py:512
  44.1 11.8 %collective-permute-start.16 = (f32[72,128]{1,0:T(8,128)S(1)}, f32[72,128]{1,0:T(8,128)S(1)}, u32[]{:S(2)}, u32[]{:S(2)}) collective-permute-start(f32[72,128]{1,0:T(8,128)S(1)} %add_add_fusion.2), channel_id=1, source_target_pairs={{0,128},{4,132},{8,136},{12,140},{16,144},{20,148},{24,152},{28,15... | collective-permute-start | bytes 110600 | tf_op jit(solution)/shard_map/ppermute | solution.py:512
  46.6 9.4 %collective-permute-start.15 = (f32[72,128]{1,0:T(8,128)S(1)}, f32[72,128]{1,0:T(8,128)S(1)}, u32[]{:S(2)}, u32[]{:S(2)}) collective-permute-start(f32[72,128]{1,0:T(8,128)S(1)} %add_add_fusion.2), channel_id=1, source_target_pairs={{0,192},{4,196},{8,200},{12,204},{16,208},{20,212},{24,216},{28,22... | collective-permute-start | bytes 110600 | tf_op jit(solution)/shard_map/ppermute | solution.py:512
  47.3 8.6 %collective-permute-start.14 = (f32[72,128]{1,0:T(8,128)S(1)}, f32[72,128]{1,0:T(8,128)S(1)}, u32[]{:S(2)}, u32[]{:S(2)}) collective-permute-start(f32[72,128]{1,0:T(8,128)S(1)} %add_add_fusion.2), channel_id=1, source_target_pairs={{0,64},{4,68},{8,72},{12,76},{16,80},{20,84},{24,88},{28,92},{32,9... | collective-permute-start | bytes 110600 | tf_op jit(solution)/shard_map/ppermute | solution.py:512
  47.3 19.9 %collective-permute-start.5 = (f32[32,8,128]{2,1,0:T(8,128)S(1)}, f32[32,8,128]{2,1,0:T(8,128)S(1)}, u32[]{:S(2)}, u32[]{:S(2)}) collective-permute-start(f32[32,8,128]{2,1,0:T(8,128)S(1)} %get-tuple-element.48.a_ref), channel_id=1, source_target_pairs={{0,1},{1,0},{2,3},{3,2},{4,5},{5,4},{6,7},{7,6},{8,9},{9,8},{10,11... | collective-permute-start | bytes 393224 | tf_op jit(solution)/shard_map/ppermute | solution.py:493
  49.7 17.6 %collective-permute-start.6 = (f32[32,8,128]{2,1,0:T(8,128)S(1)}, f32[32,8,128]{2,1,0:T(8,128)S(1)}, u32[]{:S(2)}, u32[]{:S(2)}) collective-permute-start(f32[32,8,128]{2,1,0:T(8,128)S(1)} %get-tuple-element.49.b_ref), channel_id=1, source_target_pairs={{1,2},{2,1},{5,6},{6,5},{9,10},{10,9},{13,14},{14,13},{17,18},{18,... | collective-permute-start | bytes 393224 | tf_op jit(solution)/shard_map/ppermute | solution.py:494
  56.0 3.5 %collective-permute-start.17 = (f32[72,128]{1,0:T(8,128)S(1)}, f32[72,128]{1,0:T(8,128)S(1)}, u32[]{:S(2)}, u32[]{:S(2)}) collective-permute-start(f32[72,128]{1,0:T(8,128)S(1)} %add_add_fusion.1), channel_id=1, source_target_pairs={{0,4},{4,0},{8,12},{12,8},{16,20},{20,16},{24,28},{28,24},{32,36},... | collective-permute-start | bytes 110600 | tf_op jit(solution)/shard_map/ppermute | solution.py:512
  56.9 8.8 %collective-permute-start.7 = (f32[32,2,128]{2,1,0:T(2,128)S(1)}, f32[32,2,128]{2,1,0:T(2,128)S(1)}, u32[]{:S(2)}, u32[]{:S(2)}) collective-permute-start(f32[32,2,128]{2,1,0:T(2,128)S(1)} %get-tuple-element.50), channel_id=1, source_target_pairs={{0,2},{1,3},{2,0},{3,1},{4,6},{5,7},{6,4},{7,5},{8,10},{9,11},{10,... | collective-permute-start | bytes 98312 | tf_op jit(solution)/shard_map/ppermute | solution.py:495
  59.5 15.6 %collective-permute-start.20 = (f32[72,128]{1,0:T(8,128)S(1)}, f32[72,128]{1,0:T(8,128)S(1)}, u32[]{:S(2)}, u32[]{:S(2)}) collective-permute-start(f32[72,128]{1,0:T(8,128)S(1)} %add.40), channel_id=1, source_target_pairs={{0,2},{1,3},{2,0},{3,1},{4,6},{5,7},{6,4},{7,5},{8,10},{9,11},{10,... | collective-permute-start | bytes 110600 | tf_op jit(solution)/shard_map/ppermute | solution.py:512
  62.3 12.7 %collective-permute-start.19 = (f32[72,128]{1,0:T(8,128)S(1)}, f32[72,128]{1,0:T(8,128)S(1)}, u32[]{:S(2)}, u32[]{:S(2)}) collective-permute-start(f32[72,128]{1,0:T(8,128)S(1)} %add.40), channel_id=1, source_target_pairs={{0,10},{1,11},{2,8},{3,9},{4,14},{5,15},{6,12},{7,13},{8,2},{9,3},... | collective-permute-start | bytes 110600 | tf_op jit(solution)/shard_map/ppermute | solution.py:527
  65.7 9.3 %collective-permute-start.18 = (f32[72,128]{1,0:T(8,128)S(1)}, f32[72,128]{1,0:T(8,128)S(1)}, u32[]{:S(2)}, u32[]{:S(2)}) collective-permute-start(f32[72,128]{1,0:T(8,128)S(1)} %add.40), channel_id=1, source_target_pairs={{0,8},{4,12},{8,0},{12,4},{16,24},{20,28},{24,16},{28,20},{32,40},... | collective-permute-start | bytes 110600 | tf_op jit(solution)/shard_map/ppermute | solution.py:512
  67.5 11.0 %collective-permute-start.8 = (f32[32,8,128]{2,1,0:T(8,128)S(1)}, f32[32,8,128]{2,1,0:T(8,128)S(1)}, u32[]{:S(2)}, u32[]{:S(2)}) collective-permute-start(f32[32,8,128]{2,1,0:T(8,128)S(1)} %get-tuple-element.57), channel_id=1, source_target_pairs={{0,4},{4,8},{8,12},{12,16},{16,20},{20,24},{24,28},{28,32},{32,36}... | collective-permute-start | bytes 393224 | tf_op jit(solution)/shard_map/ppermute | solution.py:505
  67.8 10.6 %collective-permute-start.9 = (f32[32,8,128]{2,1,0:T(8,128)S(1)}, f32[32,8,128]{2,1,0:T(8,128)S(1)}, u32[]{:S(2)}, u32[]{:S(2)}) collective-permute-start(f32[32,8,128]{2,1,0:T(8,128)S(1)} %get-tuple-element.58), channel_id=1, source_target_pairs={{4,0},{8,4},{12,8},{16,12},{20,16},{24,20},{28,24},{32,28},{36,32}... | collective-permute-start | bytes 393224 | tf_op jit(solution)/shard_map/ppermute | solution.py:506

commit v3 on v2

v3 whole, which is shorter than its diff:
```python
import functools
import math

import jax
import jax.numpy as jnp
import numpy as np
from jax import lax
from jax.experimental import pallas as pl
from jax.experimental.pallas import tpu as pltpu
from jax.sharding import PartitionSpec as P
from ml_dtypes import bfloat16

F32 = jnp.float32
BF16 = jnp.bfloat16

low_taps = (
    -0.010597401785069032,
    0.0328830116668852,
    0.030841381835560764,
    -0.18703481171909309,
    -0.027983769416859854,
    0.6308807679298589,
    0.7148465705529157,
    0.2303778133088965,
)
high_taps = (
    -0.2303778133088965,
    0.7148465705529157,
    -0.6308807679298589,
    -0.027983769416859854,
    0.18703481171909309,
    0.030841381835560764,
    -0.0328830116668852,
    -0.010597401785069032,
)

CHANNELS = 32
LAT_PARTS = 4
LAT_BLOCK = 64
LON_BLOCK = 128
LAT_BAND = (0, 1, 0, 1, 3, 2, 3)
LON_BAND = (0, 0, 1, 1, 2, 3, 3)
LO_LANES = 42
HI_LANE = 64


def level_matrix(size, taps, periodic):
    matrix = np.zeros((size // 2, size))
    for k in range(size // 2):
        for j in range(8):
            m = 2 * k + j - 3
            if periodic:
                matrix[k, m % size] += taps[j]
            elif 0 <= m < size:
                matrix[k, m] += taps[j]
    return matrix


def composed(size, periodic):
    two = level_matrix(size // 2, low_taps, periodic) @ level_matrix(size, low_taps, periodic)
    three_low = level_matrix(size // 4, low_taps, periodic) @ two
    three_high = level_matrix(size // 4, high_taps, periodic) @ two
    four_low = level_matrix(size // 8, low_taps, periodic) @ three_low
    four_high = level_matrix(size // 8, high_taps, periodic) @ three_low
    return (four_low, four_high, three_low, three_high)


def lane_table():
    lanes = [None] * 128
    inner = []
    for s in range(7):
        count = 14 if s < 4 else 22
        for e in range(6):
            lanes[s * 6 + e] = (s, e)
            lanes[HI_LANE + s * 6 + e] = (s, count - 6 + e)
        inner += [(s, e) for e in range(6, count - 6)]
    free = [lane for lane in range(128) if lanes[lane] is None]
    for lane, entry in zip(free, inner):
        lanes[lane] = entry
    return lanes


LANES = lane_table()
SUBBAND_OF_LANE = np.array([-1 if entry is None else entry[0] for entry in LANES])


def lon_weights():
    maps = composed(8 * LON_BLOCK, True)
    start = 3 * LON_BLOCK
    weights = np.zeros((4, LON_BLOCK, 128))
    for lane, entry in enumerate(LANES):
        if entry is None:
            continue
        s, e = entry
        per_block = 8 if s < 4 else 16
        row = maps[LON_BAND[s]][3 * per_block - 3 + e]
        weights[LAT_BAND[s], :, lane] = row[start : start + LON_BLOCK]
    return weights.reshape(4 * LON_BLOCK, 128)


def row_entries(part):
    top4, bottom4 = list(range(6)) + [None] * 2, list(range(4, 10)) + [None] * 2
    top3, bottom3 = list(range(8)), list(range(8, 14)) + [None] * 2
    four = bottom4 + top4 if part % 2 == 0 else top4 + bottom4
    three = bottom3 + top3 if part % 2 == 0 else top3 + bottom3
    four[14:16] = [8, 9] if part < 2 else [0, 1]
    return four, three


def lat_weights():
    maps = composed(LAT_PARTS * LAT_BLOCK, False)
    weights = np.zeros((LAT_PARTS, 4, 16, LAT_BLOCK))
    for part in range(LAT_PARTS):
        entries = row_entries(part)
        for band in range(4):
            per_block = 4 if band < 2 else 8
            for row, e in enumerate(entries[0 if band < 2 else 1]):
                k = per_block * part - 3 + e if e is not None else -1
                if 0 <= k < per_block * LAT_PARTS:
                    weights[part, band, row] = maps[band][
                        k, part * LAT_BLOCK : (part + 1) * LAT_BLOCK
                    ]
    return weights.reshape(LAT_PARTS, 64, LAT_BLOCK)


def own_mask():
    mask = np.ones((LAT_PARTS, 16, 128), np.float32)
    four = (SUBBAND_OF_LANE >= 0) & (SUBBAND_OF_LANE < 4)
    for part in range(LAT_PARTS):
        bottom = 0 if part % 2 == 0 else 8
        for row in (bottom, bottom + 1, 14, 15):
            mask[part, row, four] = 0.0
    return mask


def high_low(matrix):
    matrix = matrix.astype(np.float32)
    high = matrix.astype(bfloat16)
    low = (matrix - high.astype(np.float32)).astype(bfloat16)
    return np.stack([high, low], axis=-3)


LON = lon_weights()
LAT = lat_weights()
LON_ROWS = 1024


def packed(lon, lat):
    lon = high_low(lon)
    lon = np.concatenate(
        [lon[:, :, 128 * b : 128 * b + 128] for b in range(lon.shape[2] // 128)], axis=1
    )
    lat = high_low(np.tile(lat, (1, 1, 2)))
    return np.concatenate([lon.reshape(LON_ROWS, 128), lat.reshape(-1, 128)])


ANALYSIS = packed(LON, LAT)
SYNTHESIS = packed(LON.T, LAT.transpose(0, 2, 1))
OWN = own_mask()
SUBBANDS = np.tile(SUBBAND_OF_LANE.astype(np.float32), (8, 1))


def split(x):
    high = x.astype(BF16)
    low = (x - high.astype(F32)).astype(BF16)
    return high, low


def dot(a, b):
    return jnp.dot(a, b, preferred_element_type=F32)


def dot_nt(a, b):
    return lax.dot_general(a, b, (((1,), (1,)), ((), ())), preferred_element_type=F32)


def dot3(a, b, product=dot):
    return product(a[0], b[0]) + (product(a[0], b[1]) + product(a[1], b[0]))


def lat_matrix(table_ref, part):
    row = lax.broadcasted_iota(jnp.int32, (256, 256), 0)
    keep = row // 64 == lane_index((256, 256)) // 64
    first = pl.multiple_of(LON_ROWS + 128 * part, 128)
    block = table_ref[pl.ds(first, 128), :]
    return tuple(
        jnp.where(keep, jnp.tile(block[64 * k : 64 * k + 64], (4, 2)), 0.0).astype(BF16)
        for k in range(2)
    )


def lon_analysis(table_ref):
    return table_ref[0:512], table_ref[512:1024]


def lon_synthesis(table_ref):
    return tuple(
        jnp.concatenate(
            [table_ref[512 * k + 128 * b : 512 * k + 128 * b + 128] for b in range(4)], axis=1
        )
        for k in range(2)
    )


def lat_part(part_ref):
    return part_ref[0] // 2


def is_even(part_ref):
    return part_ref[0] % 2 == 0


def grouped(x):
    return jnp.concatenate(
        [x[4 * g : 4 * g + 4].reshape(256, 128) for g in range(x.shape[0] // 4)], axis=1
    )


def tiled(x):
    return jnp.concatenate(
        [x[:, 8 * t : 8 * t + 8, :].reshape(256, 128) for t in range(8)], axis=1
    )


def analysis(groups, lat, lon):
    rows = dot3(lat, split(groups))
    count = groups.shape[1] // 128
    blocks = []
    for g in range(count):
        part = rows[:, 128 * g : 128 * g + 128].reshape(4, 4, 16, 128)
        blocks.append(
            jnp.concatenate([part[:, b].reshape(64, 128) for b in range(4)], axis=1)
        )
    return dot3(split(jnp.concatenate(blocks, axis=0)), lon).reshape(4 * count, 16, 128)


def synthesis_rows(frame, lon):
    wide = dot3(split(frame), lon).reshape(8, 4, 16, 512)
    groups = []
    for g in range(8):
        part = jnp.stack(
            [wide[g, :, :, 128 * b : 128 * b + 128] for b in range(4)], axis=1
        )
        groups.append(part.reshape(256, 128))
    return jnp.concatenate(groups, axis=1)


def lane_index(shape):
    return lax.broadcasted_iota(jnp.int32, shape, len(shape) - 1)


def rolled(x, shift):
    return pltpu.roll(x, shift % 128, 2) if shift % 128 else x


def edge_lanes(frame, first):
    lane = lane_index((11, 16, 128))
    parts = [rolled(frame[c : c + 11], LO_LANES * k - first) for k, c in enumerate((0, 11, 21))]
    return jnp.where(
        lane < LO_LANES, parts[0], jnp.where(lane < 2 * LO_LANES, parts[1], parts[2])
    )


def placed_lanes(edge, first):
    parts = [rolled(edge, first - LO_LANES * k) for k in range(3)]
    whole = jnp.concatenate([parts[0], parts[1], parts[2][1:]], axis=0)
    lane = lane_index(whole.shape)
    return jnp.where((lane >= first) & (lane < first + LO_LANES), whole, 0.0)


def add_edges(frame_ref, even, first, second):
    from_left = jnp.where(even, first, second)
    from_right = jnp.where(even, second, first)
    added = placed_lanes(from_left, 0) + placed_lanes(from_right, HI_LANE)
    return frame_ref[...] + added.reshape(512, 128)


def by_row(frame_ref):
    return jnp.concatenate([frame_ref[pl.ds(r, 32, stride=16), :] for r in range(16)], axis=1)


def stacked(data, subbands):
    lanes = jnp.concatenate([subbands[0:1]] * 16, axis=1)
    return [
        jnp.concatenate(
            [jnp.where(lanes == float(s), part, 0.0).astype(BF16) for s in range(7)], axis=0
        )
        for part in (data, data - data.astype(BF16).astype(F32))
    ]


def mixed(frame_ref, weights, subbands, scratch):
    data = stacked(by_row(frame_ref), subbands)
    high, low = split(weights)
    double = dot(jnp.concatenate([high, low], axis=0), data[0])
    result = double[:32] + (double[32:] + dot(high, data[1]))
    for r in range(16):
        scratch[pl.ds(r, 32, stride=16), :] = result[:, 128 * r : 128 * r + 128]
    return scratch[...]


def store_frame(frame, frame_ref, near_ref, other_ref, far_ref):
    frame_ref[...] = frame.reshape(512, 128)
    for target, first, rows in ((near_ref, 0, 6), (other_ref, 8, 6), (far_ref, 14, 2)):
        for r in range(rows):
            target[32 * r : 32 * r + 32] = frame_ref[pl.ds(first + r, 32, stride=16), :]


def analysis_kernel(part_ref, x_ref, table_ref, frame_ref, near_ref, other_ref, far_ref):
    lat = lat_matrix(table_ref, lat_part(part_ref))
    frame = analysis(grouped(x_ref[...]), lat, lon_analysis(table_ref))
    store_frame(frame, frame_ref, near_ref, other_ref, far_ref)


def expand_matrix():
    row = lax.broadcasted_iota(jnp.int32, (256, 32), 0)
    return (row // 8 == lane_index((256, 32))).astype(BF16)


def same_row(shape):
    row = lax.broadcasted_iota(jnp.int32, shape, 0)
    return lax.rem(row, 8) == lax.rem(lane_index(shape), 8)


def expanded(weight, product):
    expand = expand_matrix()
    diagonal = same_row((256, 256))
    return tuple(
        jnp.where(diagonal, dot_nt(product(expand, part).astype(BF16), expand), 0.0).astype(BF16)
        for part in split(weight)
    )


def skip_kernel(x_ref, skip_ref, bias_ref, pre_ref):
    weight = expanded(skip_ref[...], dot_nt)
    product = dot3(weight, split(tiled(x_ref[...])))
    bias = jnp.sum(expand_matrix().astype(F32) * bias_ref[...], axis=1, keepdims=True)
    for t in range(8):
        pre_ref[:, 8 * t : 8 * t + 8, :] = (
            product[:, 128 * t : 128 * t + 128] + bias
        ).reshape(32, 8, 128)


def lat_sum_kernel(
    part_ref,
    mask_ref,
    frame_ref,
    near_ref,
    other_ref,
    far_ref,
    subband_ref,
    sum_ref,
    first_ref,
    second_ref,
    *,
    far_row,
):
    frame = frame_ref[...].reshape(32, 16, 128) * mask_ref[0][None]
    sum_ref[...] = frame.reshape(512, 128)
    subband = subband_ref[0:1]
    four = (subband >= 0.0) & (subband < 4.0)
    for r in range(6):
        sum_ref[pl.ds(r, 32, stride=16), :] += near_ref[32 * r : 32 * r + 32]
        sum_ref[pl.ds(8 + r, 32, stride=16), :] += other_ref[32 * r : 32 * r + 32]
    for r in range(2):
        far = far_ref[far_row + 32 * r : far_row + 32 * r + 32]
        sum_ref[pl.ds(14 + r, 32, stride=16), :] += jnp.where(four, far, 0.0)
    frame = sum_ref[...].reshape(32, 16, 128)
    low, high = edge_lanes(frame, 0), edge_lanes(frame, HI_LANE)
    even = is_even(part_ref)
    first_ref[...] = jnp.where(even, low, high)
    second_ref[...] = jnp.where(even, high, low)


def forward_kernel(
    part_ref,
    shares_ref,
    first_ref,
    second_ref,
    pre_ref,
    cot_ref,
    coarse_ref,
    detail_ref,
    subband_ref,
    analysis_ref,
    synthesis_ref,
    act_ref,
    grad_ref,
    coef_ref,
    frame_ref,
    near_ref,
    other_ref,
    far_ref,
    scratch,
    act,
    done,
):
    coef_ref[...] = add_edges(
        shares_ref, is_even(part_ref), first_ref[...], second_ref[...]
    )
    weights = jnp.concatenate(
        [coarse_ref[s].T for s in range(4)] + [detail_ref[s].T for s in range(3)], axis=1
    )
    frame = mixed(coef_ref, weights, subband_ref[...], scratch)
    rows = synthesis_rows(frame, lon_synthesis(synthesis_ref))
    lat = lat_matrix(synthesis_ref, lat_part(part_ref))
    grads = []
    stores = []
    for q in range(4):
        kernel = dot3(lat, split(rows[:, 256 * q : 256 * q + 256]))
        for g in (2 * q, 2 * q + 1):
            channels = slice(4 * g, 4 * g + 4)
            lanes = slice(128 * (g - 2 * q), 128 * (g - 2 * q) + 128)
            pre = kernel[:, lanes] + pre_ref[channels].reshape(256, 128)
            cumulative = 0.5 * (1.0 + lax.erf(pre * math.sqrt(0.5)))
            density = jnp.exp(-0.5 * pre * pre) * (1.0 / math.sqrt(2.0 * math.pi))
            act[channels] = (pre * cumulative).astype(BF16).reshape(4, 64, 128)
            grad = cot_ref[channels].astype(F32).reshape(256, 128) * (cumulative + pre * density)
            grad_ref[channels] = grad.reshape(4, 64, 128)
            grads.append(grad)
        block = pl.ds(8 * q, 8)
        stores.append(pltpu.make_async_copy(act.at[block], act_ref.at[block], done.at[q]))
        stores[q].start()
    frame = analysis(
        jnp.concatenate(grads, axis=1),
        lat_matrix(analysis_ref, lat_part(part_ref)),
        lon_analysis(analysis_ref),
    )
    store_frame(frame, frame_ref, near_ref, other_ref, far_ref)
    for store in stores:
        store.wait()


def weights_kernel(x_ref, g_ref, coef_ref, frame_ref, near_ref, subband_ref, sum_ref):
    def placed(parts, offset):
        row = lax.broadcasted_iota(jnp.int32, (256, 128), 0)
        place = (row // 8 + offset == lane_index((256, 128))).astype(BF16)
        return dot(parts[0], place) + dot(parts[1], place)

    coef = stacked(by_row(coef_ref), subband_ref[...])
    high, low = split(by_row(frame_ref))
    double = dot_nt(jnp.concatenate([high, low], axis=0), coef[0])
    mix = double[:32] + (double[32:] + dot_nt(high, coef[1]))
    mix = jnp.concatenate([mix, jnp.zeros((32, 32), F32)], axis=1)
    field = split(tiled(x_ref[...]))
    grad_pre = split(tiled(g_ref[...]))
    product = jnp.where(same_row((256, 256)), dot3(grad_pre, field, dot_nt), 0.0)
    skip = split(jnp.sum(product.reshape(32, 8, 256), axis=1))
    ones = jnp.ones((8, 1024), BF16)
    bias = split(dot_nt(ones, grad_pre[0]) + dot_nt(ones, grad_pre[1]))
    sum_ref[0:192] = near_ref[...]
    sum_ref[192:224] = mix[:, :128]
    sum_ref[224:256] = mix[:, 128:] + placed(skip, 96)
    sum_ref[256:264] = placed(bias, 0)


def pair_kernel(own_ref, near_ref, far_ref, out_ref):
    out_ref[0:72] = own_ref[192:264] + near_ref[192:264]
    out_ref[72:136] = far_ref[...]


def result_kernel(sum_ref, coarse_ref, detail_ref, skip_ref, bias_ref, cells):
    first = sum_ref[0:32].T
    second = sum_ref[32:64].T
    for s in range(4):
        coarse_ref[s] = first[32 * s : 32 * s + 32] * (1.0 / math.sqrt(cells // 256))
    for s in range(3):
        detail_ref[s] = second[32 * s : 32 * s + 32] * (1.0 / math.sqrt(cells // 64))
    skip_ref[...] = second[96:] * (1.0 / math.sqrt(cells))
    bias_ref[...] = sum_ref[64:65, :32] * (1.0 / math.sqrt(cells))


def skip_back_kernel(g_ref, skip_ref, out_ref):
    product = dot3(expanded(skip_ref[...], dot), split(tiled(g_ref[...])))
    for t in range(8):
        out_ref[:, 8 * t : 8 * t + 8, :] = product[:, 128 * t : 128 * t + 128].reshape(32, 8, 128)


def backward_kernel(
    part_ref,
    shares_ref,
    first_ref,
    second_ref,
    skip_ref,
    coarse_ref,
    detail_ref,
    subband_ref,
    synthesis_ref,
    out_ref,
    whole,
    scratch,
    field,
    done,
):
    whole[...] = add_edges(shares_ref, is_even(part_ref), first_ref[...], second_ref[...])
    weights = jnp.concatenate(
        [coarse_ref[s] for s in range(4)] + [detail_ref[s] for s in range(3)], axis=1
    )
    frame = mixed(whole, weights, subband_ref[...], scratch)
    rows = synthesis_rows(frame, lon_synthesis(synthesis_ref))
    lat = lat_matrix(synthesis_ref, lat_part(part_ref))
    stores = []
    for q in range(4):
        part = dot3(lat, split(rows[:, 256 * q : 256 * q + 256]))
        for g in (2 * q, 2 * q + 1):
            channels = slice(4 * g, 4 * g + 4)
            lanes = slice(128 * (g - 2 * q), 128 * (g - 2 * q) + 128)
            field[channels] = skip_ref[channels] + part[:, lanes].reshape(4, 64, 128)
        block = pl.ds(8 * q, 8)
        stores.append(pltpu.make_async_copy(field.at[block], out_ref.at[block], done.at[q]))
        stores[q].start()
    for store in stores:
        store.wait()


def full_spec(shape):
    return pl.BlockSpec(shape, lambda *_: (0,) * len(shape))


def part_spec(shape):
    return pl.BlockSpec(shape, lambda _, part: (part[0] // 2,) + (0,) * (len(shape) - 1))


def shape_of(*shape, dtype=F32):
    return jax.ShapeDtypeStruct(shape, dtype)


FRAME = pltpu.VMEM((512, 128), F32)


def call(kernel, outs, args, part=None, by_part=(), scratch=(), in_hbm=()):
    in_specs = [
        part_spec((1,) + arg.shape[1:]) if i in by_part else full_spec(arg.shape)
        for i, arg in enumerate(args)
    ]
    out_specs = [
        pl.BlockSpec(memory_space=pltpu.HBM) if i in in_hbm else full_spec(out.shape)
        for i, out in enumerate(outs)
    ]
    params = pltpu.CompilerParams(vmem_limit_bytes=48 * 1024 * 1024)
    if part is None:
        return pl.pallas_call(
            kernel,
            grid=(1,),
            in_specs=in_specs,
            out_specs=out_specs,
            out_shape=list(outs),
            scratch_shapes=list(scratch),
            compiler_params=params,
        )(*args)
    grid_spec = pltpu.PrefetchScalarGridSpec(
        num_scalar_prefetch=1,
        grid=(1,),
        in_specs=in_specs,
        out_specs=out_specs,
        scratch_shapes=list(scratch),
    )
    return pl.pallas_call(
        kernel, grid_spec=grid_spec, out_shape=list(outs), compiler_params=params
    )(part, *args)


COEFS = shape_of(512, 128)
ROWS = shape_of(192, 128)
FAR = shape_of(64, 128)
EDGE = shape_of(11, 16, 128)
FIELD = shape_of(32, 64, 128)


def swapped(values, axis, distance):
    count = lax.axis_size(axis)
    return lax.ppermute(values, axis, [(i, i ^ distance) for i in range(count)])


def ring(values, unit):
    count = lax.axis_size("lon")
    step = (3, 1, -1, -3)
    return lax.ppermute(
        values, "lon", [(i, i + step[i // unit % 4] * unit) for i in range(count)]
    )


def middle(values):
    return lax.ppermute(values, "lat", [(1, 2), (2, 1)])


def lat_sum(frame, near, other, far, far_row, part, subbands):
    return call(
        functools.partial(lat_sum_kernel, far_row=far_row),
        (COEFS, EDGE, EDGE),
        (jnp.asarray(OWN), frame, near, other, far, subbands),
        part,
        (0,),
    )


def lon_exchange(first, second):
    count = lax.axis_size("lon")
    pairs = [(i, (i - 1 + 2 * (i % 2)) % count) for i in range(count)]
    return lax.ppermute(first, "lon", pairs), swapped(second, "lon", 1)


def after(values, others):
    return lax.optimization_barrier((values, others))[0]


def on_device(ocean_field, cotangent, mix_coarse, mix_detail, skip_weight, bias_vector):
    part = (2 * lax.axis_index("lat") + lax.axis_index("lon") % 2).astype(jnp.int32).reshape(1)
    analysis_table, synthesis_table = jnp.asarray(ANALYSIS), jnp.asarray(SYNTHESIS)
    subbands = jnp.asarray(SUBBANDS)
    frame, near, other, far = call(
        analysis_kernel, (COEFS, ROWS, ROWS, FAR), (ocean_field, analysis_table), part
    )
    (pre,) = call(skip_kernel, (FIELD,), (ocean_field, skip_weight, bias_vector.reshape(1, 32)))
    near = swapped(near, "lat", 1)
    other = middle(other)
    far = swapped(far, "lat", 2)
    (near, other, far), pre = lax.optimization_barrier(((near, other, far), pre))
    shares, first, second = lat_sum(frame, near, other, far, 0, part, subbands)
    first, second = lon_exchange(first, second)
    activated, grad_pre, coef, frame, near, other, far = call(
        forward_kernel,
        (shape_of(32, 64, 128, dtype=BF16), FIELD, COEFS, COEFS, ROWS, ROWS, FAR),
        (
            shares,
            first,
            second,
            pre,
            cotangent,
            mix_coarse,
            mix_detail,
            subbands,
            analysis_table,
            synthesis_table,
        ),
        part,
        scratch=(FRAME, pltpu.VMEM((32, 64, 128), BF16), pltpu.SemaphoreType.DMA((4,))),
        in_hbm=(0,),
    )
    (own,) = call(
        weights_kernel,
        (shape_of(264, 128),),
        (ocean_field, grad_pre, coef, frame, near, subbands),
    )
    near = swapped(own, "lat", 1)
    (pair,) = call(pair_kernel, (shape_of(136, 128),), (own, near, far))
    far = swapped(pair, "lat", 2)
    other = middle(after(other, pair))
    sums = pair[:72] + far[:72]
    (skip_back,) = call(skip_back_kernel, (FIELD,), (grad_pre, skip_weight))
    steps = [swapped(sums, "lon", k) for k in (4, 12, 8)]
    near, steps[0] = lax.optimization_barrier((near, steps[0]))
    shares, first, second = lat_sum(frame, near, other, far, 72, part, subbands)
    first, second = lon_exchange(first, second)
    sums = sums + steps[0] + (steps[1] + steps[2])
    step = swapped(sums, "lon", 16)
    sums, first, second, skip_back = lax.optimization_barrier((sums, first, second, skip_back))
    sums = sums + step + (swapped(sums, "lon", 48) + swapped(sums, "lon", 32))
    steps = [swapped(sums, "lon", k) for k in (1, 3, 2)]
    sums = sums + steps[0] + (steps[1] + steps[2])
    (grad_field,) = call(
        backward_kernel,
        (FIELD,),
        (shares, first, second, skip_back, mix_coarse, mix_detail, subbands, synthesis_table),
        part,
        scratch=(FRAME, FRAME, pltpu.VMEM((32, 64, 128), F32), pltpu.SemaphoreType.DMA((4,))),
        in_hbm=(0,),
    )
    cells = LAT_PARTS * LAT_BLOCK * LON_BLOCK * lax.axis_size("lon")
    coarse, detail, grad_skip, grad_bias = call(
        functools.partial(result_kernel, cells=cells),
        (shape_of(4, 32, 32), shape_of(3, 32, 32), shape_of(32, 32), shape_of(1, 32)),
        (sums,),
    )
    return (activated, grad_field, coarse, detail, grad_skip, grad_bias.reshape(32))


def solution(mesh):
    return jax.shard_map(
        on_device,
        mesh=mesh,
        in_specs=(P(None, "lat", "lon"), P(None, "lat", "lon"), P(), P(), P(), P()),
        out_specs=(P(None, "lat", "lon"), P(None, "lat", "lon"), P(), P(), P(), P()),
        check_vma=False,
    )
```

time: 81.2 us -> 76 us (0.936)
  the two profiles are of different devices: /device:TPU:1 before, /device:TPU:6 now
where the time goes in v3:
time: 76 us; the launch traced here: 75.8 us
  starting transfers between devices  40.3 us (53%)
  waiting for transfers between devices  20.6 us (27%)
  Pallas kernels  11.7 us (15%)
  local copies, waits for them, and re-layouts  2.27 us (3%)
  between operations  0.88 us (1%)
    ppermute x15, starting transfers between devices, swapped(): return lax.ppermute(values, axis, [(i, i ^ distance) for i in range(count)])  32.9 us
    ppermute x15, waiting for transfers between devices, swapped(): return lax.ppermute(values, axis, [(i, i ^ distance) for i in range(count)])  14 us
    pallas_call x5, Pallas kernels, call(): pl.pallas_call(kernel, grid_spec=grid_spec, out_shape=list(outs), compile...  7.74 us
    ppermute x2, waiting for transfers between devices, lon_exchange(): return (lax.ppermute(first, 'lon', pairs), swapped(second, 'lon', 1))  6.59 us
    ppermute x2, starting transfers between devices, lon_exchange(): return (lax.ppermute(first, 'lon', pairs), swapped(second, 'lon', 1))  6.01 us
    pallas_call x5, Pallas kernels, call(): pl.pallas_call(kernel, grid=(1,), in_specs=in_specs, out_specs=out_specs,...  4.01 us
    unnamed x24, local copies, waits for them, and re-layouts  2.27 us
  transfers between devices with their start and end apart: 19, of which 10 were waited for; matrix products, arithmetic and copies ran while one was open for 0% of the time, Pallas kernels for 6%

profile of v3, /device:TPU:6, one launch (start us, length us, event | category | flops | bytes accessed | tf_op | source)
XLA Modules:
  0.0 75.8 jit_solution(4802384347896069408)
XLA Ops:
  0.6 0.0 copy-start
  0.7 1.2 %copy-done = f32[32,64,128]{2,1,0:T(8,128)S(1)} copy-done((f32[32,64,128]{2,1,0:T(8,128)S(1)}, f32[32,64,128]{2,1,0:T(8,128)}, u32[]{:S(2)}) %copy-start) | copy-done | bytes 1048600
  1.9 1.0 %copy-done.3 = bf16[1536,128]{1,0:T(8,128)(2,1)S(1)} copy-done((bf16[1536,128]{1,0:T(8,128)(2,1)S(1)}, bf16[1536,128]{1,0:T(8,128)(2,1)}, u32[]{:S(2)}) %copy-start.3) | copy-done | bytes 393240
  2.9 1.1 %shard_map.145 = (f32[512,128]{1,0:T(8,128)S(1)}, f32[192,128]{1,0:T(8,128)S(1)}, f32[192,128]{1,0:T(8,128)S(1)}, f32[64,128]{1,0:T(8,128)S(1)}) custom-call(s32[1]{0:T(128)} %bitcast.part_ref, f32[32,64,128]{2,1,0:T(8,128)S(1)} %copy-done, bf16[1536,128]{1,0:T(8,128)(2,1)S(1)} %copy-done.3), custom_call_target="tpu_custom_call" | custom-call | tf_op jit(solution)/shard_map/pallas_call | solution.py:558
  4.0 0.1 collective-permute-start
  4.1 0.7 collective-permute-start.1
  4.7 0.0 copy-start.11
  4.8 8.5 %collective-permute-start.2 = (f32[64,128]{1,0:T(8,128)S(1)}, f32[64,128]{1,0:T(8,128)S(1)}, u32[]{:S(2)}, u32[]{:S(2)}) collective-permute-start(f32[64,128]{1,0:T(8,128)S(1)} %get-tuple-element.41), channel_id=1, source_target_pairs={{0,2},{1,3},{2,0},{3,1},{4,6},{5,7},{6,4},{7,5},{8,10},{9,11},{10,... | collective-permute-start | bytes 98312 | tf_op jit(solution)/shard_map/ppermute | solution.py:572
  13.3 0.0 copy-done.1
  13.3 0.0 copy-done.10
  13.3 0.0 copy-done.11
  13.3 0.0 copy-start.9
  13.3 0.0 copy-start.4
  13.3 0.0 copy-start.5
  13.3 0.8 %shard_map.146.pre_ref = f32[32,64,128]{2,1,0:T(8,128)S(1)} custom-call(f32[32,64,128]{2,1,0:T(8,128)S(1)} %copy-done.1, f32[32,32]{1,0:T(8,128)S(1)} %copy-done.10, f32[1,32]{1,0:T(1,128)S(1)} %bitcast.3), custom_call_target="tpu_custom_call" | custom-call | tf_op jit(solution)/shard_map/pallas_call | solution.py:542
  14.2 0.0 copy-start.2
  14.2 2.0 %collective-permute-done.2.far_ref = f32[64,128]{1,0:T(8,128)S(1)} collective-permute-done((f32[64,128]{1,0:T(8,128)S(1)}, f32[64,128]{1,0:T(8,128)S(1)}, u32[]{:S(2)}, u32[]{:S(2)}) %collective-permute-start.2) | collective-permute-done | bytes 32800 | tf_op jit(solution)/shard_map/ppermute | solution.py:572
  16.2 0.0 collective-permute-done.near_ref
  16.2 0.0 collective-permute-done.1.other_ref
  16.2 0.0 copy-done.8
  16.2 0.0 copy-done.9
  16.2 0.0 copy-start.6
  16.2 0.0 copy-start.7
  16.2 0.3 shard_map.147
  16.6 3.7 %collective-permute-start.3 = (f32[11,16,128]{2,1,0:T(8,128)S(1)}, f32[11,16,128]{2,1,0:T(8,128)S(1)}, u32[]{:S(2)}, u32[]{:S(2)}) collective-permute-start(f32[11,16,128]{2,1,0:T(8,128)S(1)} %get-tuple-element.46), channel_id=1, source_target_pairs={{0,252},{4,8},{8,4},{12,16},{16,12},{20,24},{24,20},{28,32},{32,28... | collective-permute-start | bytes 270344 | tf_op jit(solution)/shard_map/ppermute | solution.py:600
  20.3 0.5 collective-permute-start.4
  20.7 3.2 %collective-permute-done.3.first_ref = f32[11,16,128]{2,1,0:T(8,128)S(1)} collective-permute-done((f32[11,16,128]{2,1,0:T(8,128)S(1)}, f32[11,16,128]{2,1,0:T(8,128)S(1)}, u32[]{:S(2)}, u32[]{:S(2)}) %collective-permute-start.3) | collective-permute-done | bytes 90144 | tf_op jit(solution)/shard_map/ppermute | solution.py:600
  23.9 1.0 %collective-permute-done.4.second_ref = f32[11,16,128]{2,1,0:T(8,128)S(1)} collective-permute-done((f32[11,16,128]{2,1,0:T(8,128)S(1)}, f32[11,16,128]{2,1,0:T(8,128)S(1)}, u32[]{:S(2)}, u32[]{:S(2)}) %collective-permute-start.4) | collective-permute-done | bytes 90144 | tf_op jit(solution)/shard_map/ppermute | solution.py:572
  24.9 0.0 copy-done.4
  24.9 0.0 copy-done.5
  24.9 3.6 %shard_map.148 = (bf16[32,64,128]{2,1,0:T(8,128)(2,1)}, f32[32,64,128]{2,1,0:T(8,128)S(1)}, f32[512,128]{1,0:T(8,128)S(1)}, f32[512,128]{1,0:T(8,128)S(1)}, f32[...) custom-call(s32[1]{0:T(128)} %bitcast.part_ref, f32[512,128]{1,0:T(8,128)S(1)} %get-tuple-element.45.shares_ref, ...), custom_call_target="tpu_custom_call" | custom-call | tf_op jit(solution)/shard_map/pallas_call | solution.py:558
  28.5 1.6 %shard_map.149.own_ref = f32[264,128]{1,0:T(8,128)S(1)} custom-call(f32[32,64,128]{2,1,0:T(8,128)S(1)} %copy-done.1, f32[32,64,128]{2,1,0:T(8,128)S(1)} %get-tuple-element.51.g_ref, f32[512,128]{1,0:T(8,128)S(1)} %get-tuple-element.52.coef_ref, f32[512,128]{1,0:T(8,128)S(1)} %get-tuple-element.50.frame_ref, f32[192,128]{1,0:T(8,128)S(1)} %get-tuple-element.53.near_ref, ...), custom_call_target="tpu_custom_call" | custom-call | tf_op jit(solution)/shard_map/pallas_call | solution.py:542
  30.1 2.2 %collective-permute-start.5 = (f32[264,128]{1,0:T(8,128)S(1)}, f32[264,128]{1,0:T(8,128)S(1)}, u32[]{:S(2)}, u32[]{:S(2)}) collective-permute-start(f32[264,128]{1,0:T(8,128)S(1)} %shard_map.149.own_ref), channel_id=1, source_target_pairs={{0,1},{1,0},{2,3},{3,2},{4,5},{5,4},{6,7},{7,6},{8,9},{9,8},{10,11... | collective-permute-start | bytes 405512 | tf_op jit(solution)/shard_map/ppermute | solution.py:572
  32.3 1.0 %collective-permute-done.5.near_ref = f32[264,128]{1,0:T(8,128)S(1)} collective-permute-done((f32[264,128]{1,0:T(8,128)S(1)}, f32[264,128]{1,0:T(8,128)S(1)}, u32[]{:S(2)}, u32[]{:S(2)}) %collective-permute-start.5) | collective-permute-done | bytes 135200 | tf_op jit(solution)/shard_map/ppermute | solution.py:572
  33.3 4.7 %collective-permute-start.6 = (f32[136,128]{1,0:T(8,128)S(1)}, f32[136,128]{1,0:T(8,128)S(1)}, u32[]{:S(2)}, u32[]{:S(2)}) collective-permute-start(f32[136,128]{1,0:T(8,128)S(1)} %shard_map.150), channel_id=1, source_target_pairs={{0,2},{1,3},{2,0},{3,1},{4,6},{5,7},{6,4},{7,5},{8,10},{9,11},{10,... | collective-permute-start | bytes 208904 | tf_op jit(solution)/shard_map/ppermute | solution.py:572
  38.0 0.7 collective-permute-start.8
  38.7 3.2 %collective-permute-done.6.far_ref = f32[136,128]{1,0:T(8,128)S(1)} collective-permute-done((f32[136,128]{1,0:T(8,128)S(1)}, f32[136,128]{1,0:T(8,128)S(1)}, u32[]{:S(2)}, u32[]{:S(2)}) %collective-permute-start.6) | collective-permute-done | bytes 69664 | tf_op jit(solution)/shard_map/ppermute | solution.py:572
  41.9 0.5 collective-permute-start.7
  42.4 5.5 %collective-permute-start.10 = (f32[72,128]{1,0:T(8,128)S(1)}, f32[72,128]{1,0:T(8,128)S(1)}, u32[]{:S(2)}, u32[]{:S(2)}) collective-permute-start(f32[72,128]{1,0:T(8,128)S(1)} %slice_add_fusion), channel_id=1, source_target_pairs={{0,32},{4,36},{8,40},{12,44},{16,48},{20,52},{24,56},{28,60},{32,0... | collective-permute-start | bytes 110600 | tf_op jit(solution)/shard_map/ppermute | solution.py:572
  47.9 0.0 collective-permute-start.9
  47.9 0.8 %shard_map.152.skip_ref = f32[32,64,128]{2,1,0:T(8,128)S(1)} custom-call(f32[32,64,128]{2,1,0:T(8,128)S(1)} %get-tuple-element.51.g_ref, f32[32,32]{1,0:T(8,128)S(1)} %copy-done.10), custom_call_target="tpu_custom_call" | custom-call | tf_op jit(solution)/shard_map/pallas_call | solution.py:542
  48.7 0.0 collective-permute-done.7
  48.8 0.0 collective-permute-done.8.other_ref
  48.8 0.3 shard_map.151
  49.1 2.3 %collective-permute-start.11 = (f32[11,16,128]{2,1,0:T(8,128)S(1)}, f32[11,16,128]{2,1,0:T(8,128)S(1)}, u32[]{:S(2)}, u32[]{:S(2)}) collective-permute-start(f32[11,16,128]{2,1,0:T(8,128)S(1)} %get-tuple-element.60), channel_id=1, source_target_pairs={{0,252},{4,8},{8,4},{12,16},{16,12},{20,24},{24,20},{28,32},{32,28... | collective-permute-start | bytes 270344 | tf_op jit(solution)/shard_map/ppermute | solution.py:600
  51.4 0.0 collective-permute-start.12
  51.4 0.0 collective-permute-done.10
  51.4 1.7 %collective-permute-done.9 = f32[72,128]{1,0:T(8,128)S(1)} collective-permute-done((f32[72,128]{1,0:T(8,128)S(1)}, f32[72,128]{1,0:T(8,128)S(1)}, u32[]{:S(2)}, u32[]{:S(2)}) %collective-permute-start.9) | collective-permute-done | bytes 36896 | tf_op jit(solution)/shard_map/ppermute | solution.py:572
  53.1 0.8 collective-permute-start.13
  53.8 3.4 %collective-permute-done.11.first_ref = f32[11,16,128]{2,1,0:T(8,128)S(1)} collective-permute-done((f32[11,16,128]{2,1,0:T(8,128)S(1)}, f32[11,16,128]{2,1,0:T(8,128)S(1)}, u32[]{:S(2)}, u32[]{:S(2)}) %collective-permute-start.11) | collective-permute-done | bytes 90144 | tf_op jit(solution)/shard_map/ppermute | solution.py:600
  57.3 0.0 collective-permute-done.12.second_ref
  57.3 2.8 %collective-permute-start.15 = (f32[72,128]{1,0:T(8,128)S(1)}, f32[72,128]{1,0:T(8,128)S(1)}, u32[]{:S(2)}, u32[]{:S(2)}) collective-permute-start(f32[72,128]{1,0:T(8,128)S(1)} %add_add_fusion.2), channel_id=1, source_target_pairs={{0,128},{4,132},{8,136},{12,140},{16,144},{20,148},{24,152},{28,15... | collective-permute-start | bytes 110600 | tf_op jit(solution)/shard_map/ppermute | solution.py:572
  60.1 1.0 %collective-permute-start.14 = (f32[72,128]{1,0:T(8,128)S(1)}, f32[72,128]{1,0:T(8,128)S(1)}, u32[]{:S(2)}, u32[]{:S(2)}) collective-permute-start(f32[72,128]{1,0:T(8,128)S(1)} %add_add_fusion.2), channel_id=1, source_target_pairs={{0,192},{4,196},{8,200},{12,204},{16,208},{20,212},{24,216},{28,22... | collective-permute-start | bytes 110600 | tf_op jit(solution)/shard_map/ppermute | solution.py:572
  61.1 0.0 collective-permute-done.13
  61.1 1.6 %collective-permute-done.15 = f32[72,128]{1,0:T(8,128)S(1)} collective-permute-done((f32[72,128]{1,0:T(8,128)S(1)}, f32[72,128]{1,0:T(8,128)S(1)}, u32[]{:S(2)}, u32[]{:S(2)}) %collective-permute-start.15) | collective-permute-done | bytes 36896 | tf_op jit(solution)/shard_map/ppermute | solution.py:572
  62.7 2.5 %collective-permute-done.14 = f32[72,128]{1,0:T(8,128)S(1)} collective-permute-done((f32[72,128]{1,0:T(8,128)S(1)}, f32[72,128]{1,0:T(8,128)S(1)}, u32[]{:S(2)}, u32[]{:S(2)}) %collective-permute-start.14) | collective-permute-done | bytes 36896 | tf_op jit(solution)/shard_map/ppermute | solution.py:572
  65.3 2.9 %collective-permute-start.18 = (f32[72,128]{1,0:T(8,128)S(1)}, f32[72,128]{1,0:T(8,128)S(1)}, u32[]{:S(2)}, u32[]{:S(2)}) collective-permute-start(f32[72,128]{1,0:T(8,128)S(1)} %add_add_fusion.1), channel_id=1, source_target_pairs={{0,8},{4,12},{8,0},{12,4},{16,24},{20,28},{24,16},{28,20},{32,40},... | collective-permute-start | bytes 110600 | tf_op jit(solution)/shard_map/ppermute | solution.py:572
  68.2 2.9 %collective-permute-start.17 = (f32[72,128]{1,0:T(8,128)S(1)}, f32[72,128]{1,0:T(8,128)S(1)}, u32[]{:S(2)}, u32[]{:S(2)}) collective-permute-start(f32[72,128]{1,0:T(8,128)S(1)} %add_add_fusion.1), channel_id=1, source_target_pairs={{0,12},{4,8},{8,4},{12,0},{16,28},{20,24},{24,20},{28,16},{32,44},... | collective-permute-start | bytes 110600 | tf_op jit(solution)/shard_map/ppermute | solution.py:572
  71.1 0.5 collective-permute-start.16
  71.6 2.4 %shard_map.153 = f32[32,64,128]{2,1,0:T(8,128)} custom-call(s32[1]{0:T(128)} %bitcast.part_ref, f32[512,128]{1,0:T(8,128)S(1)} %get-tuple-element.58.shares_ref, f32[11,16,128]{2,1,0:T(8,128)S(1)} %collective-permute-done.11.first_ref, f32[11,16,128]{2,1,0:T(8,128)S(1)} %collective-permute-done.12.second_ref, f32[32,64,128]{2,1,0:T(8,128)S(1)} %shard_map.152.skip_ref, ...), custom_call_target="tpu_custom_call" | custom-call | tf_op jit(solution)/shard_map/pallas_call | solution.py:558
  74.0 0.0 collective-permute-done.18
  74.0 0.0 collective-permute-done.17
  74.0 1.0 %collective-permute-done.16 = f32[72,128]{1,0:T(8,128)S(1)} collective-permute-done((f32[72,128]{1,0:T(8,128)S(1)}, f32[72,128]{1,0:T(8,128)S(1)}, u32[]{:S(2)}, u32[]{:S(2)}) %collective-permute-start.16) | collective-permute-done | bytes 36896 | tf_op jit(solution)/shard_map/ppermute | solution.py:572
  75.1 0.7 shard_map.154
  (12 shorter events, 0.1 us)
Async XLA Ops:
  0.6 1.2 %copy-start = (f32[32,64,128]{2,1,0:T(8,128)S(1)}, f32[32,64,128]{2,1,0:T(8,128)}, u32[]{:S(2)}) copy-start(f32[32,64,128]{2,1,0:T(8,128)} %x_ref.5) | copy-start | bytes 3145732
  1.9 1.0 %copy-start.3 = (bf16[1536,128]{1,0:T(8,128)(2,1)S(1)}, bf16[1536,128]{1,0:T(8,128)(2,1)}, u32[]{:S(2)}) copy-start(bf16[1536,128]{1,0:T(8,128)(2,1)} %constant.30.clone.table_ref.analysis_ref) | copy-start | bytes 1179652
  2.9 10.4 %copy-start.1 = (f32[32,64,128]{2,1,0:T(8,128)S(1)}, f32[32,64,128]{2,1,0:T(8,128)}, u32[]{:S(2)}) copy-start(f32[32,64,128]{2,1,0:T(8,128)} %x_ref.5) | copy-start | bytes 3145732
  2.9 10.4 %copy-start.10 = (f32[32,32]{1,0:T(8,128)S(1)}, f32[32,32]{1,0:T(8,128)}, u32[]{:S(2)}) copy-start(f32[32,32]{1,0:T(8,128)} %skip_ref.3) | copy-start | bytes 12292
  4.0 12.2 %collective-permute-start = (f32[192,128]{1,0:T(8,128)S(1)}, f32[192,128]{1,0:T(8,128)S(1)}, u32[]{:S(2)}, u32[]{:S(2)}) collective-permute-start(f32[192,128]{1,0:T(8,128)S(1)} %get-tuple-element.39), channel_id=1, source_target_pairs={{0,1},{1,0},{2,3},{3,2},{4,5},{5,4},{6,7},{7,6},{8,9},{9,8},{10,11... | collective-permute-start | bytes 294920 | tf_op jit(solution)/shard_map/ppermute | solution.py:572
  4.1 12.1 %collective-permute-start.1 = (f32[192,128]{1,0:T(8,128)S(1)}, f32[192,128]{1,0:T(8,128)S(1)}, u32[]{:S(2)}, u32[]{:S(2)}) collective-permute-start(f32[192,128]{1,0:T(8,128)S(1)} %get-tuple-element.40), channel_id=1, source_target_pairs={{1,2},{2,1},{5,6},{6,5},{9,10},{10,9},{13,14},{14,13},{17,18},{18,... | collective-permute-start | bytes 294920 | tf_op jit(solution)/shard_map/ppermute | solution.py:584
  4.7 8.5 %copy-start.11 = (f32[32]{0:T(128)S(1)}, f32[32]{0:T(128)}, u32[]{:S(2)}) copy-start(f32[32]{0:T(128)} %param.15) | copy-start | bytes 388
  4.8 11.4 %collective-permute-start.2 = (f32[64,128]{1,0:T(8,128)S(1)}, f32[64,128]{1,0:T(8,128)S(1)}, u32[]{:S(2)}, u32[]{:S(2)}) collective-permute-start(f32[64,128]{1,0:T(8,128)S(1)} %get-tuple-element.41), channel_id=1, source_target_pairs={{0,2},{1,3},{2,0},{3,1},{4,6},{5,7},{6,4},{7,5},{8,10},{9,11},{10,... | collective-permute-start | bytes 98312 | tf_op jit(solution)/shard_map/ppermute | solution.py:572
  13.3 2.9 %copy-start.8 = (f32[4,16,128]{2,1,0:T(8,128)S(1)}, f32[4,16,128]{2,1,0:T(8,128)}, u32[]{:S(2)}) copy-start(f32[4,16,128]{2,1,0:T(8,128)} %constant.33.clone.mask_ref) | copy-start | bytes 98308
  13.3 2.9 %copy-start.9 = (f32[8,128]{1,0:T(8,128)S(1)}, f32[8,128]{1,0:T(8,128)}, u32[]{:S(2)}) copy-start(f32[8,128]{1,0:T(8,128)} %constant.32.clone.subband_ref) | copy-start | bytes 12292
  13.3 11.6 %copy-start.4 = (bf16[1536,128]{1,0:T(8,128)(2,1)S(1)}, bf16[1536,128]{1,0:T(8,128)(2,1)}, u32[]{:S(2)}) copy-start(bf16[1536,128]{1,0:T(8,128)(2,1)} %constant.30.clone.table_ref.analysis_ref) | copy-start | bytes 1179652
  13.3 11.6 %copy-start.5 = (bf16[32,64,128]{2,1,0:T(8,128)(2,1)S(1)}, bf16[32,64,128]{2,1,0:T(8,128)(2,1)}, u32[]{:S(2)}) copy-start(bf16[32,64,128]{2,1,0:T(8,128)(2,1)} %cot_ref.1) | copy-start | bytes 1572868
  14.2 10.7 %copy-start.2 = (bf16[1536,128]{1,0:T(8,128)(2,1)S(1)}, bf16[1536,128]{1,0:T(8,128)(2,1)}, u32[]{:S(2)}) copy-start(bf16[1536,128]{1,0:T(8,128)(2,1)} %constant.31.clone.synthesis_ref) | copy-start | bytes 1179652
  16.2 8.7 %copy-start.6 = (f32[4,32,32]{2,1,0:T(8,128)S(1)}, f32[4,32,32]{2,1,0:T(8,128)}, u32[]{:S(2)}) copy-start(f32[4,32,32]{2,1,0:T(8,128)} %coarse_ref.3) | copy-start | bytes 49156
  16.2 8.7 %copy-start.7 = (f32[3,32,32]{2,1,0:T(8,128)S(1)}, f32[3,32,32]{2,1,0:T(8,128)}, u32[]{:S(2)}) copy-start(f32[3,32,32]{2,1,0:T(8,128)} %detail_ref.3) | copy-start | bytes 36868
  16.6 7.3 %collective-permute-start.3 = (f32[11,16,128]{2,1,0:T(8,128)S(1)}, f32[11,16,128]{2,1,0:T(8,128)S(1)}, u32[]{:S(2)}, u32[]{:S(2)}) collective-permute-start(f32[11,16,128]{2,1,0:T(8,128)S(1)} %get-tuple-element.46), channel_id=1, source_target_pairs={{0,252},{4,8},{8,4},{12,16},{16,12},{20,24},{24,20},{28,32},{32,28... | collective-permute-start | bytes 270344 | tf_op jit(solution)/shard_map/ppermute | solution.py:600
  20.3 4.6 %collective-permute-start.4 = (f32[11,16,128]{2,1,0:T(8,128)S(1)}, f32[11,16,128]{2,1,0:T(8,128)S(1)}, u32[]{:S(2)}, u32[]{:S(2)}) collective-permute-start(f32[11,16,128]{2,1,0:T(8,128)S(1)} %get-tuple-element.47), channel_id=1, source_target_pairs={{0,4},{4,0},{8,12},{12,8},{16,20},{20,16},{24,28},{28,24},{32,36},... | collective-permute-start | bytes 270344 | tf_op jit(solution)/shard_map/ppermute | solution.py:572
  30.1 3.2 %collective-permute-start.5 = (f32[264,128]{1,0:T(8,128)S(1)}, f32[264,128]{1,0:T(8,128)S(1)}, u32[]{:S(2)}, u32[]{:S(2)}) collective-permute-start(f32[264,128]{1,0:T(8,128)S(1)} %shard_map.149.own_ref), channel_id=1, source_target_pairs={{0,1},{1,0},{2,3},{3,2},{4,5},{5,4},{6,7},{7,6},{8,9},{9,8},{10,11... | collective-permute-start | bytes 405512 | tf_op jit(solution)/shard_map/ppermute | solution.py:572
  33.3 8.6 %collective-permute-start.6 = (f32[136,128]{1,0:T(8,128)S(1)}, f32[136,128]{1,0:T(8,128)S(1)}, u32[]{:S(2)}, u32[]{:S(2)}) collective-permute-start(f32[136,128]{1,0:T(8,128)S(1)} %shard_map.150), channel_id=1, source_target_pairs={{0,2},{1,3},{2,0},{3,1},{4,6},{5,7},{6,4},{7,5},{8,10},{9,11},{10,... | collective-permute-start | bytes 208904 | tf_op jit(solution)/shard_map/ppermute | solution.py:572
  38.0 10.7 %collective-permute-start.8 = (f32[192,128]{1,0:T(8,128)S(1)}, f32[192,128]{1,0:T(8,128)S(1)}, u32[]{:S(2)}, u32[]{:S(2)}) collective-permute-start(f32[192,128]{1,0:T(8,128)S(1)} %get-tuple-element.57), channel_id=1, source_target_pairs={{1,2},{2,1},{5,6},{6,5},{9,10},{10,9},{13,14},{14,13},{17,18},{18,... | collective-permute-start | bytes 294920 | tf_op jit(solution)/shard_map/ppermute | solution.py:584
  41.9 6.9 %collective-permute-start.7 = (f32[72,128]{1,0:T(8,128)S(1)}, f32[72,128]{1,0:T(8,128)S(1)}, u32[]{:S(2)}, u32[]{:S(2)}) collective-permute-start(f32[72,128]{1,0:T(8,128)S(1)} %slice_add_fusion), channel_id=1, source_target_pairs={{0,16},{4,20},{8,24},{12,28},{16,0},{20,4},{24,8},{28,12},{32,48},... | collective-permute-start | bytes 110600 | tf_op jit(solution)/shard_map/ppermute | solution.py:572
  42.4 9.0 %collective-permute-start.10 = (f32[72,128]{1,0:T(8,128)S(1)}, f32[72,128]{1,0:T(8,128)S(1)}, u32[]{:S(2)}, u32[]{:S(2)}) collective-permute-start(f32[72,128]{1,0:T(8,128)S(1)} %slice_add_fusion), channel_id=1, source_target_pairs={{0,32},{4,36},{8,40},{12,44},{16,48},{20,52},{24,56},{28,60},{32,0... | collective-permute-start | bytes 110600 | tf_op jit(solution)/shard_map/ppermute | solution.py:572
  47.9 5.2 %collective-permute-start.9 = (f32[72,128]{1,0:T(8,128)S(1)}, f32[72,128]{1,0:T(8,128)S(1)}, u32[]{:S(2)}, u32[]{:S(2)}) collective-permute-start(f32[72,128]{1,0:T(8,128)S(1)} %slice_add_fusion), channel_id=1, source_target_pairs={{0,48},{4,52},{8,56},{12,60},{16,32},{20,36},{24,40},{28,44},{32,1... | collective-permute-start | bytes 110600 | tf_op jit(solution)/shard_map/ppermute | solution.py:572
  49.1 8.2 %collective-permute-start.11 = (f32[11,16,128]{2,1,0:T(8,128)S(1)}, f32[11,16,128]{2,1,0:T(8,128)S(1)}, u32[]{:S(2)}, u32[]{:S(2)}) collective-permute-start(f32[11,16,128]{2,1,0:T(8,128)S(1)} %get-tuple-element.60), channel_id=1, source_target_pairs={{0,252},{4,8},{8,4},{12,16},{16,12},{20,24},{24,20},{28,32},{32,28... | collective-permute-start | bytes 270344 | tf_op jit(solution)/shard_map/ppermute | solution.py:600
  51.4 5.9 %collective-permute-start.12 = (f32[11,16,128]{2,1,0:T(8,128)S(1)}, f32[11,16,128]{2,1,0:T(8,128)S(1)}, u32[]{:S(2)}, u32[]{:S(2)}) collective-permute-start(f32[11,16,128]{2,1,0:T(8,128)S(1)} %get-tuple-element.61), channel_id=1, source_target_pairs={{0,4},{4,0},{8,12},{12,8},{16,20},{20,16},{24,28},{28,24},{32,36},... | collective-permute-start | bytes 270344 | tf_op jit(solution)/shard_map/ppermute | solution.py:572
  53.1 8.1 %collective-permute-start.13 = (f32[72,128]{1,0:T(8,128)S(1)}, f32[72,128]{1,0:T(8,128)S(1)}, u32[]{:S(2)}, u32[]{:S(2)}) collective-permute-start(f32[72,128]{1,0:T(8,128)S(1)} %add_add_fusion.2), channel_id=1, source_target_pairs={{0,64},{4,68},{8,72},{12,76},{16,80},{20,84},{24,88},{28,92},{32,9... | collective-permute-start | bytes 110600 | tf_op jit(solution)/shard_map/ppermute | solution.py:572
  57.3 5.5 %collective-permute-start.15 = (f32[72,128]{1,0:T(8,128)S(1)}, f32[72,128]{1,0:T(8,128)S(1)}, u32[]{:S(2)}, u32[]{:S(2)}) collective-permute-start(f32[72,128]{1,0:T(8,128)S(1)} %add_add_fusion.2), channel_id=1, source_target_pairs={{0,128},{4,132},{8,136},{12,140},{16,144},{20,148},{24,152},{28,15... | collective-permute-start | bytes 110600 | tf_op jit(solution)/shard_map/ppermute | solution.py:572
  60.1 5.2 %collective-permute-start.14 = (f32[72,128]{1,0:T(8,128)S(1)}, f32[72,128]{1,0:T(8,128)S(1)}, u32[]{:S(2)}, u32[]{:S(2)}) collective-permute-start(f32[72,128]{1,0:T(8,128)S(1)} %add_add_fusion.2), channel_id=1, source_target_pairs={{0,192},{4,196},{8,200},{12,204},{16,208},{20,212},{24,216},{28,22... | collective-permute-start | bytes 110600 | tf_op jit(solution)/shard_map/ppermute | solution.py:572
  65.3 8.8 %collective-permute-start.18 = (f32[72,128]{1,0:T(8,128)S(1)}, f32[72,128]{1,0:T(8,128)S(1)}, u32[]{:S(2)}, u32[]{:S(2)}) collective-permute-start(f32[72,128]{1,0:T(8,128)S(1)} %add_add_fusion.1), channel_id=1, source_target_pairs={{0,8},{4,12},{8,0},{12,4},{16,24},{20,28},{24,16},{28,20},{32,40},... | collective-permute-start | bytes 110600 | tf_op jit(solution)/shard_map/ppermute | solution.py:572
  68.2 5.9 %collective-permute-start.17 = (f32[72,128]{1,0:T(8,128)S(1)}, f32[72,128]{1,0:T(8,128)S(1)}, u32[]{:S(2)}, u32[]{:S(2)}) collective-permute-start(f32[72,128]{1,0:T(8,128)S(1)} %add_add_fusion.1), channel_id=1, source_target_pairs={{0,12},{4,8},{8,4},{12,0},{16,28},{20,24},{24,20},{28,16},{32,44},... | collective-permute-start | bytes 110600 | tf_op jit(solution)/shard_map/ppermute | solution.py:572
  71.1 4.0 %collective-permute-start.16 = (f32[72,128]{1,0:T(8,128)S(1)}, f32[72,128]{1,0:T(8,128)S(1)}, u32[]{:S(2)}, u32[]{:S(2)}) collective-permute-start(f32[72,128]{1,0:T(8,128)S(1)} %add_add_fusion.1), channel_id=1, source_target_pairs={{0,4},{4,0},{8,12},{12,8},{16,20},{20,16},{24,28},{28,24},{32,36},... | collective-permute-start | bytes 110600 | tf_op jit(solution)/shard_map/ppermute | solution.py:572

commit v4 on v3

--- a/solution.py
+++ b/solution.py
@@ -41,6 +41,7 @@
 LAT_BAND = (0, 1, 0, 1, 3, 2, 3)
 LON_BAND = (0, 0, 1, 1, 2, 3, 3)
 LO_LANES = 42
+FAR_SHIFT = 32
 HI_LANE = 64
 
 
@@ -67,13 +68,15 @@
 
 def lane_table():
     lanes = [None] * 128
-    inner = []
+    coarse_inner, inner = [], []
     for s in range(7):
         count = 14 if s < 4 else 22
         for e in range(6):
             lanes[s * 6 + e] = (s, e)
             lanes[HI_LANE + s * 6 + e] = (s, count - 6 + e)
-        inner += [(s, e) for e in range(6, count - 6)]
+        target = coarse_inner if s < 4 else inner
+        target += [(s, e) for e in range(6, count - 6)]
+    lanes[HI_LANE - 8 : HI_LANE] = coarse_inner
     free = [lane for lane in range(128) if lanes[lane] is None]
     for lane, entry in zip(free, inner):
         lanes[lane] = entry
@@ -178,15 +181,18 @@
     return product(a[0], b[0]) + (product(a[0], b[1]) + product(a[1], b[0]))
 
 
-def lat_matrix(table_ref, part):
+def lat_matrix(block):
     row = lax.broadcasted_iota(jnp.int32, (256, 256), 0)
     keep = row // 64 == lane_index((256, 256)) // 64
-    first = pl.multiple_of(LON_ROWS + 128 * part, 128)
-    block = table_ref[pl.ds(first, 128), :]
     return tuple(
         jnp.where(keep, jnp.tile(block[64 * k : 64 * k + 64], (4, 2)), 0.0).astype(BF16)
         for k in range(2)
     )
+
+
+def lat_filters(table_ref, part_ref):
+    first = pl.multiple_of(LON_ROWS + 128 * lat_part(part_ref), 128)
+    return lat_matrix(table_ref[pl.ds(first, 128), :])
 
 
 def lon_analysis(table_ref):
@@ -235,9 +241,9 @@
 
 
 def synthesis_rows(frame, lon):
-    wide = dot3(split(frame), lon).reshape(8, 4, 16, 512)
+    wide = dot3(split(frame), lon).reshape(-1, 4, 16, 512)
     groups = []
-    for g in range(8):
+    for g in range(wide.shape[0]):
         part = jnp.stack(
             [wide[g, :, :, 128 * b : 128 * b + 128] for b in range(4)], axis=1
         )
@@ -280,13 +286,10 @@
 
 
 def stacked(data, subbands):
-    lanes = jnp.concatenate([subbands[0:1]] * 16, axis=1)
-    return [
-        jnp.concatenate(
-            [jnp.where(lanes == float(s), part, 0.0).astype(BF16) for s in range(7)], axis=0
-        )
-        for part in (data, data - data.astype(BF16).astype(F32))
+    masks = [
+        jnp.concatenate([(subbands[0:1] == float(s)).astype(BF16)] * 16, axis=1) for s in range(7)
     ]
+    return [jnp.concatenate([part * mask for mask in masks], axis=0) for part in split(data)]
 
 
 def mixed(frame_ref, weights, subbands, scratch):
@@ -299,17 +302,29 @@
     return scratch[...]
 
 
-def store_frame(frame, frame_ref, near_ref, other_ref, far_ref):
+def coarse_lanes():
+    lane = lane_index((1, 128))
+    return (lane < 24) | ((lane >= HI_LANE - 8) & (lane < HI_LANE + 24))
+
+
+def store_frame(frame, frame_ref, near_ref, other_ref):
     frame_ref[...] = frame.reshape(512, 128)
-    for target, first, rows in ((near_ref, 0, 6), (other_ref, 8, 6), (far_ref, 14, 2)):
-        for r in range(rows):
+    for target, first in ((near_ref, 0), (other_ref, 8)):
+        for r in range(6):
             target[32 * r : 32 * r + 32] = frame_ref[pl.ds(first + r, 32, stride=16), :]
 
 
+def far_rows(frame_ref):
+    coarse = coarse_lanes()
+    rows = [jnp.where(coarse, frame_ref[pl.ds(14 + r, 32, stride=16), :], 0.0) for r in range(2)]
+    return rows[0] + pltpu.roll(rows[1], FAR_SHIFT, 1)
+
+
 def analysis_kernel(part_ref, x_ref, table_ref, frame_ref, near_ref, other_ref, far_ref):
-    lat = lat_matrix(table_ref, lat_part(part_ref))
+    lat = lat_filters(table_ref, part_ref)
     frame = analysis(grouped(x_ref[...]), lat, lon_analysis(table_ref))
-    store_frame(frame, frame_ref, near_ref, other_ref, far_ref)
+    store_frame(frame, frame_ref, near_ref, other_ref)
+    far_ref[...] = far_rows(frame_ref)
 
 
 def expand_matrix():
@@ -348,7 +363,6 @@
     near_ref,
     other_ref,
     far_ref,
-    subband_ref,
     sum_ref,
     first_ref,
     second_ref,
@@ -357,14 +371,13 @@
 ):
     frame = frame_ref[...].reshape(32, 16, 128) * mask_ref[0][None]
     sum_ref[...] = frame.reshape(512, 128)
-    subband = subband_ref[0:1]
-    four = (subband >= 0.0) & (subband < 4.0)
+    coarse = coarse_lanes()
     for r in range(6):
         sum_ref[pl.ds(r, 32, stride=16), :] += near_ref[32 * r : 32 * r + 32]
         sum_ref[pl.ds(8 + r, 32, stride=16), :] += other_ref[32 * r : 32 * r + 32]
-    for r in range(2):
-        far = far_ref[far_row + 32 * r : far_row + 32 * r + 32]
-        sum_ref[pl.ds(14 + r, 32, stride=16), :] += jnp.where(four, far, 0.0)
+    far = far_ref[far_row : far_row + 32]
+    for r, shared in enumerate((far, pltpu.roll(far, 128 - FAR_SHIFT, 1))):
+        sum_ref[pl.ds(14 + r, 32, stride=16), :] += jnp.where(coarse, shared, 0.0)
     frame = sum_ref[...].reshape(32, 16, 128)
     low, high = edge_lanes(frame, 0), edge_lanes(frame, HI_LANE)
     even = is_even(part_ref)
@@ -390,7 +403,6 @@
     frame_ref,
     near_ref,
     other_ref,
-    far_ref,
     scratch,
     act,
     done,
@@ -402,12 +414,12 @@
         [coarse_ref[s].T for s in range(4)] + [detail_ref[s].T for s in range(3)], axis=1
     )
     frame = mixed(coef_ref, weights, subband_ref[...], scratch)
-    rows = synthesis_rows(frame, lon_synthesis(synthesis_ref))
-    lat = lat_matrix(synthesis_ref, lat_part(part_ref))
+    lon = lon_synthesis(synthesis_ref)
+    lat = lat_filters(synthesis_ref, part_ref)
     grads = []
     stores = []
     for q in range(4):
-        kernel = dot3(lat, split(rows[:, 256 * q : 256 * q + 256]))
+        kernel = dot3(lat, split(synthesis_rows(frame[128 * q : 128 * q + 128], lon)))
         for g in (2 * q, 2 * q + 1):
             channels = slice(4 * g, 4 * g + 4)
             lanes = slice(128 * (g - 2 * q), 128 * (g - 2 * q) + 128)
@@ -423,10 +435,10 @@
         stores[q].start()
     frame = analysis(
         jnp.concatenate(grads, axis=1),
-        lat_matrix(analysis_ref, lat_part(part_ref)),
+        lat_filters(analysis_ref, part_ref),
         lon_analysis(analysis_ref),
     )
-    store_frame(frame, frame_ref, near_ref, other_ref, far_ref)
+    store_frame(frame, frame_ref, near_ref, other_ref)
     for store in stores:
         store.wait()
 
@@ -446,17 +458,18 @@
     grad_pre = split(tiled(g_ref[...]))
     product = jnp.where(same_row((256, 256)), dot3(grad_pre, field, dot_nt), 0.0)
     skip = split(jnp.sum(product.reshape(32, 8, 256), axis=1))
-    ones = jnp.ones((8, 1024), BF16)
-    bias = split(dot_nt(ones, grad_pre[0]) + dot_nt(ones, grad_pre[1]))
+    rows = split(jnp.sum(g_ref[...].reshape(32, 8, 8, 128), axis=1).reshape(256, 128))
+    ones = jnp.ones((8, 128), BF16)
+    bias = split(dot_nt(ones, rows[0]) + dot_nt(ones, rows[1]))
     sum_ref[0:192] = near_ref[...]
     sum_ref[192:224] = mix[:, :128]
     sum_ref[224:256] = mix[:, 128:] + placed(skip, 96)
     sum_ref[256:264] = placed(bias, 0)
 
 
-def pair_kernel(own_ref, near_ref, far_ref, out_ref):
+def pair_kernel(own_ref, near_ref, frame_ref, out_ref):
     out_ref[0:72] = own_ref[192:264] + near_ref[192:264]
-    out_ref[72:136] = far_ref[...]
+    out_ref[72:104] = far_rows(frame_ref)
 
 
 def result_kernel(sum_ref, coarse_ref, detail_ref, skip_ref, bias_ref, cells):
@@ -476,32 +489,32 @@
         out_ref[:, 8 * t : 8 * t + 8, :] = product[:, 128 * t : 128 * t + 128].reshape(32, 8, 128)
 
 
-def backward_kernel(
+def unmix_kernel(
     part_ref,
     shares_ref,
     first_ref,
     second_ref,
-    skip_ref,
     coarse_ref,
     detail_ref,
     subband_ref,
     synthesis_ref,
-    out_ref,
+    rows_ref,
     whole,
     scratch,
-    field,
-    done,
 ):
     whole[...] = add_edges(shares_ref, is_even(part_ref), first_ref[...], second_ref[...])
     weights = jnp.concatenate(
         [coarse_ref[s] for s in range(4)] + [detail_ref[s] for s in range(3)], axis=1
     )
     frame = mixed(whole, weights, subband_ref[...], scratch)
-    rows = synthesis_rows(frame, lon_synthesis(synthesis_ref))
-    lat = lat_matrix(synthesis_ref, lat_part(part_ref))
+    rows_ref[...] = synthesis_rows(frame, lon_synthesis(synthesis_ref))
+
+
+def field_kernel(part_ref, rows_ref, skip_ref, synthesis_ref, out_ref, field, done):
+    lat = lat_filters(synthesis_ref, part_ref)
     stores = []
     for q in range(4):
-        part = dot3(lat, split(rows[:, 256 * q : 256 * q + 256]))
+        part = dot3(lat, split(rows_ref[:, 256 * q : 256 * q + 256]))
         for g in (2 * q, 2 * q + 1):
             channels = slice(4 * g, 4 * g + 4)
             lanes = slice(128 * (g - 2 * q), 128 * (g - 2 * q) + 128)
@@ -562,7 +575,7 @@
 
 COEFS = shape_of(512, 128)
 ROWS = shape_of(192, 128)
-FAR = shape_of(64, 128)
+FAR = shape_of(32, 128)
 EDGE = shape_of(11, 16, 128)
 FIELD = shape_of(32, 64, 128)
 
@@ -584,11 +597,11 @@
     return lax.ppermute(values, "lat", [(1, 2), (2, 1)])
 
 
-def lat_sum(frame, near, other, far, far_row, part, subbands):
+def lat_sum(frame, near, other, far, far_row, part):
     return call(
         functools.partial(lat_sum_kernel, far_row=far_row),
         (COEFS, EDGE, EDGE),
-        (jnp.asarray(OWN), frame, near, other, far, subbands),
+        (jnp.asarray(OWN), frame, near, other, far),
         part,
         (0,),
     )
@@ -609,18 +622,21 @@
     analysis_table, synthesis_table = jnp.asarray(ANALYSIS), jnp.asarray(SYNTHESIS)
     subbands = jnp.asarray(SUBBANDS)
     frame, near, other, far = call(
-        analysis_kernel, (COEFS, ROWS, ROWS, FAR), (ocean_field, analysis_table), part
+        analysis_kernel,
+        (COEFS, ROWS, ROWS, FAR),
+        (ocean_field, analysis_table),
+        part,
     )
     (pre,) = call(skip_kernel, (FIELD,), (ocean_field, skip_weight, bias_vector.reshape(1, 32)))
     near = swapped(near, "lat", 1)
     other = middle(other)
     far = swapped(far, "lat", 2)
     (near, other, far), pre = lax.optimization_barrier(((near, other, far), pre))
-    shares, first, second = lat_sum(frame, near, other, far, 0, part, subbands)
+    shares, first, second = lat_sum(frame, near, other, far, 0, part)
     first, second = lon_exchange(first, second)
-    activated, grad_pre, coef, frame, near, other, far = call(
+    activated, grad_pre, coef, frame, near, other = call(
         forward_kernel,
-        (shape_of(32, 64, 128, dtype=BF16), FIELD, COEFS, COEFS, ROWS, ROWS, FAR),
+        (shape_of(32, 64, 128, dtype=BF16), FIELD, COEFS, COEFS, ROWS, ROWS),
         (
             shares,
             first,
@@ -643,29 +659,40 @@
         (ocean_field, grad_pre, coef, frame, near, subbands),
     )
     near = swapped(own, "lat", 1)
-    (pair,) = call(pair_kernel, (shape_of(136, 128),), (own, near, far))
+    (pair,) = call(pair_kernel, (shape_of(104, 128),), (own, near, frame))
     far = swapped(pair, "lat", 2)
     other = middle(after(other, pair))
     sums = pair[:72] + far[:72]
-    (skip_back,) = call(skip_back_kernel, (FIELD,), (grad_pre, skip_weight))
     steps = [swapped(sums, "lon", k) for k in (4, 12, 8)]
     near, steps[0] = lax.optimization_barrier((near, steps[0]))
-    shares, first, second = lat_sum(frame, near, other, far, 72, part, subbands)
+    shares, first, second = lat_sum(frame, near, other, far, 72, part)
+    grad_pre = after(grad_pre, first)
+    (skip_back,) = call(skip_back_kernel, (FIELD,), (grad_pre, skip_weight))
     first, second = lon_exchange(first, second)
     sums = sums + steps[0] + (steps[1] + steps[2])
-    step = swapped(sums, "lon", 16)
-    sums, first, second, skip_back = lax.optimization_barrier((sums, first, second, skip_back))
-    sums = sums + step + (swapped(sums, "lon", 48) + swapped(sums, "lon", 32))
+    steps = [swapped(sums, "lon", k) for k in (16, 48)]
+    later, second = lax.optimization_barrier((sums, second))
+    steps.append(swapped(later, "lon", 32))
+    sums = sums + steps[0] + (steps[1] + steps[2])
+    (rows,) = call(
+        unmix_kernel,
+        (shape_of(256, 1024),),
+        (shares, first, second, mix_coarse, mix_detail, subbands, synthesis_table),
+        part,
+        scratch=(FRAME, FRAME),
+    )
+    sums, rows = lax.optimization_barrier((sums, rows))
+    (grad_field,) = call(
+        field_kernel,
+        (FIELD,),
+        (rows, skip_back, synthesis_table),
+        part,
+        scratch=(pltpu.VMEM((32, 64, 128), F32), pltpu.SemaphoreType.DMA((4,))),
+        in_hbm=(0,),
+    )
     steps = [swapped(sums, "lon", k) for k in (1, 3, 2)]
     sums = sums + steps[0] + (steps[1] + steps[2])
-    (grad_field,) = call(
-        backward_kernel,
-        (FIELD,),
-        (shares, first, second, skip_back, mix_coarse, mix_detail, subbands, synthesis_table),
-        part,
-        scratch=(FRAME, FRAME, pltpu.VMEM((32, 64, 128), F32), pltpu.SemaphoreType.DMA((4,))),
-        in_hbm=(0,),
-    )
+    sums, grad_field = lax.optimization_barrier((sums, grad_field))
     cells = LAT_PARTS * LAT_BLOCK * LON_BLOCK * lax.axis_size("lon")
     coarse, detail, grad_skip, grad_bias = call(
         functools.partial(result_kernel, cells=cells),

time: 76 us -> 70 us (0.921)
  the two profiles are of different devices: /device:TPU:6 before, /device:TPU:1 now
where the time goes in v4:
time: 70 us; the launch traced here: 69.5 us
  starting transfers between devices  41 us (59%)
  waiting for transfers between devices  13.4 us (19%)
  Pallas kernels  11.3 us (16%)
  local copies, waits for them, and re-layouts  2.79 us (4%)
  between operations  0.94 us (1%)
    ppermute x15, starting transfers between devices, swapped(): return lax.ppermute(values, axis, [(i, i ^ distance) for i in range(count)])  18.8 us
    ppermute x2, starting transfers between devices, lon_exchange(): return (lax.ppermute(first, 'lon', pairs), swapped(second, 'lon', 1))  11.4 us
    ppermute x2, starting transfers between devices, middle(): return lax.ppermute(values, 'lat', [(1, 2), (2, 1)])  10.8 us
    ppermute x15, waiting for transfers between devices, swapped(): return lax.ppermute(values, axis, [(i, i ^ distance) for i in range(count)])  7.94 us
    pallas_call x6, Pallas kernels, call(): pl.pallas_call(kernel, grid_spec=grid_spec, out_shape=list(outs), compile...  7.49 us
    ppermute x2, waiting for transfers between devices, lon_exchange(): return (lax.ppermute(first, 'lon', pairs), swapped(second, 'lon', 1))  4 us
    pallas_call x5, Pallas kernels, call(): pl.pallas_call(kernel, grid=(1,), in_specs=in_specs, out_specs=out_specs,...  3.8 us
    unnamed x24, local copies, waits for them, and re-layouts  2.79 us
  transfers between devices with their start and end apart: 19, of which 8 were waited for; matrix products, arithmetic and copies ran while one was open for 0% of the time, Pallas kernels for 7%

profile of v4, /device:TPU:1, one launch (start us, length us, event | category | flops | bytes accessed | tf_op | source)
XLA Modules:
  0.0 69.5 jit_solution(15880829247281325864)
XLA Ops:
  0.6 0.0 copy-start
  0.7 1.2 %copy-done = f32[32,64,128]{2,1,0:T(8,128)S(1)} copy-done((f32[32,64,128]{2,1,0:T(8,128)S(1)}, f32[32,64,128]{2,1,0:T(8,128)}, u32[]{:S(2)}) %copy-start) | copy-done | bytes 1048600
  1.9 1.0 %copy-done.3 = bf16[1536,128]{1,0:T(8,128)(2,1)S(1)} copy-done((bf16[1536,128]{1,0:T(8,128)(2,1)S(1)}, bf16[1536,128]{1,0:T(8,128)(2,1)}, u32[]{:S(2)}) %copy-start.3) | copy-done | bytes 393240
  2.9 1.2 %shard_map.145 = (f32[512,128]{1,0:T(8,128)S(1)}, f32[192,128]{1,0:T(8,128)S(1)}, f32[192,128]{1,0:T(8,128)S(1)}, f32[32,128]{1,0:T(8,128)S(1)}) custom-call(s32[1]{0:T(128)} %bitcast.part_ref, f32[32,64,128]{2,1,0:T(8,128)S(1)} %copy-done, bf16[1536,128]{1,0:T(8,128)(2,1)S(1)} %copy-done.3), custom_call_target="tpu_custom_call" | custom-call | tf_op jit(solution)/shard_map/pallas_call | solution.py:571
  4.0 3.3 %collective-permute-start = (f32[192,128]{1,0:T(8,128)S(1)}, f32[192,128]{1,0:T(8,128)S(1)}, u32[]{:S(2)}, u32[]{:S(2)}) collective-permute-start(f32[192,128]{1,0:T(8,128)S(1)} %get-tuple-element.41), channel_id=1, source_target_pairs={{0,1},{1,0},{2,3},{3,2},{4,5},{5,4},{6,7},{7,6},{8,9},{9,8},{10,11... | collective-permute-start | bytes 294920 | tf_op jit(solution)/shard_map/ppermute | solution.py:585
  7.3 7.0 %collective-permute-start.1 = (f32[192,128]{1,0:T(8,128)S(1)}, f32[192,128]{1,0:T(8,128)S(1)}, u32[]{:S(2)}, u32[]{:S(2)}) collective-permute-start(f32[192,128]{1,0:T(8,128)S(1)} %get-tuple-element.42), channel_id=1, source_target_pairs={{1,2},{2,1},{5,6},{6,5},{9,10},{10,9},{13,14},{14,13},{17,18},{18,... | collective-permute-start | bytes 294920 | tf_op jit(solution)/shard_map/ppermute | solution.py:597
  14.3 0.0 copy-start.11
  14.3 0.1 collective-permute-start.2
  14.4 0.0 copy-done.1
  14.4 0.0 copy-done.9
  14.4 0.5 copy-done.11
  14.9 0.8 %shard_map.146.pre_ref = f32[32,64,128]{2,1,0:T(8,128)S(1)} custom-call(f32[32,64,128]{2,1,0:T(8,128)S(1)} %copy-done.1, f32[32,32]{1,0:T(8,128)S(1)} %copy-done.9, f32[1,32]{1,0:T(1,128)S(1)} %bitcast.3), custom_call_target="tpu_custom_call" | custom-call | tf_op jit(solution)/shard_map/pallas_call | solution.py:555
  15.8 0.0 copy-start.2
  15.8 5.3 %collective-permute-done.2.far_ref = f32[32,128]{1,0:T(8,128)S(1)} collective-permute-done((f32[32,128]{1,0:T(8,128)S(1)}, f32[32,128]{1,0:T(8,128)S(1)}, u32[]{:S(2)}, u32[]{:S(2)}) %collective-permute-start.2) | collective-permute-done | bytes 16416 | tf_op jit(solution)/shard_map/ppermute | solution.py:585
  21.1 0.0 collective-permute-done.near_ref
  21.1 0.0 collective-permute-done.1.other_ref
  21.1 0.0 copy-done.8
  21.1 0.0 copy-start.6
  21.1 0.0 copy-start.7
  21.1 0.3 shard_map.147
  21.4 0.0 copy-start.10
  21.4 6.3 %collective-permute-start.3 = (f32[11,16,128]{2,1,0:T(8,128)S(1)}, f32[11,16,128]{2,1,0:T(8,128)S(1)}, u32[]{:S(2)}, u32[]{:S(2)}) collective-permute-start(f32[11,16,128]{2,1,0:T(8,128)S(1)} %get-tuple-element.48), channel_id=1, source_target_pairs={{0,252},{4,8},{8,4},{12,16},{16,12},{20,24},{24,20},{28,32},{32,28... | collective-permute-start | bytes 270344 | tf_op jit(solution)/shard_map/ppermute | solution.py:613
  27.7 0.0 collective-permute-start.4
  27.7 3.3 %collective-permute-done.3.first_ref = f32[11,16,128]{2,1,0:T(8,128)S(1)} collective-permute-done((f32[11,16,128]{2,1,0:T(8,128)S(1)}, f32[11,16,128]{2,1,0:T(8,128)S(1)}, u32[]{:S(2)}, u32[]{:S(2)}) %collective-permute-start.3) | collective-permute-done | bytes 90144 | tf_op jit(solution)/shard_map/ppermute | solution.py:613
  31.0 0.1 collective-permute-done.4.second_ref
  31.1 0.0 copy-done.4
  31.1 0.0 copy-done.5
  31.1 0.0 copy-done.2
  31.1 3.1 %shard_map.148 = (bf16[32,64,128]{2,1,0:T(8,128)(2,1)}, f32[32,64,128]{2,1,0:T(8,128)S(1)}, f32[512,128]{1,0:T(8,128)S(1)}, f32[512,128]{1,0:T(8,128)S(1)}, f32[...) custom-call(s32[1]{0:T(128)} %bitcast.part_ref, f32[512,128]{1,0:T(8,128)S(1)} %get-tuple-element.47.shares_ref, ...), custom_call_target="tpu_custom_call" | custom-call | tf_op jit(solution)/shard_map/pallas_call | solution.py:571
  34.2 1.3 %shard_map.149.own_ref = f32[264,128]{1,0:T(8,128)S(1)} custom-call(f32[32,64,128]{2,1,0:T(8,128)S(1)} %copy-done.1, f32[32,64,128]{2,1,0:T(8,128)S(1)} %get-tuple-element.67.g_ref, f32[512,128]{1,0:T(8,128)S(1)} %get-tuple-element.53.coef_ref, f32[512,128]{1,0:T(8,128)S(1)} %get-tuple-element.54.frame_ref, f32[192,128]{1,0:T(8,128)S(1)} %get-tuple-element.55.near_ref, ...), custom_call_target="tpu_custom_call" | custom-call | tf_op jit(solution)/shard_map/pallas_call | solution.py:555
  35.6 0.1 collective-permute-start.5
  35.7 1.3 %collective-permute-done.5.near_ref = f32[264,128]{1,0:T(8,128)S(1)} collective-permute-done((f32[264,128]{1,0:T(8,128)S(1)}, f32[264,128]{1,0:T(8,128)S(1)}, u32[]{:S(2)}, u32[]{:S(2)}) %collective-permute-start.5) | collective-permute-done | bytes 135200 | tf_op jit(solution)/shard_map/ppermute | solution.py:585
  37.0 0.1 shard_map.150
  37.1 3.8 %collective-permute-start.6 = (f32[104,128]{1,0:T(8,128)S(1)}, f32[104,128]{1,0:T(8,128)S(1)}, u32[]{:S(2)}, u32[]{:S(2)}) collective-permute-start(f32[104,128]{1,0:T(8,128)S(1)} %shard_map.150), channel_id=1, source_target_pairs={{0,2},{1,3},{2,0},{3,1},{4,6},{5,7},{6,4},{7,5},{8,10},{9,11},{10,... | collective-permute-start | bytes 159752 | tf_op jit(solution)/shard_map/ppermute | solution.py:585
  40.9 3.8 %collective-permute-start.12 = (f32[192,128]{1,0:T(8,128)S(1)}, f32[192,128]{1,0:T(8,128)S(1)}, u32[]{:S(2)}, u32[]{:S(2)}) collective-permute-start(f32[192,128]{1,0:T(8,128)S(1)} %get-tuple-element.59), channel_id=1, source_target_pairs={{1,2},{2,1},{5,6},{6,5},{9,10},{10,9},{13,14},{14,13},{17,18},{18,... | collective-permute-start | bytes 294920 | tf_op jit(solution)/shard_map/ppermute | solution.py:597
  44.7 0.6 collective-permute-done.6.far_ref
  45.4 0.0 collective-permute-start.7
  45.4 0.1 collective-permute-start.9
  45.5 3.8 %collective-permute-start.8 = (f32[72,128]{1,0:T(8,128)S(1)}, f32[72,128]{1,0:T(8,128)S(1)}, u32[]{:S(2)}, u32[]{:S(2)}) collective-permute-start(f32[72,128]{1,0:T(8,128)S(1)} %slice_add_fusion), channel_id=1, source_target_pairs={{0,48},{4,52},{8,56},{12,60},{16,32},{20,36},{24,40},{28,44},{32,1... | collective-permute-start | bytes 110600 | tf_op jit(solution)/shard_map/ppermute | solution.py:585
  49.2 0.0 collective-permute-done.7
  49.2 1.5 %collective-permute-done.12.other_ref = f32[192,128]{1,0:T(8,128)S(1)} collective-permute-done((f32[192,128]{1,0:T(8,128)S(1)}, f32[192,128]{1,0:T(8,128)S(1)}, u32[]{:S(2)}, u32[]{:S(2)}) %collective-permute-start.12) | collective-permute-done | bytes 98336 | tf_op jit(solution)/shard_map/ppermute | solution.py:597
  50.7 0.3 shard_map.151
  51.1 0.8 %collective-permute-start.13 = (f32[11,16,128]{2,1,0:T(8,128)S(1)}, f32[11,16,128]{2,1,0:T(8,128)S(1)}, u32[]{:S(2)}, u32[]{:S(2)}) collective-permute-start(f32[11,16,128]{2,1,0:T(8,128)S(1)} %get-tuple-element.60), channel_id=1, source_target_pairs={{0,4},{4,0},{8,12},{12,8},{16,20},{20,16},{24,28},{28,24},{32,36},... | collective-permute-start | bytes 270344 | tf_op jit(solution)/shard_map/ppermute | solution.py:585
  51.9 5.2 %collective-permute-start.15 = (f32[11,16,128]{2,1,0:T(8,128)S(1)}, f32[11,16,128]{2,1,0:T(8,128)S(1)}, u32[]{:S(2)}, u32[]{:S(2)}) collective-permute-start(f32[11,16,128]{2,1,0:T(8,128)S(1)} %get-tuple-element.63), channel_id=1, source_target_pairs={{0,252},{4,8},{8,4},{12,16},{16,12},{20,24},{24,20},{28,32},{32,28... | collective-permute-start | bytes 270344 | tf_op jit(solution)/shard_map/ppermute | solution.py:613
  57.1 0.0 collective-permute-done.9
  57.1 0.0 collective-permute-done.8
  57.1 0.3 collective-permute-start.11
  57.4 0.1 collective-permute-start.10
  57.5 0.0 collective-permute-done.13.second_ref
  57.5 3.7 %collective-permute-start.14 = (f32[72,128]{1,0:T(8,128)S(1)}, f32[72,128]{1,0:T(8,128)S(1)}, u32[]{:S(2)}, u32[]{:S(2)}) collective-permute-start(f32[72,128]{1,0:T(8,128)S(1)} %add_add_fusion.2), channel_id=1, source_target_pairs={{0,128},{4,132},{8,136},{12,140},{16,144},{20,148},{24,152},{28,15... | collective-permute-start | bytes 110600 | tf_op jit(solution)/shard_map/ppermute | solution.py:585
  61.2 0.7 collective-permute-done.15.first_ref
  61.9 1.1 %shard_map.152.rows_ref = f32[256,1024]{1,0:T(8,128)S(1)} custom-call(s32[1]{0:T(128)} %bitcast.part_ref, f32[512,128]{1,0:T(8,128)S(1)} %get-tuple-element.62.shares_ref, f32[11,16,128]{2,1,0:T(8,128)S(1)} %collective-permute-done.15.first_ref, f32[11,16,128]{2,1,0:T(8,128)S(1)} %collective-permute-done.13.second_ref, f32[4,32,32]{2,1,0:T(8,128)S(1)} %copy-done.6, ...), custom_call_target="tpu_custom_call" | custom-call | tf_op jit(solution)/shard_map/pallas_call | solution.py:571
  63.1 0.6 collective-permute-done.11
  63.7 0.0 collective-permute-done.10
  63.7 0.0 collective-permute-done.14
  63.7 0.1 collective-permute-start.18
  63.8 0.1 collective-permute-start.17
  63.9 2.5 %collective-permute-start.16 = (f32[72,128]{1,0:T(8,128)S(1)}, f32[72,128]{1,0:T(8,128)S(1)}, u32[]{:S(2)}, u32[]{:S(2)}) collective-permute-start(f32[72,128]{1,0:T(8,128)S(1)} %add_add_fusion.1), channel_id=1, source_target_pairs={{0,4},{4,0},{8,12},{12,8},{16,20},{20,16},{24,28},{28,24},{32,36},... | collective-permute-start | bytes 110600 | tf_op jit(solution)/shard_map/ppermute | solution.py:585
  66.4 0.8 %shard_map.153.skip_ref = f32[32,64,128]{2,1,0:T(8,128)S(1)} custom-call(f32[32,64,128]{2,1,0:T(8,128)S(1)} %get-tuple-element.67.g_ref, f32[32,32]{1,0:T(8,128)S(1)} %copy-done.9), custom_call_target="tpu_custom_call" | custom-call | tf_op jit(solution)/shard_map/pallas_call | solution.py:555
  67.3 1.5 %shard_map.154 = f32[32,64,128]{2,1,0:T(8,128)} custom-call(s32[1]{0:T(128)} %bitcast.part_ref, f32[256,1024]{1,0:T(8,128)S(1)} %shard_map.152.rows_ref, f32[32,64,128]{2,1,0:T(8,128)S(1)} %shard_map.153.skip_ref, bf16[1536,128]{1,0:T(8,128)(2,1)S(1)} %copy-done.2), custom_call_target="tpu_custom_call" | custom-call | tf_op jit(solution)/shard_map/pallas_call | solution.py:571
  68.7 0.0 collective-permute-done.18
  68.7 0.0 collective-permute-done.17
  68.8 0.0 collective-permute-done.16
  68.8 0.7 %shard_map.155 = (f32[4,32,32]{2,1,0:T(8,128)}, f32[3,32,32]{2,1,0:T(8,128)}, f32[32,32]{1,0:T(8,128)}, f32[1,32]{1,0:T(1,128)}) custom-call(f32[72,128]{1,0:T(8,128)S(1)} %add_add_fusion.sum_ref), custom_call_target="tpu_custom_call" | custom-call | tf_op jit(solution)/shard_map/pallas_call | solution.py:555
  (13 shorter events, 0.1 us)
Async XLA Ops:
  0.6 1.2 %copy-start = (f32[32,64,128]{2,1,0:T(8,128)S(1)}, f32[32,64,128]{2,1,0:T(8,128)}, u32[]{:S(2)}) copy-start(f32[32,64,128]{2,1,0:T(8,128)} %x_ref.5) | copy-start | bytes 3145732
  1.9 1.0 %copy-start.3 = (bf16[1536,128]{1,0:T(8,128)(2,1)S(1)}, bf16[1536,128]{1,0:T(8,128)(2,1)}, u32[]{:S(2)}) copy-start(bf16[1536,128]{1,0:T(8,128)(2,1)} %constant.30.clone.table_ref.analysis_ref) | copy-start | bytes 1179652
  2.9 11.5 %copy-start.1 = (f32[32,64,128]{2,1,0:T(8,128)S(1)}, f32[32,64,128]{2,1,0:T(8,128)}, u32[]{:S(2)}) copy-start(f32[32,64,128]{2,1,0:T(8,128)} %x_ref.5) | copy-start | bytes 3145732
  2.9 11.5 %copy-start.9 = (f32[32,32]{1,0:T(8,128)S(1)}, f32[32,32]{1,0:T(8,128)}, u32[]{:S(2)}) copy-start(f32[32,32]{1,0:T(8,128)} %skip_ref.3) | copy-start | bytes 12292
  4.0 17.0 %collective-permute-start = (f32[192,128]{1,0:T(8,128)S(1)}, f32[192,128]{1,0:T(8,128)S(1)}, u32[]{:S(2)}, u32[]{:S(2)}) collective-permute-start(f32[192,128]{1,0:T(8,128)S(1)} %get-tuple-element.41), channel_id=1, source_target_pairs={{0,1},{1,0},{2,3},{3,2},{4,5},{5,4},{6,7},{7,6},{8,9},{9,8},{10,11... | collective-permute-start | bytes 294920 | tf_op jit(solution)/shard_map/ppermute | solution.py:585
  7.3 13.8 %collective-permute-start.1 = (f32[192,128]{1,0:T(8,128)S(1)}, f32[192,128]{1,0:T(8,128)S(1)}, u32[]{:S(2)}, u32[]{:S(2)}) collective-permute-start(f32[192,128]{1,0:T(8,128)S(1)} %get-tuple-element.42), channel_id=1, source_target_pairs={{1,2},{2,1},{5,6},{6,5},{9,10},{10,9},{13,14},{14,13},{17,18},{18,... | collective-permute-start | bytes 294920 | tf_op jit(solution)/shard_map/ppermute | solution.py:597
  14.3 0.7 copy-start.11
  14.3 6.8 %collective-permute-start.2 = (f32[32,128]{1,0:T(8,128)S(1)}, f32[32,128]{1,0:T(8,128)S(1)}, u32[]{:S(2)}, u32[]{:S(2)}) collective-permute-start(f32[32,128]{1,0:T(8,128)S(1)} %get-tuple-element.43), channel_id=1, source_target_pairs={{0,2},{1,3},{2,0},{3,1},{4,6},{5,7},{6,4},{7,5},{8,10},{9,11},{10,... | collective-permute-start | bytes 49160 | tf_op jit(solution)/shard_map/ppermute | solution.py:585
  14.9 6.1 %copy-start.8 = (f32[4,16,128]{2,1,0:T(8,128)S(1)}, f32[4,16,128]{2,1,0:T(8,128)}, u32[]{:S(2)}) copy-start(f32[4,16,128]{2,1,0:T(8,128)} %constant.33.clone.mask_ref) | copy-start | bytes 98308
  14.9 16.2 %copy-start.4 = (bf16[1536,128]{1,0:T(8,128)(2,1)S(1)}, bf16[1536,128]{1,0:T(8,128)(2,1)}, u32[]{:S(2)}) copy-start(bf16[1536,128]{1,0:T(8,128)(2,1)} %constant.30.clone.table_ref.analysis_ref) | copy-start | bytes 1179652
  14.9 16.2 %copy-start.5 = (bf16[32,64,128]{2,1,0:T(8,128)(2,1)S(1)}, bf16[32,64,128]{2,1,0:T(8,128)(2,1)}, u32[]{:S(2)}) copy-start(bf16[32,64,128]{2,1,0:T(8,128)(2,1)} %cot_ref.1) | copy-start | bytes 1572868
  15.8 15.3 %copy-start.2 = (bf16[1536,128]{1,0:T(8,128)(2,1)S(1)}, bf16[1536,128]{1,0:T(8,128)(2,1)}, u32[]{:S(2)}) copy-start(bf16[1536,128]{1,0:T(8,128)(2,1)} %constant.31.clone.synthesis_ref) | copy-start | bytes 1179652
  21.1 10.0 %copy-start.6 = (f32[4,32,32]{2,1,0:T(8,128)S(1)}, f32[4,32,32]{2,1,0:T(8,128)}, u32[]{:S(2)}) copy-start(f32[4,32,32]{2,1,0:T(8,128)} %coarse_ref.3) | copy-start | bytes 49156
  21.1 10.0 %copy-start.7 = (f32[3,32,32]{2,1,0:T(8,128)S(1)}, f32[3,32,32]{2,1,0:T(8,128)}, u32[]{:S(2)}) copy-start(f32[3,32,32]{2,1,0:T(8,128)} %detail_ref.3) | copy-start | bytes 36868
  21.4 9.7 %copy-start.10 = (f32[8,128]{1,0:T(8,128)S(1)}, f32[8,128]{1,0:T(8,128)}, u32[]{:S(2)}) copy-start(f32[8,128]{1,0:T(8,128)} %constant.32.clone.subband_ref) | copy-start | bytes 12292
  21.4 9.6 %collective-permute-start.3 = (f32[11,16,128]{2,1,0:T(8,128)S(1)}, f32[11,16,128]{2,1,0:T(8,128)S(1)}, u32[]{:S(2)}, u32[]{:S(2)}) collective-permute-start(f32[11,16,128]{2,1,0:T(8,128)S(1)} %get-tuple-element.48), channel_id=1, source_target_pairs={{0,252},{4,8},{8,4},{12,16},{16,12},{20,24},{24,20},{28,32},{32,28... | collective-permute-start | bytes 270344 | tf_op jit(solution)/shard_map/ppermute | solution.py:613
  27.7 3.4 %collective-permute-start.4 = (f32[11,16,128]{2,1,0:T(8,128)S(1)}, f32[11,16,128]{2,1,0:T(8,128)S(1)}, u32[]{:S(2)}, u32[]{:S(2)}) collective-permute-start(f32[11,16,128]{2,1,0:T(8,128)S(1)} %get-tuple-element.49), channel_id=1, source_target_pairs={{0,4},{4,0},{8,12},{12,8},{16,20},{20,16},{24,28},{28,24},{32,36},... | collective-permute-start | bytes 270344 | tf_op jit(solution)/shard_map/ppermute | solution.py:585
  35.6 1.4 %collective-permute-start.5 = (f32[264,128]{1,0:T(8,128)S(1)}, f32[264,128]{1,0:T(8,128)S(1)}, u32[]{:S(2)}, u32[]{:S(2)}) collective-permute-start(f32[264,128]{1,0:T(8,128)S(1)} %shard_map.149.own_ref), channel_id=1, source_target_pairs={{0,1},{1,0},{2,3},{3,2},{4,5},{5,4},{6,7},{7,6},{8,9},{9,8},{10,11... | collective-permute-start | bytes 405512 | tf_op jit(solution)/shard_map/ppermute | solution.py:585
  37.1 8.3 %collective-permute-start.6 = (f32[104,128]{1,0:T(8,128)S(1)}, f32[104,128]{1,0:T(8,128)S(1)}, u32[]{:S(2)}, u32[]{:S(2)}) collective-permute-start(f32[104,128]{1,0:T(8,128)S(1)} %shard_map.150), channel_id=1, source_target_pairs={{0,2},{1,3},{2,0},{3,1},{4,6},{5,7},{6,4},{7,5},{8,10},{9,11},{10,... | collective-permute-start | bytes 159752 | tf_op jit(solution)/shard_map/ppermute | solution.py:585
  40.9 9.8 %collective-permute-start.12 = (f32[192,128]{1,0:T(8,128)S(1)}, f32[192,128]{1,0:T(8,128)S(1)}, u32[]{:S(2)}, u32[]{:S(2)}) collective-permute-start(f32[192,128]{1,0:T(8,128)S(1)} %get-tuple-element.59), channel_id=1, source_target_pairs={{1,2},{2,1},{5,6},{6,5},{9,10},{10,9},{13,14},{14,13},{17,18},{18,... | collective-permute-start | bytes 294920 | tf_op jit(solution)/shard_map/ppermute | solution.py:597
  45.4 3.9 %collective-permute-start.7 = (f32[72,128]{1,0:T(8,128)S(1)}, f32[72,128]{1,0:T(8,128)S(1)}, u32[]{:S(2)}, u32[]{:S(2)}) collective-permute-start(f32[72,128]{1,0:T(8,128)S(1)} %slice_add_fusion), channel_id=1, source_target_pairs={{0,16},{4,20},{8,24},{12,28},{16,0},{20,4},{24,8},{28,12},{32,48},... | collective-permute-start | bytes 110600 | tf_op jit(solution)/shard_map/ppermute | solution.py:585
  45.4 11.7 %collective-permute-start.9 = (f32[72,128]{1,0:T(8,128)S(1)}, f32[72,128]{1,0:T(8,128)S(1)}, u32[]{:S(2)}, u32[]{:S(2)}) collective-permute-start(f32[72,128]{1,0:T(8,128)S(1)} %slice_add_fusion), channel_id=1, source_target_pairs={{0,32},{4,36},{8,40},{12,44},{16,48},{20,52},{24,56},{28,60},{32,0... | collective-permute-start | bytes 110600 | tf_op jit(solution)/shard_map/ppermute | solution.py:585
  45.5 11.6 %collective-permute-start.8 = (f32[72,128]{1,0:T(8,128)S(1)}, f32[72,128]{1,0:T(8,128)S(1)}, u32[]{:S(2)}, u32[]{:S(2)}) collective-permute-start(f32[72,128]{1,0:T(8,128)S(1)} %slice_add_fusion), channel_id=1, source_target_pairs={{0,48},{4,52},{8,56},{12,60},{16,32},{20,36},{24,40},{28,44},{32,1... | collective-permute-start | bytes 110600 | tf_op jit(solution)/shard_map/ppermute | solution.py:585
  51.1 6.4 %collective-permute-start.13 = (f32[11,16,128]{2,1,0:T(8,128)S(1)}, f32[11,16,128]{2,1,0:T(8,128)S(1)}, u32[]{:S(2)}, u32[]{:S(2)}) collective-permute-start(f32[11,16,128]{2,1,0:T(8,128)S(1)} %get-tuple-element.60), channel_id=1, source_target_pairs={{0,4},{4,0},{8,12},{12,8},{16,20},{20,16},{24,28},{28,24},{32,36},... | collective-permute-start | bytes 270344 | tf_op jit(solution)/shard_map/ppermute | solution.py:585
  51.9 10.0 %collective-permute-start.15 = (f32[11,16,128]{2,1,0:T(8,128)S(1)}, f32[11,16,128]{2,1,0:T(8,128)S(1)}, u32[]{:S(2)}, u32[]{:S(2)}) collective-permute-start(f32[11,16,128]{2,1,0:T(8,128)S(1)} %get-tuple-element.63), channel_id=1, source_target_pairs={{0,252},{4,8},{8,4},{12,16},{16,12},{20,24},{24,20},{28,32},{32,28... | collective-permute-start | bytes 270344 | tf_op jit(solution)/shard_map/ppermute | solution.py:613
  57.1 6.6 %collective-permute-start.11 = (f32[72,128]{1,0:T(8,128)S(1)}, f32[72,128]{1,0:T(8,128)S(1)}, u32[]{:S(2)}, u32[]{:S(2)}) collective-permute-start(f32[72,128]{1,0:T(8,128)S(1)} %add_add_fusion.2), channel_id=1, source_target_pairs={{0,192},{4,196},{8,200},{12,204},{16,208},{20,212},{24,216},{28,22... | collective-permute-start | bytes 110600 | tf_op jit(solution)/shard_map/ppermute | solution.py:585
  57.4 6.3 %collective-permute-start.10 = (f32[72,128]{1,0:T(8,128)S(1)}, f32[72,128]{1,0:T(8,128)S(1)}, u32[]{:S(2)}, u32[]{:S(2)}) collective-permute-start(f32[72,128]{1,0:T(8,128)S(1)} %add_add_fusion.2), channel_id=1, source_target_pairs={{0,64},{4,68},{8,72},{12,76},{16,80},{20,84},{24,88},{28,92},{32,9... | collective-permute-start | bytes 110600 | tf_op jit(solution)/shard_map/ppermute | solution.py:585
  57.5 6.2 %collective-permute-start.14 = (f32[72,128]{1,0:T(8,128)S(1)}, f32[72,128]{1,0:T(8,128)S(1)}, u32[]{:S(2)}, u32[]{:S(2)}) collective-permute-start(f32[72,128]{1,0:T(8,128)S(1)} %add_add_fusion.2), channel_id=1, source_target_pairs={{0,128},{4,132},{8,136},{12,140},{16,144},{20,148},{24,152},{28,15... | collective-permute-start | bytes 110600 | tf_op jit(solution)/shard_map/ppermute | solution.py:585
  63.7 5.0 %collective-permute-start.18 = (f32[72,128]{1,0:T(8,128)S(1)}, f32[72,128]{1,0:T(8,128)S(1)}, u32[]{:S(2)}, u32[]{:S(2)}) collective-permute-start(f32[72,128]{1,0:T(8,128)S(1)} %add_add_fusion.1), channel_id=1, source_target_pairs={{0,8},{4,12},{8,0},{12,4},{16,24},{20,28},{24,16},{28,20},{32,40},... | collective-permute-start | bytes 110600 | tf_op jit(solution)/shard_map/ppermute | solution.py:585
  63.8 4.9 %collective-permute-start.17 = (f32[72,128]{1,0:T(8,128)S(1)}, f32[72,128]{1,0:T(8,128)S(1)}, u32[]{:S(2)}, u32[]{:S(2)}) collective-permute-start(f32[72,128]{1,0:T(8,128)S(1)} %add_add_fusion.1), channel_id=1, source_target_pairs={{0,12},{4,8},{8,4},{12,0},{16,28},{20,24},{24,20},{28,16},{32,44},... | collective-permute-start | bytes 110600 | tf_op jit(solution)/shard_map/ppermute | solution.py:585
  63.9 4.9 %collective-permute-start.16 = (f32[72,128]{1,0:T(8,128)S(1)}, f32[72,128]{1,0:T(8,128)S(1)}, u32[]{:S(2)}, u32[]{:S(2)}) collective-permute-start(f32[72,128]{1,0:T(8,128)S(1)} %add_add_fusion.1), channel_id=1, source_target_pairs={{0,4},{4,0},{8,12},{12,8},{16,20},{20,16},{24,28},{28,24},{32,36},... | collective-permute-start | bytes 110600 | tf_op jit(solution)/shard_map/ppermute | solution.py:585

commit v5 on v4

--- a/solution.py
+++ b/solution.py
@@ -593,6 +593,15 @@
     )
 
 
+def across(values):
+    pairs = []
+    for lon in range(lax.axis_size("lon")):
+        for lat in range(LAT_PARTS):
+            other = lat ^ 2 if lon % 4 in (0, 3) else lat
+            pairs.append((LAT_PARTS * lon + lat, LAT_PARTS * (lon ^ 3) + other))
+    return lax.ppermute(values, ("lon", "lat"), pairs)
+
+
 def middle(values):
     return lax.ppermute(values, "lat", [(1, 2), (2, 1)])
 
@@ -658,16 +667,15 @@
         (shape_of(264, 128),),
         (ocean_field, grad_pre, coef, frame, near, subbands),
     )
+    (skip_back,) = call(skip_back_kernel, (FIELD,), (grad_pre, skip_weight))
     near = swapped(own, "lat", 1)
+    near, skip_back = lax.optimization_barrier((near, skip_back))
     (pair,) = call(pair_kernel, (shape_of(104, 128),), (own, near, frame))
     far = swapped(pair, "lat", 2)
     other = middle(after(other, pair))
     sums = pair[:72] + far[:72]
     steps = [swapped(sums, "lon", k) for k in (4, 12, 8)]
-    near, steps[0] = lax.optimization_barrier((near, steps[0]))
     shares, first, second = lat_sum(frame, near, other, far, 72, part)
-    grad_pre = after(grad_pre, first)
-    (skip_back,) = call(skip_back_kernel, (FIELD,), (grad_pre, skip_weight))
     first, second = lon_exchange(first, second)
     sums = sums + steps[0] + (steps[1] + steps[2])
     steps = [swapped(sums, "lon", k) for k in (16, 48)]
@@ -690,7 +698,7 @@
         scratch=(pltpu.VMEM((32, 64, 128), F32), pltpu.SemaphoreType.DMA((4,))),
         in_hbm=(0,),
     )
-    steps = [swapped(sums, "lon", k) for k in (1, 3, 2)]
+    steps = [swapped(sums, "lon", 1), across(sums), swapped(sums, "lon", 2)]
     sums = sums + steps[0] + (steps[1] + steps[2])
     sums, grad_field = lax.optimization_barrier((sums, grad_field))
     cells = LAT_PARTS * LAT_BLOCK * LON_BLOCK * lax.axis_size("lon")

time: 70 us -> 69.1 us (0.987)
  starting transfers between devices: 41 us -> 39.8 us
    ppermute x15 -> x14, starting transfers between devices: 18.8 us -> 17.3 us  [swapped(): return lax.ppermute(values, axis, [(i, i ^ distance) for i in range(count)])]
    ppermute x2, waiting for transfers between devices: 1.51 us -> 2.73 us  [middle(): return lax.ppermute(values, 'lat', [(1, 2), (2, 1)])]
    ppermute x15 -> x14, waiting for transfers between devices: 7.94 us -> 6.98 us  [swapped(): return lax.ppermute(values, axis, [(i, i ^ distance) for i in range(count)])]
where the time goes in v5:
time: 69.1 us; the launch traced here: 68.6 us
  starting transfers between devices  39.8 us (58%)
  waiting for transfers between devices  13.6 us (20%)
  Pallas kernels  11.3 us (16%)
  local copies, waits for them, and re-layouts  2.79 us (4%)
  between operations  0.96 us (1%)
    ppermute x14, starting transfers between devices, swapped(): return lax.ppermute(values, axis, [(i, i ^ distance) for i in range(count)])  17.3 us
    ppermute x2, starting transfers between devices, lon_exchange(): return (lax.ppermute(first, 'lon', pairs), swapped(second, 'lon', 1))  11.6 us
    ppermute x2, starting transfers between devices, middle(): return lax.ppermute(values, 'lat', [(1, 2), (2, 1)])  10.8 us
    pallas_call x6, Pallas kernels, call(): pl.pallas_call(kernel, grid_spec=grid_spec, out_shape=list(outs), compile...  7.48 us
    ppermute x14, waiting for transfers between devices, swapped(): return lax.ppermute(values, axis, [(i, i ^ distance) for i in range(count)])  6.98 us
    ppermute x2, waiting for transfers between devices, lon_exchange(): return (lax.ppermute(first, 'lon', pairs), swapped(second, 'lon', 1))  3.92 us
    pallas_call x5, Pallas kernels, call(): pl.pallas_call(kernel, grid=(1,), in_specs=in_specs, out_specs=out_specs,...  3.84 us
    unnamed x24, local copies, waits for them, and re-layouts  2.79 us
  transfers between devices with their start and end apart: 19, of which 8 were waited for; matrix products, arithmetic and copies ran while one was open for 0% of the time, Pallas kernels for 7%

profile of v5, /device:TPU:1, one launch (start us, length us, event | category | flops | bytes accessed | tf_op | source)
XLA Modules:
  0.0 68.6 jit_solution(3233541403353078014)
XLA Ops:
  0.6 0.0 copy-start
  0.7 1.2 %copy-done = f32[32,64,128]{2,1,0:T(8,128)S(1)} copy-done((f32[32,64,128]{2,1,0:T(8,128)S(1)}, f32[32,64,128]{2,1,0:T(8,128)}, u32[]{:S(2)}) %copy-start) | copy-done | bytes 1048600
  1.9 1.0 %copy-done.3 = bf16[1536,128]{1,0:T(8,128)(2,1)S(1)} copy-done((bf16[1536,128]{1,0:T(8,128)(2,1)S(1)}, bf16[1536,128]{1,0:T(8,128)(2,1)}, u32[]{:S(2)}) %copy-start.3) | copy-done | bytes 393240
  2.9 1.2 %shard_map.145 = (f32[512,128]{1,0:T(8,128)S(1)}, f32[192,128]{1,0:T(8,128)S(1)}, f32[192,128]{1,0:T(8,128)S(1)}, f32[32,128]{1,0:T(8,128)S(1)}) custom-call(s32[1]{0:T(128)} %bitcast.part_ref, f32[32,64,128]{2,1,0:T(8,128)S(1)} %copy-done, bf16[1536,128]{1,0:T(8,128)(2,1)S(1)} %copy-done.3), custom_call_target="tpu_custom_call" | custom-call | tf_op jit(solution)/shard_map/pallas_call | solution.py:571
  4.0 3.3 %collective-permute-start = (f32[192,128]{1,0:T(8,128)S(1)}, f32[192,128]{1,0:T(8,128)S(1)}, u32[]{:S(2)}, u32[]{:S(2)}) collective-permute-start(f32[192,128]{1,0:T(8,128)S(1)} %get-tuple-element.40), channel_id=1, source_target_pairs={{0,1},{1,0},{2,3},{3,2},{4,5},{5,4},{6,7},{7,6},{8,9},{9,8},{10,11... | collective-permute-start | bytes 294920 | tf_op jit(solution)/shard_map/ppermute | solution.py:585
  7.3 7.0 %collective-permute-start.1 = (f32[192,128]{1,0:T(8,128)S(1)}, f32[192,128]{1,0:T(8,128)S(1)}, u32[]{:S(2)}, u32[]{:S(2)}) collective-permute-start(f32[192,128]{1,0:T(8,128)S(1)} %get-tuple-element.41), channel_id=1, source_target_pairs={{1,2},{2,1},{5,6},{6,5},{9,10},{10,9},{13,14},{14,13},{17,18},{18,... | collective-permute-start | bytes 294920 | tf_op jit(solution)/shard_map/ppermute | solution.py:606
  14.3 0.0 copy-start.11
  14.3 0.1 collective-permute-start.2
  14.4 0.0 copy-done.1
  14.4 0.0 copy-done.9
  14.4 0.5 copy-done.11
  14.9 0.8 %shard_map.146.pre_ref = f32[32,64,128]{2,1,0:T(8,128)S(1)} custom-call(f32[32,64,128]{2,1,0:T(8,128)S(1)} %copy-done.1, f32[32,32]{1,0:T(8,128)S(1)} %copy-done.9, f32[1,32]{1,0:T(1,128)S(1)} %bitcast.3), custom_call_target="tpu_custom_call" | custom-call | tf_op jit(solution)/shard_map/pallas_call | solution.py:555
  15.8 0.0 copy-start.2
  15.8 5.3 %collective-permute-done.2.far_ref = f32[32,128]{1,0:T(8,128)S(1)} collective-permute-done((f32[32,128]{1,0:T(8,128)S(1)}, f32[32,128]{1,0:T(8,128)S(1)}, u32[]{:S(2)}, u32[]{:S(2)}) %collective-permute-start.2) | collective-permute-done | bytes 16416 | tf_op jit(solution)/shard_map/ppermute | solution.py:585
  21.1 0.0 collective-permute-done.near_ref
  21.1 0.0 collective-permute-done.1.other_ref
  21.1 0.0 copy-done.8
  21.1 0.0 copy-start.6
  21.1 0.0 copy-start.7
  21.1 0.3 shard_map.147
  21.4 0.0 copy-start.10
  21.4 6.3 %collective-permute-start.3 = (f32[11,16,128]{2,1,0:T(8,128)S(1)}, f32[11,16,128]{2,1,0:T(8,128)S(1)}, u32[]{:S(2)}, u32[]{:S(2)}) collective-permute-start(f32[11,16,128]{2,1,0:T(8,128)S(1)} %get-tuple-element.47), channel_id=1, source_target_pairs={{0,252},{4,8},{8,4},{12,16},{16,12},{20,24},{24,20},{28,32},{32,28... | collective-permute-start | bytes 270344 | tf_op jit(solution)/shard_map/ppermute | solution.py:622
  27.7 0.0 collective-permute-start.4
  27.7 3.3 %collective-permute-done.3.first_ref = f32[11,16,128]{2,1,0:T(8,128)S(1)} collective-permute-done((f32[11,16,128]{2,1,0:T(8,128)S(1)}, f32[11,16,128]{2,1,0:T(8,128)S(1)}, u32[]{:S(2)}, u32[]{:S(2)}) %collective-permute-start.3) | collective-permute-done | bytes 90144 | tf_op jit(solution)/shard_map/ppermute | solution.py:622
  31.0 0.1 collective-permute-done.4.second_ref
  31.1 0.0 copy-done.4
  31.1 0.0 copy-done.5
  31.1 0.0 copy-done.2
  31.1 3.1 %shard_map.148 = (bf16[32,64,128]{2,1,0:T(8,128)(2,1)}, f32[32,64,128]{2,1,0:T(8,128)S(1)}, f32[512,128]{1,0:T(8,128)S(1)}, f32[512,128]{1,0:T(8,128)S(1)}, f32[...) custom-call(s32[1]{0:T(128)} %bitcast.part_ref, f32[512,128]{1,0:T(8,128)S(1)} %get-tuple-element.46.shares_ref, ...), custom_call_target="tpu_custom_call" | custom-call | tf_op jit(solution)/shard_map/pallas_call | solution.py:571
  34.2 1.3 %shard_map.149.own_ref = f32[264,128]{1,0:T(8,128)S(1)} custom-call(f32[32,64,128]{2,1,0:T(8,128)S(1)} %copy-done.1, f32[32,64,128]{2,1,0:T(8,128)S(1)} %get-tuple-element.51.g_ref, f32[512,128]{1,0:T(8,128)S(1)} %get-tuple-element.52.coef_ref, f32[512,128]{1,0:T(8,128)S(1)} %get-tuple-element.53.frame_ref, f32[192,128]{1,0:T(8,128)S(1)} %get-tuple-element.54.near_ref, ...), custom_call_target="tpu_custom_call" | custom-call | tf_op jit(solution)/shard_map/pallas_call | solution.py:555
  35.6 0.1 collective-permute-start.5
  35.7 0.8 %shard_map.150.skip_ref = f32[32,64,128]{2,1,0:T(8,128)S(1)} custom-call(f32[32,64,128]{2,1,0:T(8,128)S(1)} %get-tuple-element.51.g_ref, f32[32,32]{1,0:T(8,128)S(1)} %copy-done.9), custom_call_target="tpu_custom_call" | custom-call | tf_op jit(solution)/shard_map/pallas_call | solution.py:555
  36.5 0.5 collective-permute-done.5.near_ref
  37.0 0.1 shard_map.151
  37.1 3.8 %collective-permute-start.6 = (f32[104,128]{1,0:T(8,128)S(1)}, f32[104,128]{1,0:T(8,128)S(1)}, u32[]{:S(2)}, u32[]{:S(2)}) collective-permute-start(f32[104,128]{1,0:T(8,128)S(1)} %shard_map.151), channel_id=1, source_target_pairs={{0,2},{1,3},{2,0},{3,1},{4,6},{5,7},{6,4},{7,5},{8,10},{9,11},{10,... | collective-permute-start | bytes 159752 | tf_op jit(solution)/shard_map/ppermute | solution.py:585
  40.9 3.8 %collective-permute-start.12 = (f32[192,128]{1,0:T(8,128)S(1)}, f32[192,128]{1,0:T(8,128)S(1)}, u32[]{:S(2)}, u32[]{:S(2)}) collective-permute-start(f32[192,128]{1,0:T(8,128)S(1)} %get-tuple-element.57), channel_id=1, source_target_pairs={{1,2},{2,1},{5,6},{6,5},{9,10},{10,9},{13,14},{14,13},{17,18},{18,... | collective-permute-start | bytes 294920 | tf_op jit(solution)/shard_map/ppermute | solution.py:606
  44.8 0.6 collective-permute-done.6.far_ref
  45.4 0.0 collective-permute-start.9
  45.4 0.1 collective-permute-start.8
  45.5 2.5 %collective-permute-start.7 = (f32[72,128]{1,0:T(8,128)S(1)}, f32[72,128]{1,0:T(8,128)S(1)}, u32[]{:S(2)}, u32[]{:S(2)}) collective-permute-start(f32[72,128]{1,0:T(8,128)S(1)} %slice_add_fusion), channel_id=1, source_target_pairs={{0,16},{4,20},{8,24},{12,28},{16,0},{20,4},{24,8},{28,12},{32,48},... | collective-permute-start | bytes 110600 | tf_op jit(solution)/shard_map/ppermute | solution.py:585
  48.0 2.7 %collective-permute-done.12.other_ref = f32[192,128]{1,0:T(8,128)S(1)} collective-permute-done((f32[192,128]{1,0:T(8,128)S(1)}, f32[192,128]{1,0:T(8,128)S(1)}, u32[]{:S(2)}, u32[]{:S(2)}) %collective-permute-start.12) | collective-permute-done | bytes 98336 | tf_op jit(solution)/shard_map/ppermute | solution.py:606
  50.8 0.3 shard_map.152
  51.1 0.8 %collective-permute-start.13 = (f32[11,16,128]{2,1,0:T(8,128)S(1)}, f32[11,16,128]{2,1,0:T(8,128)S(1)}, u32[]{:S(2)}, u32[]{:S(2)}) collective-permute-start(f32[11,16,128]{2,1,0:T(8,128)S(1)} %get-tuple-element.58), channel_id=1, source_target_pairs={{0,4},{4,0},{8,12},{12,8},{16,20},{20,16},{24,28},{28,24},{32,36},... | collective-permute-start | bytes 270344 | tf_op jit(solution)/shard_map/ppermute | solution.py:585
  51.9 5.3 %collective-permute-start.15 = (f32[11,16,128]{2,1,0:T(8,128)S(1)}, f32[11,16,128]{2,1,0:T(8,128)S(1)}, u32[]{:S(2)}, u32[]{:S(2)}) collective-permute-start(f32[11,16,128]{2,1,0:T(8,128)S(1)} %get-tuple-element.61), channel_id=1, source_target_pairs={{0,252},{4,8},{8,4},{12,16},{16,12},{20,24},{24,20},{28,32},{32,28... | collective-permute-start | bytes 270344 | tf_op jit(solution)/shard_map/ppermute | solution.py:622
  57.3 0.0 collective-permute-done.9
  57.3 0.0 collective-permute-done.8
  57.3 0.0 collective-permute-done.7
  57.3 0.1 collective-permute-start.11
  57.4 0.1 collective-permute-start.10
  57.5 0.0 collective-permute-done.13.second_ref
  57.5 3.7 %collective-permute-start.14 = (f32[72,128]{1,0:T(8,128)S(1)}, f32[72,128]{1,0:T(8,128)S(1)}, u32[]{:S(2)}, u32[]{:S(2)}) collective-permute-start(f32[72,128]{1,0:T(8,128)S(1)} %add_add_fusion.2), channel_id=1, source_target_pairs={{0,128},{4,132},{8,136},{12,140},{16,144},{20,148},{24,152},{28,15... | collective-permute-start | bytes 110600 | tf_op jit(solution)/shard_map/ppermute | solution.py:585
  61.3 0.6 collective-permute-done.15.first_ref
  61.9 1.1 %shard_map.153.rows_ref = f32[256,1024]{1,0:T(8,128)S(1)} custom-call(s32[1]{0:T(128)} %bitcast.part_ref, f32[512,128]{1,0:T(8,128)S(1)} %get-tuple-element.60.shares_ref, f32[11,16,128]{2,1,0:T(8,128)S(1)} %collective-permute-done.15.first_ref, f32[11,16,128]{2,1,0:T(8,128)S(1)} %collective-permute-done.13.second_ref, f32[4,32,32]{2,1,0:T(8,128)S(1)} %copy-done.6, ...), custom_call_target="tpu_custom_call" | custom-call | tf_op jit(solution)/shard_map/pallas_call | solution.py:571
  63.0 0.0 collective-permute-done.11
  63.0 0.0 collective-permute-done.10
  63.1 0.5 collective-permute-done.14
  63.6 0.1 collective-permute-start.18
  63.7 0.1 collective-permute-start.17
  63.8 2.5 %collective-permute-start.16 = (f32[72,128]{1,0:T(8,128)S(1)}, f32[72,128]{1,0:T(8,128)S(1)}, u32[]{:S(2)}, u32[]{:S(2)}) collective-permute-start(f32[72,128]{1,0:T(8,128)S(1)} %add_add_fusion.1), channel_id=1, source_target_pairs={{0,4},{4,0},{8,12},{12,8},{16,20},{20,16},{24,28},{28,24},{32,36},... | collective-permute-start | bytes 110600 | tf_op jit(solution)/shard_map/ppermute | solution.py:585
  66.3 1.5 %shard_map.154 = f32[32,64,128]{2,1,0:T(8,128)} custom-call(s32[1]{0:T(128)} %bitcast.part_ref, f32[256,1024]{1,0:T(8,128)S(1)} %shard_map.153.rows_ref, f32[32,64,128]{2,1,0:T(8,128)S(1)} %shard_map.150.skip_ref, bf16[1536,128]{1,0:T(8,128)(2,1)S(1)} %copy-done.2), custom_call_target="tpu_custom_call" | custom-call | tf_op jit(solution)/shard_map/pallas_call | solution.py:571
  67.8 0.0 collective-permute-done.18
  67.8 0.0 collective-permute-done.17
  67.8 0.0 collective-permute-done.16
  67.8 0.7 %shard_map.155 = (f32[4,32,32]{2,1,0:T(8,128)}, f32[3,32,32]{2,1,0:T(8,128)}, f32[32,32]{1,0:T(8,128)}, f32[1,32]{1,0:T(1,128)}) custom-call(f32[72,128]{1,0:T(8,128)S(1)} %add_add_fusion.sum_ref), custom_call_target="tpu_custom_call" | custom-call | tf_op jit(solution)/shard_map/pallas_call | solution.py:555
  (13 shorter events, 0.1 us)
Async XLA Ops:
  0.6 1.2 %copy-start = (f32[32,64,128]{2,1,0:T(8,128)S(1)}, f32[32,64,128]{2,1,0:T(8,128)}, u32[]{:S(2)}) copy-start(f32[32,64,128]{2,1,0:T(8,128)} %x_ref.5) | copy-start | bytes 3145732
  1.9 1.0 %copy-start.3 = (bf16[1536,128]{1,0:T(8,128)(2,1)S(1)}, bf16[1536,128]{1,0:T(8,128)(2,1)}, u32[]{:S(2)}) copy-start(bf16[1536,128]{1,0:T(8,128)(2,1)} %constant.30.clone.table_ref.analysis_ref) | copy-start | bytes 1179652
  2.9 11.5 %copy-start.1 = (f32[32,64,128]{2,1,0:T(8,128)S(1)}, f32[32,64,128]{2,1,0:T(8,128)}, u32[]{:S(2)}) copy-start(f32[32,64,128]{2,1,0:T(8,128)} %x_ref.5) | copy-start | bytes 3145732
  2.9 11.5 %copy-start.9 = (f32[32,32]{1,0:T(8,128)S(1)}, f32[32,32]{1,0:T(8,128)}, u32[]{:S(2)}) copy-start(f32[32,32]{1,0:T(8,128)} %skip_ref.3) | copy-start | bytes 12292
  4.0 17.0 %collective-permute-start = (f32[192,128]{1,0:T(8,128)S(1)}, f32[192,128]{1,0:T(8,128)S(1)}, u32[]{:S(2)}, u32[]{:S(2)}) collective-permute-start(f32[192,128]{1,0:T(8,128)S(1)} %get-tuple-element.40), channel_id=1, source_target_pairs={{0,1},{1,0},{2,3},{3,2},{4,5},{5,4},{6,7},{7,6},{8,9},{9,8},{10,11... | collective-permute-start | bytes 294920 | tf_op jit(solution)/shard_map/ppermute | solution.py:585
  7.3 13.8 %collective-permute-start.1 = (f32[192,128]{1,0:T(8,128)S(1)}, f32[192,128]{1,0:T(8,128)S(1)}, u32[]{:S(2)}, u32[]{:S(2)}) collective-permute-start(f32[192,128]{1,0:T(8,128)S(1)} %get-tuple-element.41), channel_id=1, source_target_pairs={{1,2},{2,1},{5,6},{6,5},{9,10},{10,9},{13,14},{14,13},{17,18},{18,... | collective-permute-start | bytes 294920 | tf_op jit(solution)/shard_map/ppermute | solution.py:606
  14.3 0.7 copy-start.11
  14.3 6.8 %collective-permute-start.2 = (f32[32,128]{1,0:T(8,128)S(1)}, f32[32,128]{1,0:T(8,128)S(1)}, u32[]{:S(2)}, u32[]{:S(2)}) collective-permute-start(f32[32,128]{1,0:T(8,128)S(1)} %get-tuple-element.42), channel_id=1, source_target_pairs={{0,2},{1,3},{2,0},{3,1},{4,6},{5,7},{6,4},{7,5},{8,10},{9,11},{10,... | collective-permute-start | bytes 49160 | tf_op jit(solution)/shard_map/ppermute | solution.py:585
  14.9 6.1 %copy-start.8 = (f32[4,16,128]{2,1,0:T(8,128)S(1)}, f32[4,16,128]{2,1,0:T(8,128)}, u32[]{:S(2)}) copy-start(f32[4,16,128]{2,1,0:T(8,128)} %constant.33.clone.mask_ref) | copy-start | bytes 98308
  14.9 16.2 %copy-start.4 = (bf16[1536,128]{1,0:T(8,128)(2,1)S(1)}, bf16[1536,128]{1,0:T(8,128)(2,1)}, u32[]{:S(2)}) copy-start(bf16[1536,128]{1,0:T(8,128)(2,1)} %constant.30.clone.table_ref.analysis_ref) | copy-start | bytes 1179652
  14.9 16.2 %copy-start.5 = (bf16[32,64,128]{2,1,0:T(8,128)(2,1)S(1)}, bf16[32,64,128]{2,1,0:T(8,128)(2,1)}, u32[]{:S(2)}) copy-start(bf16[32,64,128]{2,1,0:T(8,128)(2,1)} %cot_ref.1) | copy-start | bytes 1572868
  15.8 15.3 %copy-start.2 = (bf16[1536,128]{1,0:T(8,128)(2,1)S(1)}, bf16[1536,128]{1,0:T(8,128)(2,1)}, u32[]{:S(2)}) copy-start(bf16[1536,128]{1,0:T(8,128)(2,1)} %constant.31.clone.synthesis_ref) | copy-start | bytes 1179652
  21.1 10.1 %copy-start.6 = (f32[4,32,32]{2,1,0:T(8,128)S(1)}, f32[4,32,32]{2,1,0:T(8,128)}, u32[]{:S(2)}) copy-start(f32[4,32,32]{2,1,0:T(8,128)} %coarse_ref.3) | copy-start | bytes 49156
  21.1 10.0 %copy-start.7 = (f32[3,32,32]{2,1,0:T(8,128)S(1)}, f32[3,32,32]{2,1,0:T(8,128)}, u32[]{:S(2)}) copy-start(f32[3,32,32]{2,1,0:T(8,128)} %detail_ref.3) | copy-start | bytes 36868
  21.4 9.7 %copy-start.10 = (f32[8,128]{1,0:T(8,128)S(1)}, f32[8,128]{1,0:T(8,128)}, u32[]{:S(2)}) copy-start(f32[8,128]{1,0:T(8,128)} %constant.32.clone.subband_ref) | copy-start | bytes 12292
  21.4 9.6 %collective-permute-start.3 = (f32[11,16,128]{2,1,0:T(8,128)S(1)}, f32[11,16,128]{2,1,0:T(8,128)S(1)}, u32[]{:S(2)}, u32[]{:S(2)}) collective-permute-start(f32[11,16,128]{2,1,0:T(8,128)S(1)} %get-tuple-element.47), channel_id=1, source_target_pairs={{0,252},{4,8},{8,4},{12,16},{16,12},{20,24},{24,20},{28,32},{32,28... | collective-permute-start | bytes 270344 | tf_op jit(solution)/shard_map/ppermute | solution.py:622
  27.7 3.4 %collective-permute-start.4 = (f32[11,16,128]{2,1,0:T(8,128)S(1)}, f32[11,16,128]{2,1,0:T(8,128)S(1)}, u32[]{:S(2)}, u32[]{:S(2)}) collective-permute-start(f32[11,16,128]{2,1,0:T(8,128)S(1)} %get-tuple-element.48), channel_id=1, source_target_pairs={{0,4},{4,0},{8,12},{12,8},{16,20},{20,16},{24,28},{28,24},{32,36},... | collective-permute-start | bytes 270344 | tf_op jit(solution)/shard_map/ppermute | solution.py:585
  35.6 1.4 %collective-permute-start.5 = (f32[264,128]{1,0:T(8,128)S(1)}, f32[264,128]{1,0:T(8,128)S(1)}, u32[]{:S(2)}, u32[]{:S(2)}) collective-permute-start(f32[264,128]{1,0:T(8,128)S(1)} %shard_map.149.own_ref), channel_id=1, source_target_pairs={{0,1},{1,0},{2,3},{3,2},{4,5},{5,4},{6,7},{7,6},{8,9},{9,8},{10,11... | collective-permute-start | bytes 405512 | tf_op jit(solution)/shard_map/ppermute | solution.py:585
  37.1 8.3 %collective-permute-start.6 = (f32[104,128]{1,0:T(8,128)S(1)}, f32[104,128]{1,0:T(8,128)S(1)}, u32[]{:S(2)}, u32[]{:S(2)}) collective-permute-start(f32[104,128]{1,0:T(8,128)S(1)} %shard_map.151), channel_id=1, source_target_pairs={{0,2},{1,3},{2,0},{3,1},{4,6},{5,7},{6,4},{7,5},{8,10},{9,11},{10,... | collective-permute-start | bytes 159752 | tf_op jit(solution)/shard_map/ppermute | solution.py:585
  40.9 9.8 %collective-permute-start.12 = (f32[192,128]{1,0:T(8,128)S(1)}, f32[192,128]{1,0:T(8,128)S(1)}, u32[]{:S(2)}, u32[]{:S(2)}) collective-permute-start(f32[192,128]{1,0:T(8,128)S(1)} %get-tuple-element.57), channel_id=1, source_target_pairs={{1,2},{2,1},{5,6},{6,5},{9,10},{10,9},{13,14},{14,13},{17,18},{18,... | collective-permute-start | bytes 294920 | tf_op jit(solution)/shard_map/ppermute | solution.py:606
  45.4 11.9 %collective-permute-start.9 = (f32[72,128]{1,0:T(8,128)S(1)}, f32[72,128]{1,0:T(8,128)S(1)}, u32[]{:S(2)}, u32[]{:S(2)}) collective-permute-start(f32[72,128]{1,0:T(8,128)S(1)} %slice_add_fusion), channel_id=1, source_target_pairs={{0,32},{4,36},{8,40},{12,44},{16,48},{20,52},{24,56},{28,60},{32,0... | collective-permute-start | bytes 110600 | tf_op jit(solution)/shard_map/ppermute | solution.py:585
  45.4 11.9 %collective-permute-start.8 = (f32[72,128]{1,0:T(8,128)S(1)}, f32[72,128]{1,0:T(8,128)S(1)}, u32[]{:S(2)}, u32[]{:S(2)}) collective-permute-start(f32[72,128]{1,0:T(8,128)S(1)} %slice_add_fusion), channel_id=1, source_target_pairs={{0,48},{4,52},{8,56},{12,60},{16,32},{20,36},{24,40},{28,44},{32,1... | collective-permute-start | bytes 110600 | tf_op jit(solution)/shard_map/ppermute | solution.py:585
  45.5 11.8 %collective-permute-start.7 = (f32[72,128]{1,0:T(8,128)S(1)}, f32[72,128]{1,0:T(8,128)S(1)}, u32[]{:S(2)}, u32[]{:S(2)}) collective-permute-start(f32[72,128]{1,0:T(8,128)S(1)} %slice_add_fusion), channel_id=1, source_target_pairs={{0,16},{4,20},{8,24},{12,28},{16,0},{20,4},{24,8},{28,12},{32,48},... | collective-permute-start | bytes 110600 | tf_op jit(solution)/shard_map/ppermute | solution.py:585
  51.1 6.4 %collective-permute-start.13 = (f32[11,16,128]{2,1,0:T(8,128)S(1)}, f32[11,16,128]{2,1,0:T(8,128)S(1)}, u32[]{:S(2)}, u32[]{:S(2)}) collective-permute-start(f32[11,16,128]{2,1,0:T(8,128)S(1)} %get-tuple-element.58), channel_id=1, source_target_pairs={{0,4},{4,0},{8,12},{12,8},{16,20},{20,16},{24,28},{28,24},{32,36},... | collective-permute-start | bytes 270344 | tf_op jit(solution)/shard_map/ppermute | solution.py:585
  51.9 9.9 %collective-permute-start.15 = (f32[11,16,128]{2,1,0:T(8,128)S(1)}, f32[11,16,128]{2,1,0:T(8,128)S(1)}, u32[]{:S(2)}, u32[]{:S(2)}) collective-permute-start(f32[11,16,128]{2,1,0:T(8,128)S(1)} %get-tuple-element.61), channel_id=1, source_target_pairs={{0,252},{4,8},{8,4},{12,16},{16,12},{20,24},{24,20},{28,32},{32,28... | collective-permute-start | bytes 270344 | tf_op jit(solution)/shard_map/ppermute | solution.py:622
  57.3 5.7 %collective-permute-start.11 = (f32[72,128]{1,0:T(8,128)S(1)}, f32[72,128]{1,0:T(8,128)S(1)}, u32[]{:S(2)}, u32[]{:S(2)}) collective-permute-start(f32[72,128]{1,0:T(8,128)S(1)} %add_add_fusion.2), channel_id=1, source_target_pairs={{0,192},{4,196},{8,200},{12,204},{16,208},{20,212},{24,216},{28,22... | collective-permute-start | bytes 110600 | tf_op jit(solution)/shard_map/ppermute | solution.py:585
  57.4 5.6 %collective-permute-start.10 = (f32[72,128]{1,0:T(8,128)S(1)}, f32[72,128]{1,0:T(8,128)S(1)}, u32[]{:S(2)}, u32[]{:S(2)}) collective-permute-start(f32[72,128]{1,0:T(8,128)S(1)} %add_add_fusion.2), channel_id=1, source_target_pairs={{0,64},{4,68},{8,72},{12,76},{16,80},{20,84},{24,88},{28,92},{32,9... | collective-permute-start | bytes 110600 | tf_op jit(solution)/shard_map/ppermute | solution.py:585
  57.5 6.0 %collective-permute-start.14 = (f32[72,128]{1,0:T(8,128)S(1)}, f32[72,128]{1,0:T(8,128)S(1)}, u32[]{:S(2)}, u32[]{:S(2)}) collective-permute-start(f32[72,128]{1,0:T(8,128)S(1)} %add_add_fusion.2), channel_id=1, source_target_pairs={{0,128},{4,132},{8,136},{12,140},{16,144},{20,148},{24,152},{28,15... | collective-permute-start | bytes 110600 | tf_op jit(solution)/shard_map/ppermute | solution.py:585
  63.6 4.2 %collective-permute-start.18 = (f32[72,128]{1,0:T(8,128)S(1)}, f32[72,128]{1,0:T(8,128)S(1)}, u32[]{:S(2)}, u32[]{:S(2)}) collective-permute-start(f32[72,128]{1,0:T(8,128)S(1)} %add_add_fusion.1), channel_id=1, source_target_pairs={{0,8},{4,12},{8,0},{12,4},{16,24},{20,28},{24,16},{28,20},{32,40},... | collective-permute-start | bytes 110600 | tf_op jit(solution)/shard_map/ppermute | solution.py:585
  63.7 4.1 %collective-permute-start.17 = (f32[72,128]{1,0:T(8,128)S(1)}, f32[72,128]{1,0:T(8,128)S(1)}, u32[]{:S(2)}, u32[]{:S(2)}) collective-permute-start(f32[72,128]{1,0:T(8,128)S(1)} %add_add_fusion.1), channel_id=1, source_target_pairs={{0,14},{1,15},{2,12},{3,13},{4,8},{5,9},{6,10},{7,11},{8,4},{9,5},... | collective-permute-start | bytes 110600 | tf_op jit(solution)/shard_map/ppermute | solution.py:602
  63.8 4.0 %collective-permute-start.16 = (f32[72,128]{1,0:T(8,128)S(1)}, f32[72,128]{1,0:T(8,128)S(1)}, u32[]{:S(2)}, u32[]{:S(2)}) collective-permute-start(f32[72,128]{1,0:T(8,128)S(1)} %add_add_fusion.1), channel_id=1, source_target_pairs={{0,4},{4,0},{8,12},{12,8},{16,20},{20,16},{24,28},{28,24},{32,36},... | collective-permute-start | bytes 110600 | tf_op jit(solution)/shard_map/ppermute | solution.py:585

commit v6 on v5

--- a/solution.py
+++ b/solution.py
@@ -672,15 +672,15 @@
     near, skip_back = lax.optimization_barrier((near, skip_back))
     (pair,) = call(pair_kernel, (shape_of(104, 128),), (own, near, frame))
     far = swapped(pair, "lat", 2)
-    other = middle(after(other, pair))
+    other = middle(after(other, near))
     sums = pair[:72] + far[:72]
     steps = [swapped(sums, "lon", k) for k in (4, 12, 8)]
     shares, first, second = lat_sum(frame, near, other, far, 72, part)
     first, second = lon_exchange(first, second)
     sums = sums + steps[0] + (steps[1] + steps[2])
-    steps = [swapped(sums, "lon", k) for k in (16, 48)]
+    steps = [swapped(sums, "lon", k) for k in (16, 32)]
     later, second = lax.optimization_barrier((sums, second))
-    steps.append(swapped(later, "lon", 32))
+    steps.append(swapped(later, "lon", 48))
     sums = sums + steps[0] + (steps[1] + steps[2])
     (rows,) = call(
         unmix_kernel,

time: 69.1 us -> 69.1 us (level)
  waiting for transfers between devices: 13.6 us -> 14.3 us
where the time goes in v6:
time: 69.1 us; the launch traced here: 68.6 us
  starting transfers between devices  39.2 us (57%)
  waiting for transfers between devices  14.3 us (21%)
  Pallas kernels  11.3 us (16%)
  local copies, waits for them, and re-layouts  2.79 us (4%)
  between operations  0.96 us (1%)
    ppermute x14, starting transfers between devices, swapped(): return lax.ppermute(values, axis, [(i, i ^ distance) for i in range(count)])  16.7 us
    ppermute x2, starting transfers between devices, lon_exchange(): return (lax.ppermute(first, 'lon', pairs), swapped(second, 'lon', 1))  11.6 us
    ppermute x2, starting transfers between devices, middle(): return lax.ppermute(values, 'lat', [(1, 2), (2, 1)])  10.8 us
    pallas_call x6, Pallas kernels, call(): pl.pallas_call(kernel, grid_spec=grid_spec, out_shape=list(outs), compile...  7.48 us
    ppermute x14, waiting for transfers between devices, swapped(): return lax.ppermute(values, axis, [(i, i ^ distance) for i in range(count)])  6.99 us
    ppermute x2, waiting for transfers between devices, lon_exchange(): return (lax.ppermute(first, 'lon', pairs), swapped(second, 'lon', 1))  4.6 us
    pallas_call x5, Pallas kernels, call(): pl.pallas_call(kernel, grid=(1,), in_specs=in_specs, out_specs=out_specs,...  3.84 us
    unnamed x24, local copies, waits for them, and re-layouts  2.79 us
  transfers between devices with their start and end apart: 19, of which 8 were waited for; matrix products, arithmetic and copies ran while one was open for 0% of the time, Pallas kernels for 7%

profile of v6, /device:TPU:1, one launch (start us, length us, event | category | flops | bytes accessed | tf_op | source)
XLA Modules:
  0.0 68.6 jit_solution(13514338402526295313)
XLA Ops:
  0.6 0.0 copy-start
  0.7 1.2 %copy-done = f32[32,64,128]{2,1,0:T(8,128)S(1)} copy-done((f32[32,64,128]{2,1,0:T(8,128)S(1)}, f32[32,64,128]{2,1,0:T(8,128)}, u32[]{:S(2)}) %copy-start) | copy-done | bytes 1048600
  1.9 1.0 %copy-done.3 = bf16[1536,128]{1,0:T(8,128)(2,1)S(1)} copy-done((bf16[1536,128]{1,0:T(8,128)(2,1)S(1)}, bf16[1536,128]{1,0:T(8,128)(2,1)}, u32[]{:S(2)}) %copy-start.3) | copy-done | bytes 393240
  2.9 1.2 %shard_map.145 = (f32[512,128]{1,0:T(8,128)S(1)}, f32[192,128]{1,0:T(8,128)S(1)}, f32[192,128]{1,0:T(8,128)S(1)}, f32[32,128]{1,0:T(8,128)S(1)}) custom-call(s32[1]{0:T(128)} %bitcast.part_ref, f32[32,64,128]{2,1,0:T(8,128)S(1)} %copy-done, bf16[1536,128]{1,0:T(8,128)(2,1)S(1)} %copy-done.3), custom_call_target="tpu_custom_call" | custom-call | tf_op jit(solution)/shard_map/pallas_call | solution.py:571
  4.0 3.3 %collective-permute-start = (f32[192,128]{1,0:T(8,128)S(1)}, f32[192,128]{1,0:T(8,128)S(1)}, u32[]{:S(2)}, u32[]{:S(2)}) collective-permute-start(f32[192,128]{1,0:T(8,128)S(1)} %get-tuple-element.40), channel_id=1, source_target_pairs={{0,1},{1,0},{2,3},{3,2},{4,5},{5,4},{6,7},{7,6},{8,9},{9,8},{10,11... | collective-permute-start | bytes 294920 | tf_op jit(solution)/shard_map/ppermute | solution.py:585
  7.3 7.0 %collective-permute-start.1 = (f32[192,128]{1,0:T(8,128)S(1)}, f32[192,128]{1,0:T(8,128)S(1)}, u32[]{:S(2)}, u32[]{:S(2)}) collective-permute-start(f32[192,128]{1,0:T(8,128)S(1)} %get-tuple-element.41), channel_id=1, source_target_pairs={{1,2},{2,1},{5,6},{6,5},{9,10},{10,9},{13,14},{14,13},{17,18},{18,... | collective-permute-start | bytes 294920 | tf_op jit(solution)/shard_map/ppermute | solution.py:606
  14.3 0.0 copy-start.11
  14.3 0.1 collective-permute-start.2
  14.4 0.0 copy-done.1
  14.4 0.0 copy-done.9
  14.4 0.5 copy-done.11
  14.9 0.8 %shard_map.146.pre_ref = f32[32,64,128]{2,1,0:T(8,128)S(1)} custom-call(f32[32,64,128]{2,1,0:T(8,128)S(1)} %copy-done.1, f32[32,32]{1,0:T(8,128)S(1)} %copy-done.9, f32[1,32]{1,0:T(1,128)S(1)} %bitcast.3), custom_call_target="tpu_custom_call" | custom-call | tf_op jit(solution)/shard_map/pallas_call | solution.py:555
  15.8 0.0 copy-start.2
  15.8 5.3 %collective-permute-done.2.far_ref = f32[32,128]{1,0:T(8,128)S(1)} collective-permute-done((f32[32,128]{1,0:T(8,128)S(1)}, f32[32,128]{1,0:T(8,128)S(1)}, u32[]{:S(2)}, u32[]{:S(2)}) %collective-permute-start.2) | collective-permute-done | bytes 16416 | tf_op jit(solution)/shard_map/ppermute | solution.py:585
  21.1 0.0 collective-permute-done.near_ref
  21.1 0.0 collective-permute-done.1.other_ref
  21.1 0.0 copy-done.8
  21.1 0.0 copy-start.6
  21.1 0.0 copy-start.7
  21.1 0.3 shard_map.147
  21.4 0.0 copy-start.10
  21.4 6.3 %collective-permute-start.3 = (f32[11,16,128]{2,1,0:T(8,128)S(1)}, f32[11,16,128]{2,1,0:T(8,128)S(1)}, u32[]{:S(2)}, u32[]{:S(2)}) collective-permute-start(f32[11,16,128]{2,1,0:T(8,128)S(1)} %get-tuple-element.47), channel_id=1, source_target_pairs={{0,252},{4,8},{8,4},{12,16},{16,12},{20,24},{24,20},{28,32},{32,28... | collective-permute-start | bytes 270344 | tf_op jit(solution)/shard_map/ppermute | solution.py:622
  27.7 0.0 collective-permute-start.4
  27.7 3.3 %collective-permute-done.3.first_ref = f32[11,16,128]{2,1,0:T(8,128)S(1)} collective-permute-done((f32[11,16,128]{2,1,0:T(8,128)S(1)}, f32[11,16,128]{2,1,0:T(8,128)S(1)}, u32[]{:S(2)}, u32[]{:S(2)}) %collective-permute-start.3) | collective-permute-done | bytes 90144 | tf_op jit(solution)/shard_map/ppermute | solution.py:622
  31.0 0.1 collective-permute-done.4.second_ref
  31.1 0.0 copy-done.4
  31.1 0.0 copy-done.5
  31.1 0.0 copy-done.2
  31.1 3.1 %shard_map.148 = (bf16[32,64,128]{2,1,0:T(8,128)(2,1)}, f32[32,64,128]{2,1,0:T(8,128)S(1)}, f32[512,128]{1,0:T(8,128)S(1)}, f32[512,128]{1,0:T(8,128)S(1)}, f32[...) custom-call(s32[1]{0:T(128)} %bitcast.part_ref, f32[512,128]{1,0:T(8,128)S(1)} %get-tuple-element.46.shares_ref, ...), custom_call_target="tpu_custom_call" | custom-call | tf_op jit(solution)/shard_map/pallas_call | solution.py:571
  34.2 1.3 %shard_map.149.own_ref = f32[264,128]{1,0:T(8,128)S(1)} custom-call(f32[32,64,128]{2,1,0:T(8,128)S(1)} %copy-done.1, f32[32,64,128]{2,1,0:T(8,128)S(1)} %get-tuple-element.51.g_ref, f32[512,128]{1,0:T(8,128)S(1)} %get-tuple-element.52.coef_ref, f32[512,128]{1,0:T(8,128)S(1)} %get-tuple-element.53.frame_ref, f32[192,128]{1,0:T(8,128)S(1)} %get-tuple-element.54.near_ref, ...), custom_call_target="tpu_custom_call" | custom-call | tf_op jit(solution)/shard_map/pallas_call | solution.py:555
  35.6 0.1 collective-permute-start.5
  35.7 0.8 %shard_map.150.skip_ref = f32[32,64,128]{2,1,0:T(8,128)S(1)} custom-call(f32[32,64,128]{2,1,0:T(8,128)S(1)} %get-tuple-element.51.g_ref, f32[32,32]{1,0:T(8,128)S(1)} %copy-done.9), custom_call_target="tpu_custom_call" | custom-call | tf_op jit(solution)/shard_map/pallas_call | solution.py:555
  36.5 0.5 collective-permute-done.5.near_ref
  37.0 0.1 shard_map.151
  37.1 3.8 %collective-permute-start.6 = (f32[104,128]{1,0:T(8,128)S(1)}, f32[104,128]{1,0:T(8,128)S(1)}, u32[]{:S(2)}, u32[]{:S(2)}) collective-permute-start(f32[104,128]{1,0:T(8,128)S(1)} %shard_map.151), channel_id=1, source_target_pairs={{0,2},{1,3},{2,0},{3,1},{4,6},{5,7},{6,4},{7,5},{8,10},{9,11},{10,... | collective-permute-start | bytes 159752 | tf_op jit(solution)/shard_map/ppermute | solution.py:585
  40.9 3.8 %collective-permute-start.12 = (f32[192,128]{1,0:T(8,128)S(1)}, f32[192,128]{1,0:T(8,128)S(1)}, u32[]{:S(2)}, u32[]{:S(2)}) collective-permute-start(f32[192,128]{1,0:T(8,128)S(1)} %get-tuple-element.57), channel_id=1, source_target_pairs={{1,2},{2,1},{5,6},{6,5},{9,10},{10,9},{13,14},{14,13},{17,18},{18,... | collective-permute-start | bytes 294920 | tf_op jit(solution)/shard_map/ppermute | solution.py:606
  44.8 0.6 collective-permute-done.6.far_ref
  45.4 0.0 collective-permute-start.9
  45.4 0.1 collective-permute-start.8
  45.5 2.5 %collective-permute-start.7 = (f32[72,128]{1,0:T(8,128)S(1)}, f32[72,128]{1,0:T(8,128)S(1)}, u32[]{:S(2)}, u32[]{:S(2)}) collective-permute-start(f32[72,128]{1,0:T(8,128)S(1)} %slice_add_fusion), channel_id=1, source_target_pairs={{0,16},{4,20},{8,24},{12,28},{16,0},{20,4},{24,8},{28,12},{32,48},... | collective-permute-start | bytes 110600 | tf_op jit(solution)/shard_map/ppermute | solution.py:585
  48.0 2.7 %collective-permute-done.12.other_ref = f32[192,128]{1,0:T(8,128)S(1)} collective-permute-done((f32[192,128]{1,0:T(8,128)S(1)}, f32[192,128]{1,0:T(8,128)S(1)}, u32[]{:S(2)}, u32[]{:S(2)}) %collective-permute-start.12) | collective-permute-done | bytes 98336 | tf_op jit(solution)/shard_map/ppermute | solution.py:606
  50.8 0.3 shard_map.152
  51.1 0.8 %collective-permute-start.13 = (f32[11,16,128]{2,1,0:T(8,128)S(1)}, f32[11,16,128]{2,1,0:T(8,128)S(1)}, u32[]{:S(2)}, u32[]{:S(2)}) collective-permute-start(f32[11,16,128]{2,1,0:T(8,128)S(1)} %get-tuple-element.58), channel_id=1, source_target_pairs={{0,4},{4,0},{8,12},{12,8},{16,20},{20,16},{24,28},{28,24},{32,36},... | collective-permute-start | bytes 270344 | tf_op jit(solution)/shard_map/ppermute | solution.py:585
  51.9 5.3 %collective-permute-start.15 = (f32[11,16,128]{2,1,0:T(8,128)S(1)}, f32[11,16,128]{2,1,0:T(8,128)S(1)}, u32[]{:S(2)}, u32[]{:S(2)}) collective-permute-start(f32[11,16,128]{2,1,0:T(8,128)S(1)} %get-tuple-element.61), channel_id=1, source_target_pairs={{0,252},{4,8},{8,4},{12,16},{16,12},{20,24},{24,20},{28,32},{32,28... | collective-permute-start | bytes 270344 | tf_op jit(solution)/shard_map/ppermute | solution.py:622
  57.3 0.0 collective-permute-done.9
  57.3 0.0 collective-permute-done.8
  57.3 0.0 collective-permute-done.7
  57.3 0.1 collective-permute-start.11
  57.4 0.1 collective-permute-start.10
  57.5 0.0 collective-permute-done.13.second_ref
  57.5 3.1 %collective-permute-start.14 = (f32[72,128]{1,0:T(8,128)S(1)}, f32[72,128]{1,0:T(8,128)S(1)}, u32[]{:S(2)}, u32[]{:S(2)}) collective-permute-start(f32[72,128]{1,0:T(8,128)S(1)} %add_add_fusion.2), channel_id=1, source_target_pairs={{0,192},{4,196},{8,200},{12,204},{16,208},{20,212},{24,216},{28,22... | collective-permute-start | bytes 110600 | tf_op jit(solution)/shard_map/ppermute | solution.py:585
  60.7 1.3 %collective-permute-done.15.first_ref = f32[11,16,128]{2,1,0:T(8,128)S(1)} collective-permute-done((f32[11,16,128]{2,1,0:T(8,128)S(1)}, f32[11,16,128]{2,1,0:T(8,128)S(1)}, u32[]{:S(2)}, u32[]{:S(2)}) %collective-permute-start.15) | collective-permute-done | bytes 90144 | tf_op jit(solution)/shard_map/ppermute | solution.py:622
  62.0 1.1 %shard_map.153.rows_ref = f32[256,1024]{1,0:T(8,128)S(1)} custom-call(s32[1]{0:T(128)} %bitcast.part_ref, f32[512,128]{1,0:T(8,128)S(1)} %get-tuple-element.60.shares_ref, f32[11,16,128]{2,1,0:T(8,128)S(1)} %collective-permute-done.15.first_ref, f32[11,16,128]{2,1,0:T(8,128)S(1)} %collective-permute-done.13.second_ref, f32[4,32,32]{2,1,0:T(8,128)S(1)} %copy-done.6, ...), custom_call_target="tpu_custom_call" | custom-call | tf_op jit(solution)/shard_map/pallas_call | solution.py:571
  63.1 0.0 collective-permute-done.11
  63.1 0.0 collective-permute-done.10
  63.1 0.5 collective-permute-done.14
  63.6 0.1 collective-permute-start.18
  63.7 0.1 collective-permute-start.17
  63.8 2.5 %collective-permute-start.16 = (f32[72,128]{1,0:T(8,128)S(1)}, f32[72,128]{1,0:T(8,128)S(1)}, u32[]{:S(2)}, u32[]{:S(2)}) collective-permute-start(f32[72,128]{1,0:T(8,128)S(1)} %add_add_fusion.1), channel_id=1, source_target_pairs={{0,4},{4,0},{8,12},{12,8},{16,20},{20,16},{24,28},{28,24},{32,36},... | collective-permute-start | bytes 110600 | tf_op jit(solution)/shard_map/ppermute | solution.py:585
  66.4 1.5 %shard_map.154 = f32[32,64,128]{2,1,0:T(8,128)} custom-call(s32[1]{0:T(128)} %bitcast.part_ref, f32[256,1024]{1,0:T(8,128)S(1)} %shard_map.153.rows_ref, f32[32,64,128]{2,1,0:T(8,128)S(1)} %shard_map.150.skip_ref, bf16[1536,128]{1,0:T(8,128)(2,1)S(1)} %copy-done.2), custom_call_target="tpu_custom_call" | custom-call | tf_op jit(solution)/shard_map/pallas_call | solution.py:571
  67.8 0.0 collective-permute-done.18
  67.9 0.0 collective-permute-done.17
  67.9 0.0 collective-permute-done.16
  67.9 0.7 %shard_map.155 = (f32[4,32,32]{2,1,0:T(8,128)}, f32[3,32,32]{2,1,0:T(8,128)}, f32[32,32]{1,0:T(8,128)}, f32[1,32]{1,0:T(1,128)}) custom-call(f32[72,128]{1,0:T(8,128)S(1)} %add_add_fusion.sum_ref), custom_call_target="tpu_custom_call" | custom-call | tf_op jit(solution)/shard_map/pallas_call | solution.py:555
  (13 shorter events, 0.1 us)
Async XLA Ops:
  0.6 1.2 %copy-start = (f32[32,64,128]{2,1,0:T(8,128)S(1)}, f32[32,64,128]{2,1,0:T(8,128)}, u32[]{:S(2)}) copy-start(f32[32,64,128]{2,1,0:T(8,128)} %x_ref.5) | copy-start | bytes 3145732
  1.9 1.0 %copy-start.3 = (bf16[1536,128]{1,0:T(8,128)(2,1)S(1)}, bf16[1536,128]{1,0:T(8,128)(2,1)}, u32[]{:S(2)}) copy-start(bf16[1536,128]{1,0:T(8,128)(2,1)} %constant.30.clone.table_ref.analysis_ref) | copy-start | bytes 1179652
  2.9 11.5 %copy-start.1 = (f32[32,64,128]{2,1,0:T(8,128)S(1)}, f32[32,64,128]{2,1,0:T(8,128)}, u32[]{:S(2)}) copy-start(f32[32,64,128]{2,1,0:T(8,128)} %x_ref.5) | copy-start | bytes 3145732
  2.9 11.5 %copy-start.9 = (f32[32,32]{1,0:T(8,128)S(1)}, f32[32,32]{1,0:T(8,128)}, u32[]{:S(2)}) copy-start(f32[32,32]{1,0:T(8,128)} %skip_ref.3) | copy-start | bytes 12292
  4.0 17.0 %collective-permute-start = (f32[192,128]{1,0:T(8,128)S(1)}, f32[192,128]{1,0:T(8,128)S(1)}, u32[]{:S(2)}, u32[]{:S(2)}) collective-permute-start(f32[192,128]{1,0:T(8,128)S(1)} %get-tuple-element.40), channel_id=1, source_target_pairs={{0,1},{1,0},{2,3},{3,2},{4,5},{5,4},{6,7},{7,6},{8,9},{9,8},{10,11... | collective-permute-start | bytes 294920 | tf_op jit(solution)/shard_map/ppermute | solution.py:585
  7.3 13.8 %collective-permute-start.1 = (f32[192,128]{1,0:T(8,128)S(1)}, f32[192,128]{1,0:T(8,128)S(1)}, u32[]{:S(2)}, u32[]{:S(2)}) collective-permute-start(f32[192,128]{1,0:T(8,128)S(1)} %get-tuple-element.41), channel_id=1, source_target_pairs={{1,2},{2,1},{5,6},{6,5},{9,10},{10,9},{13,14},{14,13},{17,18},{18,... | collective-permute-start | bytes 294920 | tf_op jit(solution)/shard_map/ppermute | solution.py:606
  14.3 0.7 copy-start.11
  14.3 6.8 %collective-permute-start.2 = (f32[32,128]{1,0:T(8,128)S(1)}, f32[32,128]{1,0:T(8,128)S(1)}, u32[]{:S(2)}, u32[]{:S(2)}) collective-permute-start(f32[32,128]{1,0:T(8,128)S(1)} %get-tuple-element.42), channel_id=1, source_target_pairs={{0,2},{1,3},{2,0},{3,1},{4,6},{5,7},{6,4},{7,5},{8,10},{9,11},{10,... | collective-permute-start | bytes 49160 | tf_op jit(solution)/shard_map/ppermute | solution.py:585
  14.9 6.1 %copy-start.8 = (f32[4,16,128]{2,1,0:T(8,128)S(1)}, f32[4,16,128]{2,1,0:T(8,128)}, u32[]{:S(2)}) copy-start(f32[4,16,128]{2,1,0:T(8,128)} %constant.33.clone.mask_ref) | copy-start | bytes 98308
  14.9 16.2 %copy-start.4 = (bf16[1536,128]{1,0:T(8,128)(2,1)S(1)}, bf16[1536,128]{1,0:T(8,128)(2,1)}, u32[]{:S(2)}) copy-start(bf16[1536,128]{1,0:T(8,128)(2,1)} %constant.30.clone.table_ref.analysis_ref) | copy-start | bytes 1179652
  14.9 16.2 %copy-start.5 = (bf16[32,64,128]{2,1,0:T(8,128)(2,1)S(1)}, bf16[32,64,128]{2,1,0:T(8,128)(2,1)}, u32[]{:S(2)}) copy-start(bf16[32,64,128]{2,1,0:T(8,128)(2,1)} %cot_ref.1) | copy-start | bytes 1572868
  15.8 15.3 %copy-start.2 = (bf16[1536,128]{1,0:T(8,128)(2,1)S(1)}, bf16[1536,128]{1,0:T(8,128)(2,1)}, u32[]{:S(2)}) copy-start(bf16[1536,128]{1,0:T(8,128)(2,1)} %constant.31.clone.synthesis_ref) | copy-start | bytes 1179652
  21.1 10.1 %copy-start.6 = (f32[4,32,32]{2,1,0:T(8,128)S(1)}, f32[4,32,32]{2,1,0:T(8,128)}, u32[]{:S(2)}) copy-start(f32[4,32,32]{2,1,0:T(8,128)} %coarse_ref.3) | copy-start | bytes 49156
  21.1 10.0 %copy-start.7 = (f32[3,32,32]{2,1,0:T(8,128)S(1)}, f32[3,32,32]{2,1,0:T(8,128)}, u32[]{:S(2)}) copy-start(f32[3,32,32]{2,1,0:T(8,128)} %detail_ref.3) | copy-start | bytes 36868
  21.4 9.7 %copy-start.10 = (f32[8,128]{1,0:T(8,128)S(1)}, f32[8,128]{1,0:T(8,128)}, u32[]{:S(2)}) copy-start(f32[8,128]{1,0:T(8,128)} %constant.32.clone.subband_ref) | copy-start | bytes 12292
  21.4 9.6 %collective-permute-start.3 = (f32[11,16,128]{2,1,0:T(8,128)S(1)}, f32[11,16,128]{2,1,0:T(8,128)S(1)}, u32[]{:S(2)}, u32[]{:S(2)}) collective-permute-start(f32[11,16,128]{2,1,0:T(8,128)S(1)} %get-tuple-element.47), channel_id=1, source_target_pairs={{0,252},{4,8},{8,4},{12,16},{16,12},{20,24},{24,20},{28,32},{32,28... | collective-permute-start | bytes 270344 | tf_op jit(solution)/shard_map/ppermute | solution.py:622
  27.7 3.4 %collective-permute-start.4 = (f32[11,16,128]{2,1,0:T(8,128)S(1)}, f32[11,16,128]{2,1,0:T(8,128)S(1)}, u32[]{:S(2)}, u32[]{:S(2)}) collective-permute-start(f32[11,16,128]{2,1,0:T(8,128)S(1)} %get-tuple-element.48), channel_id=1, source_target_pairs={{0,4},{4,0},{8,12},{12,8},{16,20},{20,16},{24,28},{28,24},{32,36},... | collective-permute-start | bytes 270344 | tf_op jit(solution)/shard_map/ppermute | solution.py:585
  35.6 1.4 %collective-permute-start.5 = (f32[264,128]{1,0:T(8,128)S(1)}, f32[264,128]{1,0:T(8,128)S(1)}, u32[]{:S(2)}, u32[]{:S(2)}) collective-permute-start(f32[264,128]{1,0:T(8,128)S(1)} %shard_map.149.own_ref), channel_id=1, source_target_pairs={{0,1},{1,0},{2,3},{3,2},{4,5},{5,4},{6,7},{7,6},{8,9},{9,8},{10,11... | collective-permute-start | bytes 405512 | tf_op jit(solution)/shard_map/ppermute | solution.py:585
  37.1 8.3 %collective-permute-start.6 = (f32[104,128]{1,0:T(8,128)S(1)}, f32[104,128]{1,0:T(8,128)S(1)}, u32[]{:S(2)}, u32[]{:S(2)}) collective-permute-start(f32[104,128]{1,0:T(8,128)S(1)} %shard_map.151), channel_id=1, source_target_pairs={{0,2},{1,3},{2,0},{3,1},{4,6},{5,7},{6,4},{7,5},{8,10},{9,11},{10,... | collective-permute-start | bytes 159752 | tf_op jit(solution)/shard_map/ppermute | solution.py:585
  40.9 9.8 %collective-permute-start.12 = (f32[192,128]{1,0:T(8,128)S(1)}, f32[192,128]{1,0:T(8,128)S(1)}, u32[]{:S(2)}, u32[]{:S(2)}) collective-permute-start(f32[192,128]{1,0:T(8,128)S(1)} %get-tuple-element.57), channel_id=1, source_target_pairs={{1,2},{2,1},{5,6},{6,5},{9,10},{10,9},{13,14},{14,13},{17,18},{18,... | collective-permute-start | bytes 294920 | tf_op jit(solution)/shard_map/ppermute | solution.py:606
  45.4 11.9 %collective-permute-start.9 = (f32[72,128]{1,0:T(8,128)S(1)}, f32[72,128]{1,0:T(8,128)S(1)}, u32[]{:S(2)}, u32[]{:S(2)}) collective-permute-start(f32[72,128]{1,0:T(8,128)S(1)} %slice_add_fusion), channel_id=1, source_target_pairs={{0,32},{4,36},{8,40},{12,44},{16,48},{20,52},{24,56},{28,60},{32,0... | collective-permute-start | bytes 110600 | tf_op jit(solution)/shard_map/ppermute | solution.py:585
  45.4 11.9 %collective-permute-start.8 = (f32[72,128]{1,0:T(8,128)S(1)}, f32[72,128]{1,0:T(8,128)S(1)}, u32[]{:S(2)}, u32[]{:S(2)}) collective-permute-start(f32[72,128]{1,0:T(8,128)S(1)} %slice_add_fusion), channel_id=1, source_target_pairs={{0,48},{4,52},{8,56},{12,60},{16,32},{20,36},{24,40},{28,44},{32,1... | collective-permute-start | bytes 110600 | tf_op jit(solution)/shard_map/ppermute | solution.py:585
  45.5 11.8 %collective-permute-start.7 = (f32[72,128]{1,0:T(8,128)S(1)}, f32[72,128]{1,0:T(8,128)S(1)}, u32[]{:S(2)}, u32[]{:S(2)}) collective-permute-start(f32[72,128]{1,0:T(8,128)S(1)} %slice_add_fusion), channel_id=1, source_target_pairs={{0,16},{4,20},{8,24},{12,28},{16,0},{20,4},{24,8},{28,12},{32,48},... | collective-permute-start | bytes 110600 | tf_op jit(solution)/shard_map/ppermute | solution.py:585
  51.1 6.4 %collective-permute-start.13 = (f32[11,16,128]{2,1,0:T(8,128)S(1)}, f32[11,16,128]{2,1,0:T(8,128)S(1)}, u32[]{:S(2)}, u32[]{:S(2)}) collective-permute-start(f32[11,16,128]{2,1,0:T(8,128)S(1)} %get-tuple-element.58), channel_id=1, source_target_pairs={{0,4},{4,0},{8,12},{12,8},{16,20},{20,16},{24,28},{28,24},{32,36},... | collective-permute-start | bytes 270344 | tf_op jit(solution)/shard_map/ppermute | solution.py:585
  51.9 10.0 %collective-permute-start.15 = (f32[11,16,128]{2,1,0:T(8,128)S(1)}, f32[11,16,128]{2,1,0:T(8,128)S(1)}, u32[]{:S(2)}, u32[]{:S(2)}) collective-permute-start(f32[11,16,128]{2,1,0:T(8,128)S(1)} %get-tuple-element.61), channel_id=1, source_target_pairs={{0,252},{4,8},{8,4},{12,16},{16,12},{20,24},{24,20},{28,32},{32,28... | collective-permute-start | bytes 270344 | tf_op jit(solution)/shard_map/ppermute | solution.py:622
  57.3 5.8 %collective-permute-start.11 = (f32[72,128]{1,0:T(8,128)S(1)}, f32[72,128]{1,0:T(8,128)S(1)}, u32[]{:S(2)}, u32[]{:S(2)}) collective-permute-start(f32[72,128]{1,0:T(8,128)S(1)} %add_add_fusion.2), channel_id=1, source_target_pairs={{0,128},{4,132},{8,136},{12,140},{16,144},{20,148},{24,152},{28,15... | collective-permute-start | bytes 110600 | tf_op jit(solution)/shard_map/ppermute | solution.py:585
  57.4 5.7 %collective-permute-start.10 = (f32[72,128]{1,0:T(8,128)S(1)}, f32[72,128]{1,0:T(8,128)S(1)}, u32[]{:S(2)}, u32[]{:S(2)}) collective-permute-start(f32[72,128]{1,0:T(8,128)S(1)} %add_add_fusion.2), channel_id=1, source_target_pairs={{0,64},{4,68},{8,72},{12,76},{16,80},{20,84},{24,88},{28,92},{32,9... | collective-permute-start | bytes 110600 | tf_op jit(solution)/shard_map/ppermute | solution.py:585
  57.5 6.1 %collective-permute-start.14 = (f32[72,128]{1,0:T(8,128)S(1)}, f32[72,128]{1,0:T(8,128)S(1)}, u32[]{:S(2)}, u32[]{:S(2)}) collective-permute-start(f32[72,128]{1,0:T(8,128)S(1)} %add_add_fusion.2), channel_id=1, source_target_pairs={{0,192},{4,196},{8,200},{12,204},{16,208},{20,212},{24,216},{28,22... | collective-permute-start | bytes 110600 | tf_op jit(solution)/shard_map/ppermute | solution.py:585
  63.6 4.2 %collective-permute-start.18 = (f32[72,128]{1,0:T(8,128)S(1)}, f32[72,128]{1,0:T(8,128)S(1)}, u32[]{:S(2)}, u32[]{:S(2)}) collective-permute-start(f32[72,128]{1,0:T(8,128)S(1)} %add_add_fusion.1), channel_id=1, source_target_pairs={{0,8},{4,12},{8,0},{12,4},{16,24},{20,28},{24,16},{28,20},{32,40},... | collective-permute-start | bytes 110600 | tf_op jit(solution)/shard_map/ppermute | solution.py:585
  63.7 4.1 %collective-permute-start.17 = (f32[72,128]{1,0:T(8,128)S(1)}, f32[72,128]{1,0:T(8,128)S(1)}, u32[]{:S(2)}, u32[]{:S(2)}) collective-permute-start(f32[72,128]{1,0:T(8,128)S(1)} %add_add_fusion.1), channel_id=1, source_target_pairs={{0,14},{1,15},{2,12},{3,13},{4,8},{5,9},{6,10},{7,11},{8,4},{9,5},... | collective-permute-start | bytes 110600 | tf_op jit(solution)/shard_map/ppermute | solution.py:602
  63.8 4.0 %collective-permute-start.16 = (f32[72,128]{1,0:T(8,128)S(1)}, f32[72,128]{1,0:T(8,128)S(1)}, u32[]{:S(2)}, u32[]{:S(2)}) collective-permute-start(f32[72,128]{1,0:T(8,128)S(1)} %add_add_fusion.1), channel_id=1, source_target_pairs={{0,4},{4,0},{8,12},{12,8},{16,20},{20,16},{24,28},{28,24},{32,36},... | collective-permute-start | bytes 110600 | tf_op jit(solution)/shard_map/ppermute | solution.py:585
